TPU v7x, 32 devices: a whole 2x2x4 slice. The times are simulated.
32 devices in a mesh: space: 8 (over z, y), tm: 4 (over x, core).
Axes of the slice: x: 2, y: 2, z: 4, core: 2. Of those that a mesh axis runs over, the one named last changes fastest.
Arguments:
- snapshots: bfloat16 [16384, 2048], P('space', 'tm'), as said below
- sketch: bfloat16 [2048, 256], P('tm'), may hold values from -0.125 to 0.125
- rotation: float32 [256, 256], replicated, may hold values from -0.375 to 0.375
Outputs:
- basis: float32 [16384, 256], P(('space', 'tm'))
- triangle: float32 [256, 256], replicated
Inputs may be any that keep to these rules, and one draw needn't show every extreme that they name: `snapshots`: the sketch has full column rank.
All inputs are finite; a program needn't handle non-finite values.
Results may differ from a plain program's by a relative error of at most 0.0003.
Values sent between devices are 32-bit elements; how exact they have to be, the bound alone decides.
No kernel may reach another device: no remote copies, remote signals or barrier semaphores. Data moves between devices by JAX's collectives and lax.ppermute only.
A program may use at most 64 MiB of HBM per device.

v0:
```python
import jax
import jax.numpy as jnp
from jax import lax
from jax.sharding import PartitionSpec as P


def partner(shard, axis, stride):
    return lax.ppermute(shard, axis, [(i, i ^ 1 << stride) for i in range(lax.axis_size(axis))])


def shards(snapshots, sketch, rotation):
    sketched = lax.psum_scatter(
        jnp.dot(snapshots, sketch, preferred_element_type=jnp.float32),
        "tm",
        scatter_dimension=0,
        tiled=True,
    )
    gram = lax.dot_general(
        sketched,
        sketched,
        (((0,), (0,)), ((), ())),
        precision=lax.Precision.HIGHEST,
        preferred_element_type=jnp.float32,
    )
    for level in range(lax.axis_size("space").bit_length() - 1):
        gram = gram + partner(gram, "space", level)
    for level in range(lax.axis_size("tm").bit_length() - 1):
        gram = gram + partner(gram, "tm", level)
    lower = jnp.linalg.cholesky(gram)
    orthonormal = lax.linalg.triangular_solve(
        lower, sketched, left_side=False, lower=True, transpose_a=True
    )
    cell_count = sketched.shape[0] * lax.axis_size("space") * lax.axis_size("tm")
    scale = jnp.sqrt(jnp.float32(cell_count))
    basis = scale * jnp.dot(
        orthonormal, rotation, precision=lax.Precision.HIGHEST, preferred_element_type=jnp.float32
    )
    triangle = lower.T / scale
    return (basis, triangle)


def solution(mesh):
    in_specs = (P("space", "tm"), P("tm", None), P())
    out_specs = (P(("space", "tm"), None), P())
    return jax.shard_map(shards, mesh=mesh, in_specs=in_specs, out_specs=out_specs, check_vma=False)
```

profile of v0, /device:TPU:0, one launch (start us, length us, event | category | flops | bytes accessed | tf_op | source)
XLA Modules:
  0.0 159.8 jit_solution(5284063239321607241)
XLA Ops:
  7.2 1.5 copy-done
  8.8 3.0 %fusion.14 = f32[2048,256]{1,0:T(8,128)} fusion(bf16[2048,512]{1,0:T(8,128)(2,1)S(1)} %copy-done, bf16[512,256]{1,0:T(8,128)(2,1)} %param.4), kind=kOutput, calls=%fused_computation.35 | convolution fusion | flops 536870912 | bytes 4456448 | tf_op jit(solution)/shard_map/dot_general | solution.py:13
  11.8 34.3 %reduce-scatter.2.cloned.1.call-done = f32[512,256]{1,0:T(8,128)} async-done(((f32[2048,256]{1,0:T(8,128)}), f32[512,256]{1,0:T(8,128)}) %reduce-scatter.2.cloned.1.call-update) | async-done | bytes 524304 | tf_op jit(solution)/shard_map/reduce_scatter | solution.py:12
  46.1 2.2 %fusion.15 = f32[256,256]{0,1:T(8,128)S(1)} fusion(f32[512,256]{1,0:T(8,128)} %reduce-scatter.2.cloned.1.call-done), kind=kOutput, calls=%fused_computation.36 | convolution fusion | flops 402653184 | bytes 786432 | tf_op jit(solution)/shard_map/dot_general | solution.py:18
  48.3 1.5 collective-permute-start
  49.8 6.6 %collective-permute-done = f32[256,256]{0,1:T(8,128)S(1)} collective-permute-done((f32[256,256]{0,1:T(8,128)S(1)}, f32[256,256]{0,1:T(8,128)S(1)}, u32[]{:S(2)}, u32[]{:S(2)}) %collective-permute-start) | collective-permute-done | bytes 262176 | tf_op jit(solution)/shard_map/ppermute | solution.py:8
  56.4 1.6 collective-permute-start.1
  58.0 5.7 %collective-permute-done.1 = f32[256,256]{0,1:T(8,128)S(1)} collective-permute-done((f32[256,256]{0,1:T(8,128)S(1)}, f32[256,256]{0,1:T(8,128)S(1)}, u32[]{:S(2)}, u32[]{:S(2)}) %collective-permute-start.1) | collective-permute-done | bytes 262176 | tf_op jit(solution)/shard_map/ppermute | solution.py:8
  63.7 2.5 %collective-permute-start.2 = (f32[256,256]{0,1:T(8,128)S(1)}, f32[256,256]{0,1:T(8,128)S(1)}, u32[]{:S(2)}, u32[]{:S(2)}) collective-permute-start(f32[256,256]{0,1:T(8,128)S(1)} %add.40), channel_id=1, source_target_pairs={{0,16},{4,20},{8,24},{12,28},{16,0},{20,4},{24,8},{28,12},{1,17},{... | collective-permute-start | bytes 786440 | tf_op jit(solution)/shard_map/ppermute | solution.py:8
  66.2 10.3 %collective-permute-done.2 = f32[256,256]{0,1:T(8,128)S(1)} collective-permute-done((f32[256,256]{0,1:T(8,128)S(1)}, f32[256,256]{0,1:T(8,128)S(1)}, u32[]{:S(2)}, u32[]{:S(2)}) %collective-permute-start.2) | collective-permute-done | bytes 262176 | tf_op jit(solution)/shard_map/ppermute | solution.py:8
  76.6 1.5 collective-permute-done.3
  78.2 0.9 collective-permute-start.4
  79.1 7.5 %collective-permute-done.4 = f32[256,256]{0,1:T(8,128)S(1)} collective-permute-done((f32[256,256]{0,1:T(8,128)S(1)}, f32[256,256]{0,1:T(8,128)S(1)}, u32[]{:S(2)}, u32[]{:S(2)}) %collective-permute-start.4) | collective-permute-done | bytes 262176 | tf_op jit(solution)/shard_map/ppermute | solution.py:8
  86.7 0.1 copy.7
  86.8 11.7 %cholesky.50 = f32[128,128]{1,0:T(8,128)S(1)} custom-call(f32[128,128]{1,0:T(8,128)S(1)} %cholesky.118), custom_call_target="Cholesky" | custom-call | tf_op jit(solution)/shard_map/jit(cholesky)/cholesky | solution.py:29
  98.6 9.8 %custom-call.14 = f32[1,128,128]{1,2,0:T(8,128)S(1)} custom-call(f32[1,128,128]{2,1,0:T(8,128)S(1)} %get-tuple-element.27), custom_call_target="InvertDiagBlocksLowerTriangular" | custom-call | tf_op jit(solution)/shard_map/jit(cholesky)/cholesky | solution.py:29
  108.4 0.2 constant_dynamic-update-slice_fusion.1
  108.6 0.3 slice_subtract_fusion
  108.9 11.9 %cholesky.105 = f32[128,128]{1,0:T(8,128)S(1)} custom-call(f32[128,128]{1,0:T(8,128)S(1)} %slice_subtract_fusion), custom_call_target="Cholesky" | custom-call | tf_op jit(solution)/shard_map/jit(cholesky)/cholesky | solution.py:29
  120.8 0.7 compare_reduce_fusion
  122.9 3.9 %while.1 = (s32[]{:T(128)}, f32[256,256]{1,0:T(8,128)S(1)}, s32[2,2]{1,0:T(2,128)S(1)}, f32[2,128,128]{2,1,0:T(8,128)S(1)}, s32[]{:T(128)}) while((s32[]{:T(128)}, f32[256,256]{1,0:T(8,128)S(1)}, s32[2,2]{1,0:T(2,128)S(1)}, f32[2,128,128]{2,1,0:T(8,128)S(1)}, s32[]{:T(128)}) %tuple.29), condition=%wide.while_cond, body=%wide.while_body.sunk | while | flops 2 | bytes 131181 | solution.py:30
  122.9 0.6 fusion.26
  123.5 1.3 bitcast_dynamic-update-slice_fusion.2
  124.9 0.6 fusion.26
  125.4 1.3 bitcast_dynamic-update-slice_fusion.2
  126.8 0.6 copy-done.2
  127.5 20.5 %custom-call.15 = f32[2,128,128]{1,2,0:T(8,128)S(1)} custom-call(f32[2,128,128]{2,1,0:T(8,128)} %copy-done.2), custom_call_target="InvertDiagBlocksLowerTriangular" | custom-call | tf_op jit(solution)/shard_map/triangular_solve | solution.py:30
  148.0 0.4 fusion.3
  148.4 0.6 convolution_subtract_fusion
  149.0 0.4 fusion.7
  149.4 0.8 copy.8
  150.2 2.7 %convolution_multiply_fusion = f32[512,256]{1,0:T(8,128)} fusion(f32[256,256]{1,0:T(8,128)} %param.5, f32[512,128]{0,1:T(8,128)S(1)} %fusion.7, f32[512,128]{0,1:T(8,128)S(1)} %fusion.3), kind=kOutput, calls=%fused_computation.2 | convolution fusion | flops 402915328 | bytes 1310720 | tf_op jit(solution)/shard_map/dot_general | solution.py:35
  (23 shorter events, 0.6 us)
Async XLA Ops:
  7.2 1.6 copy-start
  7.2 38.9 %reduce-scatter.2.cloned.1.call-start = ((), (), s32[]{:S(2)}) async-start(), calls=%async_computation.1 | async-start | bytes 2621440 | tf_op jit(solution)/shard_map/reduce_scatter | solution.py:12
  48.3 8.1 %collective-permute-start = (f32[256,256]{0,1:T(8,128)S(1)}, f32[256,256]{0,1:T(8,128)S(1)}, u32[]{:S(2)}, u32[]{:S(2)}) collective-permute-start(f32[256,256]{0,1:T(8,128)S(1)} %fusion.15), channel_id=1, source_target_pairs={{0,4},{4,0},{8,12},{12,8},{16,20},{20,16},{24,28},{28,24},{1,5},{5... | collective-permute-start | bytes 786440 | tf_op jit(solution)/shard_map/ppermute | solution.py:8
  56.4 7.2 %collective-permute-start.1 = (f32[256,256]{0,1:T(8,128)S(1)}, f32[256,256]{0,1:T(8,128)S(1)}, u32[]{:S(2)}, u32[]{:S(2)}) collective-permute-start(f32[256,256]{0,1:T(8,128)S(1)} %add.39), channel_id=1, source_target_pairs={{0,8},{4,12},{8,0},{12,4},{16,24},{20,28},{24,16},{28,20},{1,9},{5... | collective-permute-start | bytes 786440 | tf_op jit(solution)/shard_map/ppermute | solution.py:8
  63.7 12.8 %collective-permute-start.2 = (f32[256,256]{0,1:T(8,128)S(1)}, f32[256,256]{0,1:T(8,128)S(1)}, u32[]{:S(2)}, u32[]{:S(2)}) collective-permute-start(f32[256,256]{0,1:T(8,128)S(1)} %add.40), channel_id=1, source_target_pairs={{0,16},{4,20},{8,24},{12,28},{16,0},{20,4},{24,8},{28,12},{1,17},{... | collective-permute-start | bytes 786440 | tf_op jit(solution)/shard_map/ppermute | solution.py:8
  76.6 1.6 %collective-permute-start.3 = (f32[256,256]{0,1:T(8,128)S(1)}, f32[256,256]{0,1:T(8,128)S(1)}, u32[]{:S(2)}, u32[]{:S(2)}) collective-permute-start(f32[256,256]{0,1:T(8,128)S(1)} %add.41), channel_id=1, source_target_pairs={{0,1},{1,0},{2,3},{3,2},{4,5},{5,4},{6,7},{7,6},{8,9},{9,8},{10,11... | collective-permute-start | bytes 786440 | tf_op jit(solution)/shard_map/ppermute | solution.py:8
  78.2 8.4 %collective-permute-start.4 = (f32[256,256]{0,1:T(8,128)S(1)}, f32[256,256]{0,1:T(8,128)S(1)}, u32[]{:S(2)}, u32[]{:S(2)}) collective-permute-start(f32[256,256]{0,1:T(8,128)S(1)} %add.42), channel_id=1, source_target_pairs={{0,2},{1,3},{2,0},{3,1},{4,6},{5,7},{6,4},{7,5},{8,10},{9,11},{10,... | collective-permute-start | bytes 786440 | tf_op jit(solution)/shard_map/ppermute | solution.py:8
  86.6 61.3 %copy-start.1 = (f32[512,256]{1,0:T(8,128)S(1)}, f32[512,256]{1,0:T(8,128)}, u32[]{:S(2)}) copy-start(f32[512,256]{1,0:T(8,128)} %reduce-scatter.2.cloned.1.call-done) | copy-start | bytes 1572868
  126.8 0.7 copy-start.2
Sparse Core Ops, SparseCore 0:
  11.9 34.1 reduce-scatter.1
where the time goes:
time: 160 us
  waiting for transfers between devices  65.9 us (41%)
  other arithmetic  54.9 us (34%)
  between operations  15.5 us (10%)
  matrix products  9.81 us (6%)
  local copies, waits for them, and re-layouts  7.14 us (4%)
  starting transfers between devices  6.63 us (4%)
    reduce_scatter x1, waiting for transfers between devices, shards(): lax.psum_scatter(jnp.dot(snapshots, sketch, preferred_element_type=jnp.fl...  34.3 us
    another operation x6, other arithmetic, shards(): lower = jnp.linalg.cholesky(gram)  34.1 us
    ppermute x5, waiting for transfers between devices, partner(): lax.ppermute(shard, axis, [(i, i ^ 1 << stride) for i in range(lax.axis_s...  31.6 us
    another operation x2, other arithmetic, shards(): lax.linalg.triangular_solve(lower, sketched, left_side=False, lower=True,...  20.5 us
    ppermute x5, starting transfers between devices, partner(): lax.ppermute(shard, axis, [(i, i ^ 1 << stride) for i in range(lax.axis_s...  6.59 us
    another operation x6, local copies, waits for them, and re-layouts  3.88 us
  transfers between devices with their start and end apart: 6, of which 6 were waited for; matrix products, arithmetic and copies ran while one was open for 0% of the time, Pallas kernels for 0%

commit v1 on v0

v1 whole, which is shorter than its diff:
```python
import functools
import math

import jax
import jax.numpy as jnp
from jax import lax
from jax.experimental import pallas as pl
from jax.experimental.pallas import tpu as pltpu
from jax.sharding import PartitionSpec as P

F32, BF16 = jnp.float32, jnp.bfloat16
VMEM = pl.BlockSpec(memory_space=pltpu.VMEM)
SMEM = pl.BlockSpec(memory_space=pltpu.SMEM)
PANEL = 32


def params():
    return pltpu.CompilerParams(vmem_limit_bytes=40 << 20)


def partner(shard, axis, level):
    return lax.ppermute(shard, axis, [(i, i ^ 1 << level) for i in range(lax.axis_size(axis))])


def levels(axis):
    return lax.axis_size(axis).bit_length() - 1


def split(x):
    high = x.astype(BF16)
    rest = x - high.astype(F32)
    middle = rest.astype(BF16)
    low = (rest - middle.astype(F32)).astype(BF16)
    return high, middle, low


def product(x, y, dims):
    return lax.dot_general(x, y, (dims, ((), ())), preferred_element_type=F32)


def dot_parts(x, y, dims):
    x1, x2, x3 = split(x)
    y1, y2, y3 = split(y)
    small = product(x1, y3, dims) + product(x2, y2, dims) + product(x3, y1, dims)
    return product(x1, y1, dims) + (product(x1, y2, dims) + product(x2, y1, dims) + small)


def dot_stacked(x, y):
    x1, x2, x3 = split(x)
    y1, y2, y3 = split(y)
    left = jnp.concatenate([x1, x1, x2, x1, x2, x3], axis=0)
    right = jnp.concatenate([y1, y2, y1, y3, y2, y1], axis=0)
    return product(left, right, ((0,), (0,)))


def sketch_kernel(blocks_ref, snapshots_ref, sketch_ref, out_ref):
    out_ref[0] = jnp.dot(snapshots_ref[...], sketch_ref[...], preferred_element_type=F32)


def sketch_blocks(blocks, snapshots, sketch, rows):
    count, (depth, columns) = blocks.shape[0], sketch.shape
    return pl.pallas_call(
        sketch_kernel,
        grid_spec=pltpu.PrefetchScalarGridSpec(
            num_scalar_prefetch=1,
            grid=(count,),
            in_specs=[
                pl.BlockSpec((rows, depth), lambda i, blocks: (blocks[i], 0)),
                pl.BlockSpec((depth, columns), lambda i, blocks: (0, 0)),
            ],
            out_specs=pl.BlockSpec((1, rows, columns), lambda i, blocks: (i, 0, 0)),
        ),
        out_shape=jax.ShapeDtypeStruct((count, rows, columns), F32),
        compiler_params=params(),
        cost_estimate=pl.CostEstimate(
            flops=2 * count * rows * depth * columns,
            bytes_accessed=count * rows * (2 * depth + 4 * columns) + 2 * depth * columns,
            transcendentals=0,
        ),
    )(blocks, snapshots, sketch)


def gram_kernel(side_ref, kept_ref, arrived_ref, sketched_ref, keep_ref, send_ref):
    sketched = kept_ref[...] + arrived_ref[...]
    sketched_ref[...] = sketched
    high, middle, low = split(sketched)
    rows = ((0,), (0,))
    cross = product(high, middle, rows) + product(high, low, rows)
    gram = product(high, high, rows) + (cross + cross.T + product(middle, middle, rows))
    h = gram.shape[0] // 2
    row = lax.broadcasted_iota(jnp.int32, (h, h), 0)
    column = lax.broadcasted_iota(jnp.int32, (h, h), 1)
    corner = gram[h:, h:]
    diagonal = jnp.sum(jnp.where(row == column, corner, 0.0), axis=0, keepdims=True)
    mixed = jnp.where(row >= column, gram[:h, :h], corner)
    first = side_ref[0] == 0
    keep_ref[:h, :] = jnp.where(first, gram[h:, :h], mixed)
    send_ref[:h, :] = jnp.where(first, mixed, gram[h:, :h])
    keep_ref[h:, :] = jnp.broadcast_to(diagonal, (8, h))
    send_ref[h:, :] = jnp.broadcast_to(diagonal, (8, h))


def gram_halves(side, kept, arrived):
    rows, n = kept.shape
    half = jax.ShapeDtypeStruct((n // 2 + 8, n // 2), F32)
    return pl.pallas_call(
        gram_kernel,
        out_shape=[jax.ShapeDtypeStruct((rows, n), F32), half, half],
        in_specs=[SMEM, VMEM, VMEM],
        out_specs=[VMEM] * 3,
        compiler_params=params(),
        cost_estimate=pl.CostEstimate(
            flops=8 * rows * n * n, bytes_accessed=12 * rows * n + 4 * n * n, transcendentals=0
        ),
    )(side, kept, arrived)


def inverse_root(x):
    y = lax.rsqrt(x)
    return y * (1.5 - 0.5 * x * y * y)


def factor(a, upper, inverse):
    n = a.shape[0]
    lane = lax.broadcasted_iota(jnp.int32, (8, n), 1)
    sub = lax.broadcasted_iota(jnp.int32, (8, n), 0)
    lane1 = lax.broadcasted_iota(jnp.int32, (8, 128), 1)
    sub1 = lax.broadcasted_iota(jnp.int32, (8, 128), 0)
    groups = PANEL // 8

    def wide(v):
        return jnp.concatenate([v] * (n // 128), axis=1)

    def column(v, c):
        return jnp.broadcast_to(v[:, c : c + 1], (8, 128))

    def row(v, k):
        return jnp.broadcast_to(v[k : k + 1, :], (8, v.shape[1]))

    for start in range(0, n, PANEL):
        tile = start // 128
        t = [a[start + 8 * i : start + 8 * i + 8, :] for i in range(groups)]
        e = [jnp.where(lane1 + 128 * tile == sub1 + (start + 8 * i), 1.0, 0.0) for i in range(groups)]
        for q in range(groups):
            c0 = start + 8 * q
            c = [column(t[q], c0 + j) for j in range(8)]
            s = {(k, j): row(c[j], k) for j in range(8) for k in range(j, 8)}
            r, m = {}, {}
            for j in range(8):
                r[j] = inverse_root(s[j, j])
                for k in range(j + 1, 8):
                    m[k, j] = s[k, j] * r[j]
                for k in range(j + 1, 8):
                    for i in range(j + 1, k + 1):
                        s[k, i] = s[k, i] - m[k, j] * m[i, j]
            pt = [row(t[q], j) for j in range(8)]
            pe = [row(e[q], j) for j in range(8)]
            for j in range(8):
                pt[j] = pt[j] * wide(r[j])
                pe[j] = pe[j] * r[j]
                for k in range(j + 1, 8):
                    pt[k] = pt[k] - wide(m[k, j]) * pt[j]
                    pe[k] = pe[k] - m[k, j] * pe[j]
            for i in range(q + 1, groups):
                c = [column(t[i], c0 + j) for j in range(8)]
                for j in range(8):
                    c[j] = c[j] * r[j]
                    for k in range(j + 1, 8):
                        c[k] = c[k] - c[j] * m[k, j]
                for j in range(8):
                    t[i] = t[i] - wide(c[j]) * pt[j]
                    e[i] = e[i] - c[j] * pe[j]
            tq, eq = pt[0], pe[0]
            for j in range(1, 8):
                tq = jnp.where(sub == j, pt[j], tq)
                eq = jnp.where(sub1 == j, pe[j], eq)
            t[q], e[q] = tq, eq
        done = (lane >= start) & (lane < start + PANEL)
        mixed = []
        for i in range(groups):
            top = start + 8 * i
            parts = [jnp.zeros((8, 128), F32)] * (n // 128)
            parts[tile] = e[i]
            own = jnp.concatenate(parts, axis=1)
            upper[top : top + 8, :] = jnp.where(lane >= sub + top, t[i], 0.0)
            inverse[top : top + 8, :] = jnp.where(lane < start, t[i], own)
            mixed.append(jnp.where(done, own, t[i]))
        after = start + PANEL
        if after < n:
            base = after // 128 * 128
            left = jnp.concatenate([v[:, base:] for v in t], axis=0)
            update = dot_stacked(left, jnp.concatenate(mixed, axis=0))
            for top in range(after, n, 8):
                old = jnp.where(done, 0.0, a[top : top + 8, :])
                a[top : top + 8, :] = old - update[top - base : top - base + 8, :]


def basis_kernel(scale, side_ref, mine_ref, other_ref, rotation_ref, sketched_ref, basis_ref, triangle_ref, a, upper, inverse):
    n = a.shape[0]
    h = n // 2
    first = side_ref[0] == 0
    mine, other = mine_ref[...], other_ref[...]
    below = jnp.where(first, mine[:h, :], other[:h, :])
    mixed = jnp.where(first, other[:h, :], mine[:h, :])
    flipped = mixed.T
    row = lax.broadcasted_iota(jnp.int32, (h, h), 0)
    column = lax.broadcasted_iota(jnp.int32, (h, h), 1)
    diagonal = jnp.broadcast_to(mine[h : h + 1, :], (h, h))
    a[:h, :h] = jnp.where(row >= column, mixed, flipped)
    a[h:, :h] = below
    a[:h, h:] = below.T
    a[h:, h:] = jnp.where(row < column, mixed, jnp.where(row > column, flipped, diagonal))
    factor(a, upper, inverse)
    triangle_ref[...] = upper[...] * (1.0 / scale)
    mapping = dot_parts(inverse[...], scale * rotation_ref[...], ((0,), (0,)))
    basis_ref[...] = dot_parts(sketched_ref[...], mapping, ((1,), (0,)))


def basis_and_triangle(side, mine, other, rotation, sketched, scale):
    (rows, n) = sketched.shape
    return pl.pallas_call(
        functools.partial(basis_kernel, scale),
        out_shape=[jax.ShapeDtypeStruct((rows, n), F32), jax.ShapeDtypeStruct((n, n), F32)],
        in_specs=[SMEM, VMEM, VMEM, VMEM, VMEM],
        out_specs=[VMEM] * 2,
        scratch_shapes=[pltpu.VMEM((n, n), F32)] * 3,
        compiler_params=params(),
        cost_estimate=pl.CostEstimate(
            flops=12 * rows * n * n + 40 * n * n * n, bytes_accessed=8 * rows * n + 12 * n * n, transcendentals=n
        ),
    )(side, mine, other, rotation, sketched)


def shards(snapshots, sketch, rotation):
    groups, depth = lax.axis_size("tm"), levels("tm")
    rows = snapshots.shape[0] // groups
    cells = snapshots.shape[0] * lax.axis_size("space")
    index = lax.axis_index("tm").astype(jnp.int32)
    side = (index & 1).reshape(1)

    def masks(low):
        half = groups // 2
        return jnp.array(
            [low | sum((1 - (p >> (depth - 1 - l) & 1)) << l for l in range(1, depth)) for p in range(half)], jnp.int32
        )

    leaving = sketch_blocks(index ^ masks(1), snapshots, sketch, rows)
    arrived = partner(leaving, "tm", 0)
    kept = sketch_blocks(index ^ masks(0), snapshots, sketch, rows)
    for level in range(1, depth):
        middle = kept.shape[0] // 2
        leaving = kept[:middle] + arrived[:middle]
        kept = kept[middle:] + arrived[middle:]
        arrived = partner(leaving, "tm", level)
    sketched, mine, send = gram_halves(side, kept[0], arrived[0])
    mine = mine + partner(send, "tm", 0)
    for level in range(1, depth):
        mine = mine + partner(mine, "tm", level)
    for level in range(levels("space")):
        mine = mine + partner(mine, "space", level)
    other = partner(mine, "tm", 0)
    return tuple(basis_and_triangle(side, mine, other, rotation, sketched, math.sqrt(cells)))


def solution(mesh):
    in_specs = (P("space", "tm"), P("tm", None), P())
    out_specs = (P(("space", "tm"), None), P())
    return jax.shard_map(shards, mesh=mesh, in_specs=in_specs, out_specs=out_specs, check_vma=False)
```

time: 160 us -> 57.5 us (0.36)
  other arithmetic: 54.9 us -> 0.85 us
  waiting for transfers between devices: 65.9 us -> 26.4 us
  between operations: 15.5 us -> 0.71 us
  Pallas kernels: 0 us -> 14 us
  matrix products: 9.81 us -> 0 us
  starting transfers between devices: 6.63 us -> 12.8 us
  local copies, waits for them, and re-layouts: 7.14 us -> 2.56 us
    another operation x8 -> x0, other arithmetic: 54.6 us -> none  [the longest x6 34.1 us: shards(): lower = jnp.linalg.cholesky(gram)]
    reduce_scatter x1 -> x0, waiting for transfers between devices: 34.3 us -> none  [shards(): lax.psum_scatter(jnp.dot(snapshots, sketch, preferred_element_type=jnp.fl...]
    pallas_call x0 -> x4, Pallas kernels: none -> 14 us  [the longest x1 11.1 us: basis_and_triangle(): pl.pallas_call(functools.partial(basis_kernel, scale), out_shape=[jax.Sha...]
    dot_general x3 -> x0, matrix products: 7.92 us -> none  [the longest x1 2.99 us: shards(): jnp.dot(snapshots, sketch, preferred_element_type=jnp.float32)]
    ppermute x5 -> x8, starting transfers between devices: 6.59 us -> 12.8 us  [partner(): lax.ppermute(shard, axis, [(i, i ^ 1 << level) for i in range(lax.axis_si...]
    ppermute x5 -> x8, waiting for transfers between devices: 31.6 us -> 26.4 us  [partner(): lax.ppermute(shard, axis, [(i, i ^ 1 << level) for i in range(lax.axis_si...]
    another operation x9 -> x0, local copies, waits for them, and re-layouts: 3.97 us -> none
    another operation x5 -> x0, matrix products: 1.89 us -> none  [the longest x3 1.42 us: shards(): lax.linalg.triangular_solve(lower, sketched, left_side=False, lower=True,...]
  transfers between devices with their start and end apart: 6 -> 8, of which waited for: 6 -> 8; matrix products, arithmetic and copies ran while one was open for 0% -> 0% of each run, Pallas kernels for 0% -> 2%
where the time goes in v1:
time: 57.5 us; the launch traced here: 57.3 us
  waiting for transfers between devices  26.4 us (46%)
  Pallas kernels  14 us (24%)
  starting transfers between devices  12.8 us (22%)
  local copies, waits for them, and re-layouts  2.56 us (4%)
  other arithmetic  0.85 us (1%)
  between operations  0.71 us (1%)
    ppermute x8, waiting for transfers between devices, partner(): lax.ppermute(shard, axis, [(i, i ^ 1 << level) for i in range(lax.axis_si...  26.4 us
    ppermute x8, starting transfers between devices, partner(): lax.ppermute(shard, axis, [(i, i ^ 1 << level) for i in range(lax.axis_si...  12.8 us
    pallas_call x1, Pallas kernels, basis_and_triangle(): pl.pallas_call(functools.partial(basis_kernel, scale), out_shape=[jax.Sha...  11.1 us
    unnamed x12, local copies, waits for them, and re-layouts  2.56 us
    pallas_call x2, Pallas kernels, sketch_blocks(): pl.pallas_call(sketch_kernel, grid_spec=pltpu.PrefetchScalarGridSpec(num_...  2.32 us
  transfers between devices with their start and end apart: 8, of which 8 were waited for; matrix products, arithmetic and copies ran while one was open for 0% of the time, Pallas kernels for 2%

profile of v1, /device:TPU:0, one launch (start us, length us, event | category | flops | bytes accessed | tf_op | source)
XLA Modules:
  0.0 57.3 jit_solution(4609660422110610646)
XLA Ops:
  0.6 0.0 copy-start.5
  0.6 0.7 %broadcast_xor_fusion.blocks_ref = s32[2]{0:T(128)S(1)} fusion(s32[2]{0:T(128)} %constant.10.clone, s32[]{:T(128)S(6)} %axis_index.12), kind=kLoop, calls=%fused_computation.3 | loop fusion | flops 2 | bytes 20 | tf_op jit(solution)/shard_map/xor | solution.py:247
  1.3 0.0 copy-start
  1.3 1.6 %copy-done = bf16[2048,512]{1,0:T(8,128)(2,1)S(1)} copy-done((bf16[2048,512]{1,0:T(8,128)(2,1)S(1)}, bf16[2048,512]{1,0:T(8,128)(2,1)}, u32[]{:S(2)}) %copy-start) | copy-done | bytes 2097176
  2.9 0.0 copy-start.2
  2.9 0.9 %copy-done.2 = bf16[512,256]{1,0:T(8,128)(2,1)S(1)} copy-done((bf16[512,256]{1,0:T(8,128)(2,1)S(1)}, bf16[512,256]{1,0:T(8,128)(2,1)}, u32[]{:S(2)}) %copy-start.2) | copy-done | bytes 262168
  3.9 1.2 %shard_map.69 = f32[2,512,256]{2,1,0:T(8,128)S(1)} custom-call(s32[2]{0:T(128)S(1)} %broadcast_xor_fusion.blocks_ref, bf16[2048,512]{1,0:T(8,128)(2,1)S(1)} %copy-done, bf16[512,256]{1,0:T(8,128)(2,1)S(1)} %copy-done.2), custom_call_target="tpu_custom_call" | custom-call | flops 268435456 | bytes 2359296 | tf_op jit(solution)/shard_map/pallas_call | solution.py:62
  5.0 0.5 collective-permute-start
  5.5 0.0 copy-done.5
  5.5 0.0 copy-done.1
  5.6 0.0 copy-done.3
  5.6 1.2 %shard_map.68 = f32[2,512,256]{2,1,0:T(8,128)S(1)} custom-call(s32[2]{0:T(128)S(1)} %broadcast_xor_fusion.1.blocks_ref, bf16[2048,512]{1,0:T(8,128)(2,1)S(1)} %copy-done.1, bf16[512,256]{1,0:T(8,128)(2,1)S(1)} %copy-done.3), custom_call_target="tpu_custom_call" | custom-call | flops 268435456 | bytes 2359296 | tf_op jit(solution)/shard_map/pallas_call | solution.py:62
  6.7 0.0 copy-start.4
  6.7 1.1 %collective-permute-done = f32[2,512,256]{2,1,0:T(8,128)S(1)} collective-permute-done((f32[2,512,256]{2,1,0:T(8,128)S(1)}, f32[2,512,256]{2,1,0:T(8,128)S(1)}, u32[]{:S(2)}, u32[]{:S(2)}) %collective-permute-start) | collective-permute-done | bytes 1048608 | tf_op jit(solution)/shard_map/ppermute | solution.py:22
  7.8 0.1 slice_add_fusion
  8.0 2.9 %collective-permute-start.1 = (f32[1,512,256]{2,1,0:T(8,128)S(1)}, f32[1,512,256]{2,1,0:T(8,128)S(1)}, u32[]{:S(2)}, u32[]{:S(2)}) collective-permute-start(f32[1,512,256]{2,1,0:T(8,128)S(1)} %get-tuple-element.8), channel_id=1, source_target_pairs={{0,2},{1,3},{2,0},{3,1},{4,6},{5,7},{6,4},{7,5},{8,10},{9,11},{10,... | collective-permute-start | bytes 1572872 | tf_op jit(solution)/shard_map/ppermute | solution.py:22
  10.9 12.2 %collective-permute-done.1 = f32[1,512,256]{2,1,0:T(8,128)S(1)} collective-permute-done((f32[1,512,256]{2,1,0:T(8,128)S(1)}, f32[1,512,256]{2,1,0:T(8,128)S(1)}, u32[]{:S(2)}, u32[]{:S(2)}) %collective-permute-start.1) | collective-permute-done | bytes 524320 | tf_op jit(solution)/shard_map/ppermute | solution.py:22
  23.1 0.5 shard_map.70
  23.7 0.1 collective-permute-start.2
  23.7 1.2 %collective-permute-done.2 = f32[136,128]{1,0:T(8,128)S(1)} collective-permute-done((f32[136,128]{1,0:T(8,128)S(1)}, f32[136,128]{1,0:T(8,128)S(1)}, u32[]{:S(2)}, u32[]{:S(2)}) %collective-permute-start.2) | collective-permute-done | bytes 69664 | tf_op jit(solution)/shard_map/ppermute | solution.py:22
  25.0 1.8 %collective-permute-start.3 = (f32[136,128]{1,0:T(8,128)S(1)}, f32[136,128]{1,0:T(8,128)S(1)}, u32[]{:S(2)}, u32[]{:S(2)}) collective-permute-start(f32[136,128]{1,0:T(8,128)S(1)} %add.23), channel_id=1, source_target_pairs={{0,2},{1,3},{2,0},{3,1},{4,6},{5,7},{6,4},{7,5},{8,10},{9,11},{10,... | collective-permute-start | bytes 208904 | tf_op jit(solution)/shard_map/ppermute | solution.py:22
  26.8 2.6 %collective-permute-done.3 = f32[136,128]{1,0:T(8,128)S(1)} collective-permute-done((f32[136,128]{1,0:T(8,128)S(1)}, f32[136,128]{1,0:T(8,128)S(1)}, u32[]{:S(2)}, u32[]{:S(2)}) %collective-permute-start.3) | collective-permute-done | bytes 69664 | tf_op jit(solution)/shard_map/ppermute | solution.py:22
  29.4 1.8 %collective-permute-start.4 = (f32[136,128]{1,0:T(8,128)S(1)}, f32[136,128]{1,0:T(8,128)S(1)}, u32[]{:S(2)}, u32[]{:S(2)}) collective-permute-start(f32[136,128]{1,0:T(8,128)S(1)} %add.24), channel_id=1, source_target_pairs={{0,4},{4,0},{8,12},{12,8},{16,20},{20,16},{24,28},{28,24},{1,5},{5... | collective-permute-start | bytes 208904 | tf_op jit(solution)/shard_map/ppermute | solution.py:22
  31.2 2.5 %collective-permute-done.4 = f32[136,128]{1,0:T(8,128)S(1)} collective-permute-done((f32[136,128]{1,0:T(8,128)S(1)}, f32[136,128]{1,0:T(8,128)S(1)}, u32[]{:S(2)}, u32[]{:S(2)}) %collective-permute-start.4) | collective-permute-done | bytes 69664 | tf_op jit(solution)/shard_map/ppermute | solution.py:22
  33.8 1.9 %collective-permute-start.5 = (f32[136,128]{1,0:T(8,128)S(1)}, f32[136,128]{1,0:T(8,128)S(1)}, u32[]{:S(2)}, u32[]{:S(2)}) collective-permute-start(f32[136,128]{1,0:T(8,128)S(1)} %add.25), channel_id=1, source_target_pairs={{0,8},{4,12},{8,0},{12,4},{16,24},{20,28},{24,16},{28,20},{1,9},{5... | collective-permute-start | bytes 208904 | tf_op jit(solution)/shard_map/ppermute | solution.py:22
  35.7 2.5 %collective-permute-done.5 = f32[136,128]{1,0:T(8,128)S(1)} collective-permute-done((f32[136,128]{1,0:T(8,128)S(1)}, f32[136,128]{1,0:T(8,128)S(1)}, u32[]{:S(2)}, u32[]{:S(2)}) %collective-permute-start.5) | collective-permute-done | bytes 69664 | tf_op jit(solution)/shard_map/ppermute | solution.py:22
  38.2 3.6 %collective-permute-start.6 = (f32[136,128]{1,0:T(8,128)S(1)}, f32[136,128]{1,0:T(8,128)S(1)}, u32[]{:S(2)}, u32[]{:S(2)}) collective-permute-start(f32[136,128]{1,0:T(8,128)S(1)} %add.26), channel_id=1, source_target_pairs={{0,16},{4,20},{8,24},{12,28},{16,0},{20,4},{24,8},{28,12},{1,17},{... | collective-permute-start | bytes 208904 | tf_op jit(solution)/shard_map/ppermute | solution.py:22
  41.8 3.0 %collective-permute-done.6 = f32[136,128]{1,0:T(8,128)S(1)} collective-permute-done((f32[136,128]{1,0:T(8,128)S(1)}, f32[136,128]{1,0:T(8,128)S(1)}, u32[]{:S(2)}, u32[]{:S(2)}) %collective-permute-start.6) | collective-permute-done | bytes 69664 | tf_op jit(solution)/shard_map/ppermute | solution.py:22
  44.9 0.1 collective-permute-start.7
  44.9 1.2 %collective-permute-done.7.other_ref = f32[136,128]{1,0:T(8,128)S(1)} collective-permute-done((f32[136,128]{1,0:T(8,128)S(1)}, f32[136,128]{1,0:T(8,128)S(1)}, u32[]{:S(2)}, u32[]{:S(2)}) %collective-permute-start.7) | collective-permute-done | bytes 69664 | tf_op jit(solution)/shard_map/ppermute | solution.py:22
  46.2 0.0 copy-done.4
  46.2 11.1 %shard_map.71 = (f32[512,256]{1,0:T(8,128)}, f32[256,256]{1,0:T(8,128)}) custom-call(s32[1]{0:T(128)} %bitcast.side_ref, f32[136,128]{1,0:T(8,128)S(1)} %add.27.mine_ref, f32[136,128]{1,0:T(8,128)S(1)} %collective-permute-done.7.other_ref, f32[256,256]{1,0:T(8,128)S(1)} %copy-done.4, f32[512,256]{1,0:T(8,128)S(1)} %get-tuple-element.7.sketched_ref), custom_call_target="tpu_custom_call" | custom-call | flops 1073741824 | bytes 1835008 | tf_op jit(solution)/shard_map/pallas_call | solution.py:221
  (8 shorter events, 0.1 us)
Async XLA Ops:
  0.6 4.9 %copy-start.5 = (s32[2]{0:T(128)S(1)}, s32[2]{0:T(128)}, u32[]{:S(2)}) copy-start(s32[2]{0:T(128)} %constant.11.clone) | copy-start | bytes 28
  1.3 1.6 %copy-start = (bf16[2048,512]{1,0:T(8,128)(2,1)S(1)}, bf16[2048,512]{1,0:T(8,128)(2,1)}, u32[]{:S(2)}) copy-start(bf16[2048,512]{1,0:T(8,128)(2,1)} %snapshots_ref.3) | copy-start | bytes 6291460
  2.9 0.9 %copy-start.2 = (bf16[512,256]{1,0:T(8,128)(2,1)S(1)}, bf16[512,256]{1,0:T(8,128)(2,1)}, u32[]{:S(2)}) copy-start(bf16[512,256]{1,0:T(8,128)(2,1)} %sketch_ref.3) | copy-start | bytes 786436
  3.9 1.7 %copy-start.1 = (bf16[2048,512]{1,0:T(8,128)(2,1)S(1)}, bf16[2048,512]{1,0:T(8,128)(2,1)}, u32[]{:S(2)}) copy-start(bf16[2048,512]{1,0:T(8,128)(2,1)} %snapshots_ref.3) | copy-start | bytes 6291460
  3.9 1.7 %copy-start.3 = (bf16[512,256]{1,0:T(8,128)(2,1)S(1)}, bf16[512,256]{1,0:T(8,128)(2,1)}, u32[]{:S(2)}) copy-start(bf16[512,256]{1,0:T(8,128)(2,1)} %sketch_ref.3) | copy-start | bytes 786436
  5.0 2.8 %collective-permute-start = (f32[2,512,256]{2,1,0:T(8,128)S(1)}, f32[2,512,256]{2,1,0:T(8,128)S(1)}, u32[]{:S(2)}, u32[]{:S(2)}) collective-permute-start(f32[2,512,256]{2,1,0:T(8,128)S(1)} %shard_map.69), channel_id=1, source_target_pairs={{0,1},{1,0},{2,3},{3,2},{4,5},{5,4},{6,7},{7,6},{8,9},{9,8},{10,11... | collective-permute-start | bytes 3145736 | tf_op jit(solution)/shard_map/ppermute | solution.py:22
  6.7 39.5 %copy-start.4 = (f32[256,256]{1,0:T(8,128)S(1)}, f32[256,256]{1,0:T(8,128)}, u32[]{:S(2)}) copy-start(f32[256,256]{1,0:T(8,128)} %rotation_ref.1) | copy-start | bytes 786436
  8.0 15.1 %collective-permute-start.1 = (f32[1,512,256]{2,1,0:T(8,128)S(1)}, f32[1,512,256]{2,1,0:T(8,128)S(1)}, u32[]{:S(2)}, u32[]{:S(2)}) collective-permute-start(f32[1,512,256]{2,1,0:T(8,128)S(1)} %get-tuple-element.8), channel_id=1, source_target_pairs={{0,2},{1,3},{2,0},{3,1},{4,6},{5,7},{6,4},{7,5},{8,10},{9,11},{10,... | collective-permute-start | bytes 1572872 | tf_op jit(solution)/shard_map/ppermute | solution.py:22
  23.7 1.3 %collective-permute-start.2 = (f32[136,128]{1,0:T(8,128)S(1)}, f32[136,128]{1,0:T(8,128)S(1)}, u32[]{:S(2)}, u32[]{:S(2)}) collective-permute-start(f32[136,128]{1,0:T(8,128)S(1)} %get-tuple-element.6), channel_id=1, source_target_pairs={{0,1},{1,0},{2,3},{3,2},{4,5},{5,4},{6,7},{7,6},{8,9},{9,8},{10,11... | collective-permute-start | bytes 208904 | tf_op jit(solution)/shard_map/ppermute | solution.py:22
  25.0 4.4 %collective-permute-start.3 = (f32[136,128]{1,0:T(8,128)S(1)}, f32[136,128]{1,0:T(8,128)S(1)}, u32[]{:S(2)}, u32[]{:S(2)}) collective-permute-start(f32[136,128]{1,0:T(8,128)S(1)} %add.23), channel_id=1, source_target_pairs={{0,2},{1,3},{2,0},{3,1},{4,6},{5,7},{6,4},{7,5},{8,10},{9,11},{10,... | collective-permute-start | bytes 208904 | tf_op jit(solution)/shard_map/ppermute | solution.py:22
  29.4 4.4 %collective-permute-start.4 = (f32[136,128]{1,0:T(8,128)S(1)}, f32[136,128]{1,0:T(8,128)S(1)}, u32[]{:S(2)}, u32[]{:S(2)}) collective-permute-start(f32[136,128]{1,0:T(8,128)S(1)} %add.24), channel_id=1, source_target_pairs={{0,4},{4,0},{8,12},{12,8},{16,20},{20,16},{24,28},{28,24},{1,5},{5... | collective-permute-start | bytes 208904 | tf_op jit(solution)/shard_map/ppermute | solution.py:22
  33.8 4.4 %collective-permute-start.5 = (f32[136,128]{1,0:T(8,128)S(1)}, f32[136,128]{1,0:T(8,128)S(1)}, u32[]{:S(2)}, u32[]{:S(2)}) collective-permute-start(f32[136,128]{1,0:T(8,128)S(1)} %add.25), channel_id=1, source_target_pairs={{0,8},{4,12},{8,0},{12,4},{16,24},{20,28},{24,16},{28,20},{1,9},{5... | collective-permute-start | bytes 208904 | tf_op jit(solution)/shard_map/ppermute | solution.py:22
  38.2 6.7 %collective-permute-start.6 = (f32[136,128]{1,0:T(8,128)S(1)}, f32[136,128]{1,0:T(8,128)S(1)}, u32[]{:S(2)}, u32[]{:S(2)}) collective-permute-start(f32[136,128]{1,0:T(8,128)S(1)} %add.26), channel_id=1, source_target_pairs={{0,16},{4,20},{8,24},{12,28},{16,0},{20,4},{24,8},{28,12},{1,17},{... | collective-permute-start | bytes 208904 | tf_op jit(solution)/shard_map/ppermute | solution.py:22
  44.9 1.3 %collective-permute-start.7 = (f32[136,128]{1,0:T(8,128)S(1)}, f32[136,128]{1,0:T(8,128)S(1)}, u32[]{:S(2)}, u32[]{:S(2)}) collective-permute-start(f32[136,128]{1,0:T(8,128)S(1)} %add.27.mine_ref), channel_id=1, source_target_pairs={{0,1},{1,0},{2,3},{3,2},{4,5},{5,4},{6,7},{7,6},{8,9},{9,8},{10,11... | collective-permute-start | bytes 208904 | tf_op jit(solution)/shard_map/ppermute | solution.py:22

commit v2 on v1

v2 whole, which is shorter than its diff:
```python
import functools
import math

import jax
import jax.numpy as jnp
from jax import lax
from jax.experimental import pallas as pl
from jax.experimental.pallas import tpu as pltpu
from jax.sharding import PartitionSpec as P

F32, BF16 = jnp.float32, jnp.bfloat16
VMEM = pl.BlockSpec(memory_space=pltpu.VMEM)
SMEM = pl.BlockSpec(memory_space=pltpu.SMEM)
BLOCK = 64
PANEL = 2


def params():
    return pltpu.CompilerParams(vmem_limit_bytes=40 << 20)


def partner(shard, axis, level):
    return lax.ppermute(shard, axis, [(i, i ^ 1 << level) for i in range(lax.axis_size(axis))])


def levels(axis):
    return lax.axis_size(axis).bit_length() - 1


def split(x):
    high = x.astype(BF16)
    rest = x - high.astype(F32)
    middle = rest.astype(BF16)
    low = (rest - middle.astype(F32)).astype(BF16)
    return high, middle, low


def product(x, y, dims):
    return lax.dot_general(x, y, (dims, ((), ())), preferred_element_type=F32)


def dot_parts(x, y, dims):
    x1, x2, x3 = split(x)
    y1, y2, y3 = split(y)
    small = product(x1, y3, dims) + product(x2, y2, dims) + product(x3, y1, dims)
    return product(x1, y1, dims) + (product(x1, y2, dims) + product(x2, y1, dims) + small)


PIECES = 4


def sketch_kernel(masks, snapshots_ref, sketch_ref, *rest):
    outs, (tall, wide, arrived, ready) = rest[: len(masks)], rest[len(masks) :]
    rows, step = tall.shape[0] // len(masks), tall.shape[0] // len(masks) // PIECES
    index = lax.axis_index("tm")
    fetch = pltpu.make_async_copy(sketch_ref, wide, ready)
    fetch.start()
    copies = []
    for i, mask in enumerate(masks):
        start = pl.multiple_of((index ^ mask) * rows, rows)
        for j in range(PIECES):
            copies.append(
                pltpu.make_async_copy(
                    snapshots_ref.at[pl.ds(start + step * j, step)],
                    tall.at[pl.ds(rows * i + step * j, step)],
                    arrived.at[PIECES * i + j],
                )
            )
            copies[-1].start()
    fetch.wait()
    for i, out in enumerate(outs):
        for j in range(PIECES):
            copies[PIECES * i + j].wait()
            block = tall[rows * i + step * j : rows * i + step * (j + 1), :]
            out[step * j : step * (j + 1), :] = jnp.dot(block, wide[...], preferred_element_type=F32)


def sketch_blocks(masks, snapshots, sketch):
    rows = snapshots.shape[0] // lax.axis_size("tm")
    depth, columns = sketch.shape
    count = len(masks)
    return pl.pallas_call(
        functools.partial(sketch_kernel, masks),
        out_shape=[jax.ShapeDtypeStruct((rows, columns), F32)] * count,
        in_specs=[pl.BlockSpec(memory_space=pltpu.HBM)] * 2,
        out_specs=[VMEM] * count,
        scratch_shapes=[
            pltpu.VMEM((count * rows, depth), BF16),
            pltpu.VMEM((depth, columns), BF16),
            pltpu.SemaphoreType.DMA((PIECES * count,)),
            pltpu.SemaphoreType.DMA,
        ],
        compiler_params=params(),
        cost_estimate=pl.CostEstimate(
            flops=2 * count * rows * depth * columns,
            bytes_accessed=count * rows * (2 * depth + 4 * columns) + 2 * depth * columns,
            transcendentals=0,
        ),
    )(snapshots, sketch)


def gram_kernel(side_ref, kept_ref, near_ref, far_ref, sketched_ref, keep_ref, send_ref):
    sketched = (kept_ref[...] + near_ref[...]) + far_ref[...]
    sketched_ref[...] = sketched
    high, middle, low = split(sketched)
    rows = ((0,), (0,))
    cross = product(high, middle, rows) + product(high, low, rows)
    gram = product(high, high, rows) + (cross + cross.T + product(middle, middle, rows))
    h = gram.shape[0] // 2
    row = lax.broadcasted_iota(jnp.int32, (h, h), 0)
    column = lax.broadcasted_iota(jnp.int32, (h, h), 1)
    corner = gram[h:, h:]
    diagonal = jnp.sum(jnp.where(row == column, corner, 0.0), axis=0, keepdims=True)
    mixed = jnp.where(row >= column, gram[:h, :h], corner)
    first = side_ref[0] == 0
    keep_ref[:h, :] = jnp.where(first, gram[h:, :h], mixed)
    send_ref[:h, :] = jnp.where(first, mixed, gram[h:, :h])
    keep_ref[h:, :] = jnp.broadcast_to(diagonal, (8, h))
    send_ref[h:, :] = jnp.broadcast_to(diagonal, (8, h))


def gram_halves(side, kept, near, far):
    rows, n = kept.shape
    half = jax.ShapeDtypeStruct((n // 2 + 8, n // 2), F32)
    return pl.pallas_call(
        gram_kernel,
        out_shape=[jax.ShapeDtypeStruct((rows, n), F32), half, half],
        in_specs=[SMEM, VMEM, VMEM, VMEM],
        out_specs=[VMEM] * 3,
        compiler_params=params(),
        cost_estimate=pl.CostEstimate(
            flops=8 * rows * n * n, bytes_accessed=16 * rows * n + 4 * n * n, transcendentals=0
        ),
    )(side, kept, near, far)


def column(v, c):
    return jnp.broadcast_to(v[:, c : c + 1], (8, 128))


def row(v, k):
    return jnp.broadcast_to(v[k : k + 1, :], (8, 128))


def stacked(x, order):
    parts = split(x)
    return jnp.concatenate([parts[i] for i in order], axis=0)


def factor(a, upper, inverse):
    n = a.shape[0]
    tiles = n // 128
    lane = lax.broadcasted_iota(jnp.int32, (8, 128), 1)
    sub = lax.broadcasted_iota(jnp.int32, (8, 128), 0)
    groups, width = BLOCK // 8, 8 * PANEL
    zero = jnp.zeros((8, 128), F32)
    for start in range(0, n, BLOCK):
        tile, offset = divmod(start, 128)
        t = []
        for i in range(groups):
            top = start + 8 * i
            t.append([a[top : top + 8, 128 * x : 128 * x + 128] for x in range(tiles)])
            t[i].append(jnp.where(lane == sub + (offset + 8 * i), 1.0, 0.0))
        for q in range(0, groups, PANEL):
            first = offset + 8 * q
            c = {(g, j): column(t[q + g][tile], first + j) for g in range(PANEL) for j in range(8 * g + 8)}
            r, l, m = {}, {}, {}
            pivot = row(c[0, 0], 0)
            for j in range(width):
                r[j] = lax.rsqrt(pivot)
                if j + 1 < width:
                    g, k = divmod(j + 1, 8)
                    m[j + 1, j] = row(c[g, j], k) * r[j]
                    pivot = row(c[g, j + 1], k) - m[j + 1, j] * m[j + 1, j]
                for g in range(j // 8, PANEL):
                    l[g, j] = c[g, j] * r[j]
                for k in range(j + 1, width):
                    if k > j + 1:
                        m[k, j] = row(l[k // 8, j], k % 8)
                    for g in range(k // 8, PANEL):
                        c[g, k] = c[g, k] - l[g, j] * m[k, j]
            p = {}
            for g in range(PANEL):
                mine = t[q + g]
                for j in range(8 * g):
                    mine = [x - l[g, j] * y for x, y in zip(mine, p[j])]
                roots = r[8 * g]
                for jj in range(8):
                    j = 8 * g + jj
                    p[j] = [row(x, jj) * r[j] for x in mine]
                    below = jnp.where(sub > jj, l[g, j], 0.0)
                    mine = [x - below * y for x, y in zip(mine, p[j])]
                    roots = jnp.where(sub == jj, r[j], roots)
                t[q + g] = [x * roots for x in mine]
            for i in range(q + PANEL, groups):
                for g in range(PANEL):
                    c = [column(t[i][tile], first + 8 * g + jj) for jj in range(8)]
                    for jj in range(8):
                        c[jj] = c[jj] * r[8 * g + jj]
                        for kk in range(jj + 1, 8):
                            c[kk] = c[kk] - c[jj] * m[8 * g + kk, 8 * g + jj]
                    for jj in range(8):
                        t[i] = [x - c[jj] * y for x, y in zip(t[i], p[8 * g + jj])]
        done = (lane >= offset) & (lane < offset + BLOCK)
        left, right = [[] for _ in range(tiles)], [[] for _ in range(tiles)]
        for i in range(groups):
            top, own = start + 8 * i, t[i][tiles]
            for x in range(tiles):
                u = w = z = t[i][x]
                if x < tile:
                    u = zero
                elif x > tile:
                    w = zero
                else:
                    u = jnp.where(lane >= sub + (offset + 8 * i), u, 0.0)
                    w = jnp.where(lane < offset, w, own)
                    z = jnp.where(done, own, z)
                upper[top : top + 8, 128 * x : 128 * x + 128] = u
                inverse[top : top + 8, 128 * x : 128 * x + 128] = w
                left[x].append(u)
                right[x].append(z)
        after = start + BLOCK
        if after < n:
            y = stacked(jnp.concatenate([jnp.concatenate(v, axis=0) for v in right], axis=1), (0, 1, 0, 2, 1, 0))
            for x in range(after // 128, tiles):
                update = product(stacked(jnp.concatenate(left[x], axis=0), (0, 0, 1, 0, 1, 2)), y, ((0,), (0,)))
                for top in range(max(after, 128 * x), 128 * x + 128, 8):
                    for k in range(tiles):
                        old = a[top : top + 8, 128 * k : 128 * k + 128]
                        if k == tile:
                            old = jnp.where(done, 0.0, old)
                        new = update[top - 128 * x : top - 128 * x + 8, 128 * k : 128 * k + 128]
                        a[top : top + 8, 128 * k : 128 * k + 128] = old - new


def basis_kernel(scale, side_ref, mine_ref, other_ref, rotation_ref, sketched_ref, basis_ref, triangle_ref, a, upper, inverse):
    n = a.shape[0]
    h = n // 2
    first = side_ref[0] == 0
    mine, other = mine_ref[...], other_ref[...]
    below = jnp.where(first, mine[:h, :], other[:h, :])
    mixed = jnp.where(first, other[:h, :], mine[:h, :])
    flipped = mixed.T
    row = lax.broadcasted_iota(jnp.int32, (h, h), 0)
    column = lax.broadcasted_iota(jnp.int32, (h, h), 1)
    diagonal = jnp.broadcast_to(mine[h : h + 1, :], (h, h))
    a[:h, :h] = jnp.where(row >= column, mixed, flipped)
    a[h:, :h] = below
    a[:h, h:] = below.T
    a[h:, h:] = jnp.where(row < column, mixed, jnp.where(row > column, flipped, diagonal))
    factor(a, upper, inverse)
    triangle_ref[...] = upper[...] * (1.0 / scale)
    mapping = dot_parts(inverse[...], scale * rotation_ref[...], ((0,), (0,)))
    basis_ref[...] = dot_parts(sketched_ref[...], mapping, ((1,), (0,)))


def basis_and_triangle(side, mine, other, rotation, sketched, scale):
    (rows, n) = sketched.shape
    return pl.pallas_call(
        functools.partial(basis_kernel, scale),
        out_shape=[jax.ShapeDtypeStruct((rows, n), F32), jax.ShapeDtypeStruct((n, n), F32)],
        in_specs=[SMEM, VMEM, VMEM, VMEM, VMEM],
        out_specs=[VMEM] * 2,
        scratch_shapes=[pltpu.VMEM((n, n), F32)] * 3,
        compiler_params=params(),
        cost_estimate=pl.CostEstimate(
            flops=12 * rows * n * n + 40 * n * n * n, bytes_accessed=8 * rows * n + 12 * n * n, transcendentals=n
        ),
    )(side, mine, other, rotation, sketched)


def shards(snapshots, sketch, rotation):
    depth = levels("tm")
    cells = snapshots.shape[0] * lax.axis_size("space")
    side = (lax.axis_index("tm").astype(jnp.int32) & 1).reshape(1)

    kept, near = {}, {}
    for mask in range(lax.axis_size("tm") - 2, -1, -2):
        if mask:
            (leaving,) = sketch_blocks([mask | 1], snapshots, sketch)
            (kept[mask],) = sketch_blocks([mask], snapshots, sketch)
        else:
            leaving, kept[mask] = sketch_blocks([mask | 1, mask], snapshots, sketch)
        near[mask] = partner(leaving, "tm", 0)
    for level in range(1, depth):
        for mask in [m for m in kept if m >> level & 1]:
            arrived = partner(kept.pop(mask) + near.pop(mask), "tm", level)
            stays = mask ^ 1 << level
            near[stays] = near[stays] + arrived if level < depth - 1 else near[stays]
    sketched, mine, send = gram_halves(side, kept[0], near[0], arrived)
    mine = mine + partner(send, "tm", 0)
    for level in range(1, depth):
        mine = mine + partner(mine, "tm", level)
    for level in range(levels("space")):
        mine = mine + partner(mine, "space", level)
    other = partner(mine, "tm", 0)
    return tuple(basis_and_triangle(side, mine, other, rotation, sketched, math.sqrt(cells)))


def solution(mesh):
    in_specs = (P("space", "tm"), P("tm", None), P())
    out_specs = (P(("space", "tm"), None), P())
    return jax.shard_map(shards, mesh=mesh, in_specs=in_specs, out_specs=out_specs, check_vma=False)
```

time: 57.5 us -> 56.6 us (0.984)
  waiting for transfers between devices: 26.4 us -> 25.2 us
  Pallas kernels: 14 us -> 14.8 us
  other arithmetic: 0.85 us -> 0.12 us
    pallas_call x2 -> x3, Pallas kernels: 2.32 us -> 6.42 us  [sketch_blocks(): pl.pallas_call(functools.partial(sketch_kernel, masks), out_shape=[jax.Sh...]
    pallas_call x1, Pallas kernels: 11.1 us -> 7.86 us  [basis_and_triangle(): pl.pallas_call(functools.partial(basis_kernel, scale), out_shape=[jax.Sha...]
    ppermute x8 -> x9, waiting for transfers between devices: 26.4 us -> 25.2 us  [partner(): lax.ppermute(shard, axis, [(i, i ^ 1 << level) for i in range(lax.axis_si...]
    xor x2 -> x0, other arithmetic: 0.67 us -> none  [the longest x1 0.66 us: shards(): leaving = sketch_blocks(index ^ masks(1), snapshots, sketch, rows)]
    ppermute x8 -> x9, starting transfers between devices: 12.8 us -> 12.9 us  [partner(): lax.ppermute(shard, axis, [(i, i ^ 1 << level) for i in range(lax.axis_si...]
    unnamed x12 -> x6, local copies, waits for them, and re-layouts: 2.56 us -> 2.54 us
  transfers between devices with their start and end apart: 8 -> 9, of which waited for: 8 -> 7; matrix products, arithmetic and copies ran while one was open for 0% -> 0% of each run, Pallas kernels for 2% -> 9%
where the time goes in v2:
time: 56.6 us; the launch traced here: 56.4 us
  waiting for transfers between devices  25.2 us (45%)
  Pallas kernels  14.8 us (26%)
  starting transfers between devices  12.9 us (23%)
  local copies, waits for them, and re-layouts  2.54 us (4%)
  between operations  0.73 us (1%)
    ppermute x9, waiting for transfers between devices, partner(): lax.ppermute(shard, axis, [(i, i ^ 1 << level) for i in range(lax.axis_si...  25.2 us
    ppermute x9, starting transfers between devices, partner(): lax.ppermute(shard, axis, [(i, i ^ 1 << level) for i in range(lax.axis_si...  12.9 us
    pallas_call x1, Pallas kernels, basis_and_triangle(): pl.pallas_call(functools.partial(basis_kernel, scale), out_shape=[jax.Sha...  7.86 us
    pallas_call x3, Pallas kernels, sketch_blocks(): pl.pallas_call(functools.partial(sketch_kernel, masks), out_shape=[jax.Sh...  6.42 us
    unnamed x6, local copies, waits for them, and re-layouts  2.54 us
  transfers between devices with their start and end apart: 9, of which 7 were waited for; matrix products, arithmetic and copies ran while one was open for 0% of the time, Pallas kernels for 9%

profile of v2, /device:TPU:0, one launch (start us, length us, event | category | flops | bytes accessed | tf_op | source)
XLA Modules:
  0.0 56.4 jit_solution(736976510117595889)
XLA Ops:
  0.6 0.0 copy-start
  0.6 1.6 %copy-done = bf16[2048,512]{1,0:T(8,128)(2,1)S(1)} copy-done((bf16[2048,512]{1,0:T(8,128)(2,1)S(1)}, bf16[2048,512]{1,0:T(8,128)(2,1)}, u32[]{:S(2)}) %copy-start) | copy-done | bytes 2097176
  2.2 0.0 copy-start.1
  2.2 0.9 %copy-done.1 = bf16[512,256]{1,0:T(8,128)(2,1)S(1)} copy-done((bf16[512,256]{1,0:T(8,128)(2,1)S(1)}, bf16[512,256]{1,0:T(8,128)(2,1)}, u32[]{:S(2)}) %copy-start.1) | copy-done | bytes 262168
  3.2 1.6 %shard_map.52 = f32[512,256]{1,0:T(8,128)S(1)} custom-call(bf16[2048,512]{1,0:T(8,128)(2,1)S(1)} %copy-done, bf16[512,256]{1,0:T(8,128)(2,1)S(1)} %copy-done.1), custom_call_target="tpu_custom_call" | custom-call | flops 134217728 | bytes 1310720 | tf_op jit(solution)/shard_map/pallas_call | solution.py:82
  4.8 0.5 collective-permute-start.1
  5.3 3.2 %shard_map.50 = (f32[512,256]{1,0:T(8,128)S(1)}, f32[512,256]{1,0:T(8,128)S(1)}) custom-call(bf16[2048,512]{1,0:T(8,128)(2,1)S(1)} %copy-done, bf16[512,256]{1,0:T(8,128)(2,1)S(1)} %copy-done.1), custom_call_target="tpu_custom_call" | custom-call | flops 268435456 | bytes 2359296 | tf_op jit(solution)/shard_map/pallas_call | solution.py:82
  8.5 0.1 collective-permute-start
  8.6 1.6 %shard_map.51 = f32[512,256]{1,0:T(8,128)S(1)} custom-call(bf16[2048,512]{1,0:T(8,128)(2,1)S(1)} %copy-done, bf16[512,256]{1,0:T(8,128)(2,1)S(1)} %copy-done.1), custom_call_target="tpu_custom_call" | custom-call | flops 134217728 | bytes 1310720 | tf_op jit(solution)/shard_map/pallas_call | solution.py:82
  10.3 0.0 copy-start.2
  10.3 0.0 collective-permute-done.1
  10.3 0.1 add.18
  10.4 3.0 %collective-permute-start.2 = (f32[512,256]{1,0:T(8,128)S(1)}, f32[512,256]{1,0:T(8,128)S(1)}, u32[]{:S(2)}, u32[]{:S(2)}) collective-permute-start(f32[512,256]{1,0:T(8,128)S(1)} %add.18), channel_id=1, source_target_pairs={{0,2},{1,3},{2,0},{3,1},{4,6},{5,7},{6,4},{7,5},{8,10},{9,11},{10,... | collective-permute-start | bytes 1572872 | tf_op jit(solution)/shard_map/ppermute | solution.py:23
  13.4 0.0 collective-permute-done.near_ref
  13.4 12.1 %collective-permute-done.2.far_ref = f32[512,256]{1,0:T(8,128)S(1)} collective-permute-done((f32[512,256]{1,0:T(8,128)S(1)}, f32[512,256]{1,0:T(8,128)S(1)}, u32[]{:S(2)}, u32[]{:S(2)}) %collective-permute-start.2) | collective-permute-done | bytes 524320 | tf_op jit(solution)/shard_map/ppermute | solution.py:23
  25.5 0.6 %shard_map.53 = (f32[512,256]{1,0:T(8,128)S(1)}, f32[136,128]{1,0:T(8,128)S(1)}, f32[136,128]{1,0:T(8,128)S(1)}) custom-call(s32[1]{0:T(128)} %bitcast.side_ref, f32[512,256]{1,0:T(8,128)S(1)} %get-tuple-element.7.kept_ref, f32[512,256]{1,0:T(8,128)S(1)} %collective-permute-done.near_ref, f32[512,256]{1,0:T(8,128)S(1)} %collective-permute-done.2.far_ref), custom_call_target="tpu_custom_call" | custom-call | flops 268435456 | bytes 2359296 | tf_op jit(solution)/shard_map/pallas_call | solution.py:125
  26.0 0.1 collective-permute-start.3
  26.1 1.2 %collective-permute-done.3 = f32[136,128]{1,0:T(8,128)S(1)} collective-permute-done((f32[136,128]{1,0:T(8,128)S(1)}, f32[136,128]{1,0:T(8,128)S(1)}, u32[]{:S(2)}, u32[]{:S(2)}) %collective-permute-start.3) | collective-permute-done | bytes 69664 | tf_op jit(solution)/shard_map/ppermute | solution.py:23
  27.4 1.8 %collective-permute-start.4 = (f32[136,128]{1,0:T(8,128)S(1)}, f32[136,128]{1,0:T(8,128)S(1)}, u32[]{:S(2)}, u32[]{:S(2)}) collective-permute-start(f32[136,128]{1,0:T(8,128)S(1)} %add.19), channel_id=1, source_target_pairs={{0,2},{1,3},{2,0},{3,1},{4,6},{5,7},{6,4},{7,5},{8,10},{9,11},{10,... | collective-permute-start | bytes 208904 | tf_op jit(solution)/shard_map/ppermute | solution.py:23
  29.2 2.6 %collective-permute-done.4 = f32[136,128]{1,0:T(8,128)S(1)} collective-permute-done((f32[136,128]{1,0:T(8,128)S(1)}, f32[136,128]{1,0:T(8,128)S(1)}, u32[]{:S(2)}, u32[]{:S(2)}) %collective-permute-start.4) | collective-permute-done | bytes 69664 | tf_op jit(solution)/shard_map/ppermute | solution.py:23
  31.8 1.8 %collective-permute-start.5 = (f32[136,128]{1,0:T(8,128)S(1)}, f32[136,128]{1,0:T(8,128)S(1)}, u32[]{:S(2)}, u32[]{:S(2)}) collective-permute-start(f32[136,128]{1,0:T(8,128)S(1)} %add.20), channel_id=1, source_target_pairs={{0,4},{4,0},{8,12},{12,8},{16,20},{20,16},{24,28},{28,24},{1,5},{5... | collective-permute-start | bytes 208904 | tf_op jit(solution)/shard_map/ppermute | solution.py:23
  33.6 2.5 %collective-permute-done.5 = f32[136,128]{1,0:T(8,128)S(1)} collective-permute-done((f32[136,128]{1,0:T(8,128)S(1)}, f32[136,128]{1,0:T(8,128)S(1)}, u32[]{:S(2)}, u32[]{:S(2)}) %collective-permute-start.5) | collective-permute-done | bytes 69664 | tf_op jit(solution)/shard_map/ppermute | solution.py:23
  36.2 1.9 %collective-permute-start.6 = (f32[136,128]{1,0:T(8,128)S(1)}, f32[136,128]{1,0:T(8,128)S(1)}, u32[]{:S(2)}, u32[]{:S(2)}) collective-permute-start(f32[136,128]{1,0:T(8,128)S(1)} %add.21), channel_id=1, source_target_pairs={{0,8},{4,12},{8,0},{12,4},{16,24},{20,28},{24,16},{28,20},{1,9},{5... | collective-permute-start | bytes 208904 | tf_op jit(solution)/shard_map/ppermute | solution.py:23
  38.0 2.5 %collective-permute-done.6 = f32[136,128]{1,0:T(8,128)S(1)} collective-permute-done((f32[136,128]{1,0:T(8,128)S(1)}, f32[136,128]{1,0:T(8,128)S(1)}, u32[]{:S(2)}, u32[]{:S(2)}) %collective-permute-start.6) | collective-permute-done | bytes 69664 | tf_op jit(solution)/shard_map/ppermute | solution.py:23
  40.5 3.6 %collective-permute-start.7 = (f32[136,128]{1,0:T(8,128)S(1)}, f32[136,128]{1,0:T(8,128)S(1)}, u32[]{:S(2)}, u32[]{:S(2)}) collective-permute-start(f32[136,128]{1,0:T(8,128)S(1)} %add.22), channel_id=1, source_target_pairs={{0,16},{4,20},{8,24},{12,28},{16,0},{20,4},{24,8},{28,12},{1,17},{... | collective-permute-start | bytes 208904 | tf_op jit(solution)/shard_map/ppermute | solution.py:23
  44.2 3.0 %collective-permute-done.7 = f32[136,128]{1,0:T(8,128)S(1)} collective-permute-done((f32[136,128]{1,0:T(8,128)S(1)}, f32[136,128]{1,0:T(8,128)S(1)}, u32[]{:S(2)}, u32[]{:S(2)}) %collective-permute-start.7) | collective-permute-done | bytes 69664 | tf_op jit(solution)/shard_map/ppermute | solution.py:23
  47.2 0.1 collective-permute-start.8
  47.3 1.2 %collective-permute-done.8.other_ref = f32[136,128]{1,0:T(8,128)S(1)} collective-permute-done((f32[136,128]{1,0:T(8,128)S(1)}, f32[136,128]{1,0:T(8,128)S(1)}, u32[]{:S(2)}, u32[]{:S(2)}) %collective-permute-start.8) | collective-permute-done | bytes 69664 | tf_op jit(solution)/shard_map/ppermute | solution.py:23
  48.5 0.0 copy-done.2
  48.6 7.9 %shard_map.54 = (f32[512,256]{1,0:T(8,128)}, f32[256,256]{1,0:T(8,128)}) custom-call(s32[1]{0:T(128)} %bitcast.side_ref, f32[136,128]{1,0:T(8,128)S(1)} %add.23.mine_ref, f32[136,128]{1,0:T(8,128)S(1)} %collective-permute-done.8.other_ref, f32[256,256]{1,0:T(8,128)S(1)} %copy-done.2, f32[512,256]{1,0:T(8,128)S(1)} %get-tuple-element.11.sketched_ref), custom_call_target="tpu_custom_call" | custom-call | flops 1073741824 | bytes 1835008 | tf_op jit(solution)/shard_map/pallas_call | solution.py:259
  (5 shorter events, 0.1 us)
Async XLA Ops:
  0.6 1.6 %copy-start = (bf16[2048,512]{1,0:T(8,128)(2,1)S(1)}, bf16[2048,512]{1,0:T(8,128)(2,1)}, u32[]{:S(2)}) copy-start(bf16[2048,512]{1,0:T(8,128)(2,1)} %snapshots_ref.5) | copy-start | bytes 6291460
  2.2 0.9 %copy-start.1 = (bf16[512,256]{1,0:T(8,128)(2,1)S(1)}, bf16[512,256]{1,0:T(8,128)(2,1)}, u32[]{:S(2)}) copy-start(bf16[512,256]{1,0:T(8,128)(2,1)} %sketch_ref.5) | copy-start | bytes 786436
  4.8 5.5 %collective-permute-start.1 = (f32[512,256]{1,0:T(8,128)S(1)}, f32[512,256]{1,0:T(8,128)S(1)}, u32[]{:S(2)}, u32[]{:S(2)}) collective-permute-start(f32[512,256]{1,0:T(8,128)S(1)} %shard_map.52), channel_id=1, source_target_pairs={{0,1},{1,0},{2,3},{3,2},{4,5},{5,4},{6,7},{7,6},{8,9},{9,8},{10,11... | collective-permute-start | bytes 1572872 | tf_op jit(solution)/shard_map/ppermute | solution.py:23
  8.5 4.8 %collective-permute-start = (f32[512,256]{1,0:T(8,128)S(1)}, f32[512,256]{1,0:T(8,128)S(1)}, u32[]{:S(2)}, u32[]{:S(2)}) collective-permute-start(f32[512,256]{1,0:T(8,128)S(1)} %get-tuple-element.8), channel_id=1, source_target_pairs={{0,1},{1,0},{2,3},{3,2},{4,5},{5,4},{6,7},{7,6},{8,9},{9,8},{10,11... | collective-permute-start | bytes 1572872 | tf_op jit(solution)/shard_map/ppermute | solution.py:23
  10.3 38.3 %copy-start.2 = (f32[256,256]{1,0:T(8,128)S(1)}, f32[256,256]{1,0:T(8,128)}, u32[]{:S(2)}) copy-start(f32[256,256]{1,0:T(8,128)} %rotation_ref.1) | copy-start | bytes 786436
  10.4 15.1 %collective-permute-start.2 = (f32[512,256]{1,0:T(8,128)S(1)}, f32[512,256]{1,0:T(8,128)S(1)}, u32[]{:S(2)}, u32[]{:S(2)}) collective-permute-start(f32[512,256]{1,0:T(8,128)S(1)} %add.18), channel_id=1, source_target_pairs={{0,2},{1,3},{2,0},{3,1},{4,6},{5,7},{6,4},{7,5},{8,10},{9,11},{10,... | collective-permute-start | bytes 1572872 | tf_op jit(solution)/shard_map/ppermute | solution.py:23
  26.0 1.3 %collective-permute-start.3 = (f32[136,128]{1,0:T(8,128)S(1)}, f32[136,128]{1,0:T(8,128)S(1)}, u32[]{:S(2)}, u32[]{:S(2)}) collective-permute-start(f32[136,128]{1,0:T(8,128)S(1)} %get-tuple-element.10), channel_id=1, source_target_pairs={{0,1},{1,0},{2,3},{3,2},{4,5},{5,4},{6,7},{7,6},{8,9},{9,8},{10,11... | collective-permute-start | bytes 208904 | tf_op jit(solution)/shard_map/ppermute | solution.py:23
  27.4 4.4 %collective-permute-start.4 = (f32[136,128]{1,0:T(8,128)S(1)}, f32[136,128]{1,0:T(8,128)S(1)}, u32[]{:S(2)}, u32[]{:S(2)}) collective-permute-start(f32[136,128]{1,0:T(8,128)S(1)} %add.19), channel_id=1, source_target_pairs={{0,2},{1,3},{2,0},{3,1},{4,6},{5,7},{6,4},{7,5},{8,10},{9,11},{10,... | collective-permute-start | bytes 208904 | tf_op jit(solution)/shard_map/ppermute | solution.py:23
  31.8 4.4 %collective-permute-start.5 = (f32[136,128]{1,0:T(8,128)S(1)}, f32[136,128]{1,0:T(8,128)S(1)}, u32[]{:S(2)}, u32[]{:S(2)}) collective-permute-start(f32[136,128]{1,0:T(8,128)S(1)} %add.20), channel_id=1, source_target_pairs={{0,4},{4,0},{8,12},{12,8},{16,20},{20,16},{24,28},{28,24},{1,5},{5... | collective-permute-start | bytes 208904 | tf_op jit(solution)/shard_map/ppermute | solution.py:23
  36.2 4.4 %collective-permute-start.6 = (f32[136,128]{1,0:T(8,128)S(1)}, f32[136,128]{1,0:T(8,128)S(1)}, u32[]{:S(2)}, u32[]{:S(2)}) collective-permute-start(f32[136,128]{1,0:T(8,128)S(1)} %add.21), channel_id=1, source_target_pairs={{0,8},{4,12},{8,0},{12,4},{16,24},{20,28},{24,16},{28,20},{1,9},{5... | collective-permute-start | bytes 208904 | tf_op jit(solution)/shard_map/ppermute | solution.py:23
  40.5 6.7 %collective-permute-start.7 = (f32[136,128]{1,0:T(8,128)S(1)}, f32[136,128]{1,0:T(8,128)S(1)}, u32[]{:S(2)}, u32[]{:S(2)}) collective-permute-start(f32[136,128]{1,0:T(8,128)S(1)} %add.22), channel_id=1, source_target_pairs={{0,16},{4,20},{8,24},{12,28},{16,0},{20,4},{24,8},{28,12},{1,17},{... | collective-permute-start | bytes 208904 | tf_op jit(solution)/shard_map/ppermute | solution.py:23
  47.2 1.3 %collective-permute-start.8 = (f32[136,128]{1,0:T(8,128)S(1)}, f32[136,128]{1,0:T(8,128)S(1)}, u32[]{:S(2)}, u32[]{:S(2)}) collective-permute-start(f32[136,128]{1,0:T(8,128)S(1)} %add.23.mine_ref), channel_id=1, source_target_pairs={{0,1},{1,0},{2,3},{3,2},{4,5},{5,4},{6,7},{7,6},{8,9},{9,8},{10,11... | collective-permute-start | bytes 208904 | tf_op jit(solution)/shard_map/ppermute | solution.py:23

commit v3 on v2

--- a/solution.py
+++ b/solution.py
@@ -15,8 +15,8 @@
 PANEL = 2
 
 
-def params():
-    return pltpu.CompilerParams(vmem_limit_bytes=40 << 20)
+def params(mib=40):
+    return pltpu.CompilerParams(vmem_limit_bytes=int(mib * 2**20))
 
 
 def partner(shard, axis, level):
@@ -46,11 +46,12 @@
     return product(x1, y1, dims) + (product(x1, y2, dims) + product(x2, y1, dims) + small)
 
 
-PIECES = 4
-
-
-def sketch_kernel(masks, snapshots_ref, sketch_ref, *rest):
-    outs, (tall, wide, arrived, ready) = rest[: len(masks)], rest[len(masks) :]
+PIECES = 1
+
+
+def sketch_kernel(masks, keep, snapshots_ref, sketch_ref, *rest):
+    *outs, tall, wide, arrived, ready = rest
+    held = outs.pop() if keep else None
     rows, step = tall.shape[0] // len(masks), tall.shape[0] // len(masks) // PIECES
     index = lax.axis_index("tm")
     fetch = pltpu.make_async_copy(sketch_ref, wide, ready)
@@ -68,6 +69,8 @@
             )
             copies[-1].start()
     fetch.wait()
+    if keep:
+        held[...] = wide[...]
     for i, out in enumerate(outs):
         for j in range(PIECES):
             copies[PIECES * i + j].wait()
@@ -75,22 +78,23 @@
             out[step * j : step * (j + 1), :] = jnp.dot(block, wide[...], preferred_element_type=F32)
 
 
-def sketch_blocks(masks, snapshots, sketch):
+def sketch_blocks(masks, snapshots, sketch, keep=False):
     rows = snapshots.shape[0] // lax.axis_size("tm")
     depth, columns = sketch.shape
     count = len(masks)
     return pl.pallas_call(
-        functools.partial(sketch_kernel, masks),
-        out_shape=[jax.ShapeDtypeStruct((rows, columns), F32)] * count,
+        functools.partial(sketch_kernel, masks, keep),
+        out_shape=[jax.ShapeDtypeStruct((rows, columns), F32)] * count
+        + [jax.ShapeDtypeStruct((depth, columns), BF16)] * keep,
         in_specs=[pl.BlockSpec(memory_space=pltpu.HBM)] * 2,
-        out_specs=[VMEM] * count,
+        out_specs=[VMEM] * (count + keep),
         scratch_shapes=[
             pltpu.VMEM((count * rows, depth), BF16),
             pltpu.VMEM((depth, columns), BF16),
             pltpu.SemaphoreType.DMA((PIECES * count,)),
             pltpu.SemaphoreType.DMA,
         ],
-        compiler_params=params(),
+        compiler_params=params(53.5 if keep else 52),
         cost_estimate=pl.CostEstimate(
             flops=2 * count * rows * depth * columns,
             bytes_accessed=count * rows * (2 * depth + 4 * columns) + 2 * depth * columns,
@@ -233,40 +237,85 @@
                         a[top : top + 8, 128 * k : 128 * k + 128] = old - new
 
 
-def basis_kernel(scale, side_ref, mine_ref, other_ref, rotation_ref, sketched_ref, basis_ref, triangle_ref, a, upper, inverse):
-    n = a.shape[0]
-    h = n // 2
+def triangles(shape):
+    row = lax.broadcasted_iota(jnp.int32, shape, 0)
+    column = lax.broadcasted_iota(jnp.int32, shape, 1)
+    return row > column, row == column
+
+
+def first_kernel(side_ref, mine_ref, out_ref, a, upper, inverse):
+    h = a.shape[0]
+    lower, middle = triangles((h, h))
+
+    @pl.when(side_ref[0] == 1)
+    def _():
+        mixed = mine_ref[:h, :]
+        a[...] = jnp.where(lower | middle, mixed, mixed.T)
+        factor(a, upper, inverse)
+        out_ref[:h, :] = jnp.where(lower | middle, inverse[...], upper[...])
+        diagonal = jnp.sum(jnp.where(middle, upper[...], 0.0), axis=0, keepdims=True)
+        out_ref[h:, :] = jnp.broadcast_to(diagonal, (8, h))
+
+    @pl.when(side_ref[0] == 0)
+    def _():
+        out_ref[...] = jnp.zeros_like(out_ref)
+
+
+def first_factor(side, mine):
+    h = mine.shape[1]
+    return pl.pallas_call(
+        first_kernel,
+        out_shape=jax.ShapeDtypeStruct(mine.shape, F32),
+        in_specs=[SMEM, VMEM],
+        out_specs=VMEM,
+        scratch_shapes=[pltpu.VMEM((h, h), F32)] * 3,
+        compiler_params=params(),
+        cost_estimate=pl.CostEstimate(flops=10 * h * h * h, bytes_accessed=8 * h * h, transcendentals=h),
+    )(side, mine)
+
+
+def basis_kernel(
+    scale, side_ref, mine_ref, other_ref, own_ref, sent_ref, rotation_ref, sketched_ref, basis_ref, triangle_ref, a, upper, inverse
+):
+    h = a.shape[0]
+    lower, middle = triangles((h, h))
     first = side_ref[0] == 0
     mine, other = mine_ref[...], other_ref[...]
     below = jnp.where(first, mine[:h, :], other[:h, :])
     mixed = jnp.where(first, other[:h, :], mine[:h, :])
-    flipped = mixed.T
-    row = lax.broadcasted_iota(jnp.int32, (h, h), 0)
-    column = lax.broadcasted_iota(jnp.int32, (h, h), 1)
-    diagonal = jnp.broadcast_to(mine[h : h + 1, :], (h, h))
-    a[:h, :h] = jnp.where(row >= column, mixed, flipped)
-    a[h:, :h] = below
-    a[:h, h:] = below.T
-    a[h:, h:] = jnp.where(row < column, mixed, jnp.where(row > column, flipped, diagonal))
+    factors = jnp.where(first, sent_ref[...], own_ref[...])
+    inverse1 = jnp.where(lower | middle, factors[:h, :], 0.0)
+    upper1 = jnp.where(lower, 0.0, jnp.where(middle, factors[h : h + 1, :], factors[:h, :]))
+    corner = jnp.where(lower, mixed.T, jnp.where(middle, mine[h : h + 1, :], mixed))
+    left = dot_parts(below, inverse1, ((1,), (1,)))
+    a[...] = corner - dot_parts(left, left, ((1,), (1,)))
+    ahead = dot_parts(left, inverse1, ((1,), (0,)))
+    x1, x2 = sketched_ref[:, :h], sketched_ref[:, h:]
+    mapping = dot_parts(inverse1, scale * rotation_ref[:h, :], ((0,), (0,)))
+    basis = dot_parts(x1, mapping, ((1,), (0,)))
+    rest = x2 - dot_parts(x1, ahead, ((1,), (1,)))
     factor(a, upper, inverse)
-    triangle_ref[...] = upper[...] * (1.0 / scale)
-    mapping = dot_parts(inverse[...], scale * rotation_ref[...], ((0,), (0,)))
-    basis_ref[...] = dot_parts(sketched_ref[...], mapping, ((1,), (0,)))
-
-
-def basis_and_triangle(side, mine, other, rotation, sketched, scale):
-    (rows, n) = sketched.shape
+    mapping = dot_parts(inverse[...], scale * rotation_ref[h:, :], ((0,), (0,)))
+    basis_ref[...] = basis + dot_parts(rest, mapping, ((1,), (0,)))
+    triangle_ref[:h, :h] = upper1 * (1.0 / scale)
+    triangle_ref[:h, h:] = left.T * (1.0 / scale)
+    triangle_ref[h:, :h] = jnp.zeros((h, h), F32)
+    triangle_ref[h:, h:] = upper[...] * (1.0 / scale)
+
+
+def basis_and_triangle(side, mine, other, own, sent, rotation, sketched, scale):
+    rows, n = sketched.shape
     return pl.pallas_call(
         functools.partial(basis_kernel, scale),
         out_shape=[jax.ShapeDtypeStruct((rows, n), F32), jax.ShapeDtypeStruct((n, n), F32)],
-        in_specs=[SMEM, VMEM, VMEM, VMEM, VMEM],
+        in_specs=[SMEM] + [VMEM] * 6,
         out_specs=[VMEM] * 2,
-        scratch_shapes=[pltpu.VMEM((n, n), F32)] * 3,
+        scratch_shapes=[pltpu.VMEM((n // 2, n // 2), F32)] * 3,
         compiler_params=params(),
         cost_estimate=pl.CostEstimate(
             flops=12 * rows * n * n + 40 * n * n * n, bytes_accessed=8 * rows * n + 12 * n * n, transcendentals=n
         ),
-    )(side, mine, other, rotation, sketched)
+    )(side, mine, other, own, sent, rotation, sketched)
 
 
 def shards(snapshots, sketch, rotation):
@@ -275,26 +324,28 @@
     side = (lax.axis_index("tm").astype(jnp.int32) & 1).reshape(1)
 
     kept, near = {}, {}
-    for mask in range(lax.axis_size("tm") - 2, -1, -2):
-        if mask:
-            (leaving,) = sketch_blocks([mask | 1], snapshots, sketch)
-            (kept[mask],) = sketch_blocks([mask], snapshots, sketch)
-        else:
-            leaving, kept[mask] = sketch_blocks([mask | 1, mask], snapshots, sketch)
+    for mask in range(lax.axis_size("tm") - 2, 0, -2):
+        leaving, sketch = sketch_blocks([mask | 1], snapshots, sketch, keep=True)
         near[mask] = partner(leaving, "tm", 0)
+        (kept[mask],) = sketch_blocks([mask], snapshots, sketch)
     for level in range(1, depth):
         for mask in [m for m in kept if m >> level & 1]:
-            arrived = partner(kept.pop(mask) + near.pop(mask), "tm", level)
-            stays = mask ^ 1 << level
-            near[stays] = near[stays] + arrived if level < depth - 1 else near[stays]
+            leaving = kept.pop(mask) + near.pop(mask)
+            arrived = partner(leaving, "tm", level)
+            snapshots, leaving = lax.optimization_barrier((snapshots, leaving))
+            if level < depth - 1:
+                near[mask ^ 1 << level] = near[mask ^ 1 << level] + arrived
+    leaving, kept[0] = sketch_blocks([1, 0], snapshots, sketch)
+    near[0] = partner(leaving, "tm", 0)
     sketched, mine, send = gram_halves(side, kept[0], near[0], arrived)
     mine = mine + partner(send, "tm", 0)
     for level in range(1, depth):
         mine = mine + partner(mine, "tm", level)
     for level in range(levels("space")):
         mine = mine + partner(mine, "space", level)
-    other = partner(mine, "tm", 0)
-    return tuple(basis_and_triangle(side, mine, other, rotation, sketched, math.sqrt(cells)))
+    mine, own = lax.optimization_barrier((mine, first_factor(side, mine)))
+    other, sent = partner(mine, "tm", 0), partner(own, "tm", 0)
+    return tuple(basis_and_triangle(side, mine, other, own, sent, rotation, sketched, math.sqrt(cells)))
 
 
 def solution(mesh):

time: 56.6 us -> 49.4 us (0.87)
  Pallas kernels: 14.8 us -> 11.7 us
  local copies, waits for them, and re-layouts: 2.54 us -> 0.01 us
  waiting for transfers between devices: 25.2 us -> 23.4 us
    unnamed x6 -> x2, local copies, waits for them, and re-layouts: 2.54 us -> 0.01 us
    pallas_call x1, Pallas kernels: 7.86 us -> 5.53 us  [basis_and_triangle(): pl.pallas_call(functools.partial(basis_kernel, scale), out_shape=[jax.Sha...]
    ppermute x9 -> x10, waiting for transfers between devices: 25.2 us -> 23.4 us  [partner(): lax.ppermute(shard, axis, [(i, i ^ 1 << level) for i in range(lax.axis_si...]
    pallas_call x3 -> x4, Pallas kernels: 6.42 us -> 5.56 us  [the longest x3 5.53 us: sketch_blocks(): pl.pallas_call(functools.partial(sketch_kernel, masks, keep), out_shape=[...]
    ppermute x9 -> x10, starting transfers between devices: 12.9 us -> 13.3 us  [partner(): lax.ppermute(shard, axis, [(i, i ^ 1 << level) for i in range(lax.axis_si...]
  transfers between devices with their start and end apart: 9 -> 10, of which waited for: 7 -> 9; matrix products, arithmetic and copies ran while one was open for 0% -> 0% of each run, Pallas kernels for 9% -> 7%
where the time goes in v3:
time: 49.4 us; the launch traced here: 49.2 us
  waiting for transfers between devices  23.4 us (47%)
  starting transfers between devices  13.3 us (27%)
  Pallas kernels  11.7 us (24%)
  between operations  0.73 us (1%)
    ppermute x10, waiting for transfers between devices, partner(): lax.ppermute(shard, axis, [(i, i ^ 1 << level) for i in range(lax.axis_si...  23.4 us
    ppermute x10, starting transfers between devices, partner(): lax.ppermute(shard, axis, [(i, i ^ 1 << level) for i in range(lax.axis_si...  13.3 us
    pallas_call x1, Pallas kernels, basis_and_triangle(): pl.pallas_call(functools.partial(basis_kernel, scale), out_shape=[jax.Sha...  5.53 us
    pallas_call x3, Pallas kernels, sketch_blocks(): pl.pallas_call(functools.partial(sketch_kernel, masks, keep), out_shape=[...  5.53 us
  transfers between devices with their start and end apart: 10, of which 9 were waited for; matrix products, arithmetic and copies ran while one was open for 0% of the time, Pallas kernels for 7%

profile of v3, /device:TPU:0, one launch (start us, length us, event | category | flops | bytes accessed | tf_op | source)
XLA Modules:
  0.0 49.2 jit_solution(4162156272957320116)
XLA Ops:
  0.6 2.2 %shard_map.50 = (f32[512,256]{1,0:T(8,128)}, bf16[512,256]{1,0:T(8,128)(2,1)S(1)}) custom-call(bf16[2048,512]{1,0:T(8,128)(2,1)} %snapshots_ref.4, bf16[512,256]{1,0:T(8,128)(2,1)} %sketch_ref.1), custom_call_target="tpu_custom_call" | custom-call | flops 134217728 | bytes 1310720 | tf_op jit(solution)/shard_map/pallas_call | solution.py:85
  2.9 0.5 %collective-permute-start = (f32[512,256]{1,0:T(8,128)}, f32[512,256]{1,0:T(8,128)S(1)}, u32[]{:S(2)}, u32[]{:S(2)}) collective-permute-start(f32[512,256]{1,0:T(8,128)} %get-tuple-element.13), channel_id=1, source_target_pairs={{0,1},{1,0},{2,3},{3,2},{4,5},{5,4},{6,7},{7,6},{8,9},{9,8},{10,11... | collective-permute-start | bytes 1572872 | tf_op jit(solution)/shard_map/ppermute | solution.py:23
  3.4 1.4 %shard_map.51 = f32[512,256]{1,0:T(8,128)S(1)} custom-call(bf16[2048,512]{1,0:T(8,128)(2,1)} %snapshots_ref.4, bf16[512,256]{1,0:T(8,128)(2,1)S(1)} %get-tuple-element.12.sketch_ref), custom_call_target="tpu_custom_call" | custom-call | flops 134217728 | bytes 1310720 | tf_op jit(solution)/shard_map/pallas_call | solution.py:85
  4.8 0.4 collective-permute-done
  5.1 0.1 add.18
  5.2 0.0 copy-start
  5.2 2.9 %collective-permute-start.2 = (f32[512,256]{1,0:T(8,128)S(1)}, f32[512,256]{1,0:T(8,128)S(1)}, u32[]{:S(2)}, u32[]{:S(2)}) collective-permute-start(f32[512,256]{1,0:T(8,128)S(1)} %add.18), channel_id=1, source_target_pairs={{0,2},{1,3},{2,0},{3,1},{4,6},{5,7},{6,4},{7,5},{8,10},{9,11},{10,... | collective-permute-start | bytes 1572872 | tf_op jit(solution)/shard_map/ppermute | solution.py:23
  8.1 1.9 %shard_map.52 = (f32[512,256]{1,0:T(8,128)S(1)}, f32[512,256]{1,0:T(8,128)S(1)}) custom-call(bf16[2048,512]{1,0:T(8,128)(2,1)} %snapshots_ref.4, bf16[512,256]{1,0:T(8,128)(2,1)S(1)} %get-tuple-element.12.sketch_ref), custom_call_target="tpu_custom_call" | custom-call | flops 268435456 | bytes 2359296 | tf_op jit(solution)/shard_map/pallas_call | solution.py:85
  10.1 0.1 collective-permute-start.1
  10.2 10.2 %collective-permute-done.2.far_ref = f32[512,256]{1,0:T(8,128)S(1)} collective-permute-done((f32[512,256]{1,0:T(8,128)S(1)}, f32[512,256]{1,0:T(8,128)S(1)}, u32[]{:S(2)}, u32[]{:S(2)}) %collective-permute-start.2) | collective-permute-done | bytes 524320 | tf_op jit(solution)/shard_map/ppermute | solution.py:23
  20.4 0.0 collective-permute-done.1.near_ref
  20.4 0.6 %shard_map.53 = (f32[512,256]{1,0:T(8,128)S(1)}, f32[136,128]{1,0:T(8,128)S(1)}, f32[136,128]{1,0:T(8,128)S(1)}) custom-call(s32[1]{0:T(128)} %bitcast.side_ref, f32[512,256]{1,0:T(8,128)S(1)} %get-tuple-element.15.kept_ref, f32[512,256]{1,0:T(8,128)S(1)} %collective-permute-done.1.near_ref, f32[512,256]{1,0:T(8,128)S(1)} %collective-permute-done.2.far_ref), custom_call_target="tpu_custom_call" | custom-call | flops 268435456 | bytes 2359296 | tf_op jit(solution)/shard_map/pallas_call | solution.py:129
  20.9 0.1 collective-permute-start.3
  21.0 1.2 %collective-permute-done.3 = f32[136,128]{1,0:T(8,128)S(1)} collective-permute-done((f32[136,128]{1,0:T(8,128)S(1)}, f32[136,128]{1,0:T(8,128)S(1)}, u32[]{:S(2)}, u32[]{:S(2)}) %collective-permute-start.3) | collective-permute-done | bytes 69664 | tf_op jit(solution)/shard_map/ppermute | solution.py:23
  22.3 1.8 %collective-permute-start.4 = (f32[136,128]{1,0:T(8,128)S(1)}, f32[136,128]{1,0:T(8,128)S(1)}, u32[]{:S(2)}, u32[]{:S(2)}) collective-permute-start(f32[136,128]{1,0:T(8,128)S(1)} %add.19), channel_id=1, source_target_pairs={{0,2},{1,3},{2,0},{3,1},{4,6},{5,7},{6,4},{7,5},{8,10},{9,11},{10,... | collective-permute-start | bytes 208904 | tf_op jit(solution)/shard_map/ppermute | solution.py:23
  24.1 2.6 %collective-permute-done.4 = f32[136,128]{1,0:T(8,128)S(1)} collective-permute-done((f32[136,128]{1,0:T(8,128)S(1)}, f32[136,128]{1,0:T(8,128)S(1)}, u32[]{:S(2)}, u32[]{:S(2)}) %collective-permute-start.4) | collective-permute-done | bytes 69664 | tf_op jit(solution)/shard_map/ppermute | solution.py:23
  26.7 1.8 %collective-permute-start.5 = (f32[136,128]{1,0:T(8,128)S(1)}, f32[136,128]{1,0:T(8,128)S(1)}, u32[]{:S(2)}, u32[]{:S(2)}) collective-permute-start(f32[136,128]{1,0:T(8,128)S(1)} %add.20), channel_id=1, source_target_pairs={{0,4},{4,0},{8,12},{12,8},{16,20},{20,16},{24,28},{28,24},{1,5},{5... | collective-permute-start | bytes 208904 | tf_op jit(solution)/shard_map/ppermute | solution.py:23
  28.5 2.5 %collective-permute-done.5 = f32[136,128]{1,0:T(8,128)S(1)} collective-permute-done((f32[136,128]{1,0:T(8,128)S(1)}, f32[136,128]{1,0:T(8,128)S(1)}, u32[]{:S(2)}, u32[]{:S(2)}) %collective-permute-start.5) | collective-permute-done | bytes 69664 | tf_op jit(solution)/shard_map/ppermute | solution.py:23
  31.1 1.9 %collective-permute-start.6 = (f32[136,128]{1,0:T(8,128)S(1)}, f32[136,128]{1,0:T(8,128)S(1)}, u32[]{:S(2)}, u32[]{:S(2)}) collective-permute-start(f32[136,128]{1,0:T(8,128)S(1)} %add.21), channel_id=1, source_target_pairs={{0,8},{4,12},{8,0},{12,4},{16,24},{20,28},{24,16},{28,20},{1,9},{5... | collective-permute-start | bytes 208904 | tf_op jit(solution)/shard_map/ppermute | solution.py:23
  32.9 2.5 %collective-permute-done.6 = f32[136,128]{1,0:T(8,128)S(1)} collective-permute-done((f32[136,128]{1,0:T(8,128)S(1)}, f32[136,128]{1,0:T(8,128)S(1)}, u32[]{:S(2)}, u32[]{:S(2)}) %collective-permute-start.6) | collective-permute-done | bytes 69664 | tf_op jit(solution)/shard_map/ppermute | solution.py:23
  35.4 3.6 %collective-permute-start.7 = (f32[136,128]{1,0:T(8,128)S(1)}, f32[136,128]{1,0:T(8,128)S(1)}, u32[]{:S(2)}, u32[]{:S(2)}) collective-permute-start(f32[136,128]{1,0:T(8,128)S(1)} %add.22), channel_id=1, source_target_pairs={{0,16},{4,20},{8,24},{12,28},{16,0},{20,4},{24,8},{28,12},{1,17},{... | collective-permute-start | bytes 208904 | tf_op jit(solution)/shard_map/ppermute | solution.py:23
  39.1 3.0 %collective-permute-done.7 = f32[136,128]{1,0:T(8,128)S(1)} collective-permute-done((f32[136,128]{1,0:T(8,128)S(1)}, f32[136,128]{1,0:T(8,128)S(1)}, u32[]{:S(2)}, u32[]{:S(2)}) %collective-permute-start.7) | collective-permute-done | bytes 69664 | tf_op jit(solution)/shard_map/ppermute | solution.py:23
  42.2 0.1 collective-permute-start.8
  42.2 0.5 %collective-permute-start.9 = (f32[136,128]{1,0:T(8,128)S(1)}, f32[136,128]{1,0:T(8,128)S(1)}, u32[]{:S(2)}, u32[]{:S(2)}) collective-permute-start(f32[136,128]{1,0:T(8,128)S(1)} %shard_map.54.own_ref), channel_id=1, source_target_pairs={{0,1},{1,0},{2,3},{3,2},{4,5},{5,4},{6,7},{7,6},{8,9},{9,8},{10,11... | collective-permute-start | bytes 208904 | tf_op jit(solution)/shard_map/ppermute | solution.py:23
  42.7 0.7 %collective-permute-done.8.other_ref = f32[136,128]{1,0:T(8,128)S(1)} collective-permute-done((f32[136,128]{1,0:T(8,128)S(1)}, f32[136,128]{1,0:T(8,128)S(1)}, u32[]{:S(2)}, u32[]{:S(2)}) %collective-permute-start.8) | collective-permute-done | bytes 69664 | tf_op jit(solution)/shard_map/ppermute | solution.py:23
  43.5 0.2 collective-permute-done.9.sent_ref
  43.6 0.0 copy-done
  43.6 5.5 %shard_map.55 = (f32[512,256]{1,0:T(8,128)}, f32[256,256]{1,0:T(8,128)}) custom-call(s32[1]{0:T(128)} %bitcast.side_ref, f32[136,128]{1,0:T(8,128)S(1)} %add.23.mine_ref, f32[136,128]{1,0:T(8,128)S(1)} %collective-permute-done.8.other_ref, f32[136,128]{1,0:T(8,128)S(1)} %shard_map.54.own_ref, f32[136,128]{1,0:T(8,128)S(1)} %collective-permute-done.9.sent_ref, ...), custom_call_target="tpu_custom_call" | custom-call | flops 1073741824 | bytes 1835008 | tf_op jit(solution)/shard_map/pallas_call | solution.py:308
  (6 shorter events, 0.1 us)
Async XLA Ops:
  2.9 2.3 %collective-permute-start = (f32[512,256]{1,0:T(8,128)}, f32[512,256]{1,0:T(8,128)S(1)}, u32[]{:S(2)}, u32[]{:S(2)}) collective-permute-start(f32[512,256]{1,0:T(8,128)} %get-tuple-element.13), channel_id=1, source_target_pairs={{0,1},{1,0},{2,3},{3,2},{4,5},{5,4},{6,7},{7,6},{8,9},{9,8},{10,11... | collective-permute-start | bytes 1572872 | tf_op jit(solution)/shard_map/ppermute | solution.py:23
  5.2 38.4 %copy-start = (f32[256,256]{1,0:T(8,128)S(1)}, f32[256,256]{1,0:T(8,128)}, u32[]{:S(2)}) copy-start(f32[256,256]{1,0:T(8,128)} %rotation_ref.1) | copy-start | bytes 786436
  5.2 15.2 %collective-permute-start.2 = (f32[512,256]{1,0:T(8,128)S(1)}, f32[512,256]{1,0:T(8,128)S(1)}, u32[]{:S(2)}, u32[]{:S(2)}) collective-permute-start(f32[512,256]{1,0:T(8,128)S(1)} %add.18), channel_id=1, source_target_pairs={{0,2},{1,3},{2,0},{3,1},{4,6},{5,7},{6,4},{7,5},{8,10},{9,11},{10,... | collective-permute-start | bytes 1572872 | tf_op jit(solution)/shard_map/ppermute | solution.py:23
  10.1 10.3 %collective-permute-start.1 = (f32[512,256]{1,0:T(8,128)S(1)}, f32[512,256]{1,0:T(8,128)S(1)}, u32[]{:S(2)}, u32[]{:S(2)}) collective-permute-start(f32[512,256]{1,0:T(8,128)S(1)} %get-tuple-element.16), channel_id=1, source_target_pairs={{0,1},{1,0},{2,3},{3,2},{4,5},{5,4},{6,7},{7,6},{8,9},{9,8},{10,11... | collective-permute-start | bytes 1572872 | tf_op jit(solution)/shard_map/ppermute | solution.py:23
  20.9 1.3 %collective-permute-start.3 = (f32[136,128]{1,0:T(8,128)S(1)}, f32[136,128]{1,0:T(8,128)S(1)}, u32[]{:S(2)}, u32[]{:S(2)}) collective-permute-start(f32[136,128]{1,0:T(8,128)S(1)} %get-tuple-element.18), channel_id=1, source_target_pairs={{0,1},{1,0},{2,3},{3,2},{4,5},{5,4},{6,7},{7,6},{8,9},{9,8},{10,11... | collective-permute-start | bytes 208904 | tf_op jit(solution)/shard_map/ppermute | solution.py:23
  22.3 4.4 %collective-permute-start.4 = (f32[136,128]{1,0:T(8,128)S(1)}, f32[136,128]{1,0:T(8,128)S(1)}, u32[]{:S(2)}, u32[]{:S(2)}) collective-permute-start(f32[136,128]{1,0:T(8,128)S(1)} %add.19), channel_id=1, source_target_pairs={{0,2},{1,3},{2,0},{3,1},{4,6},{5,7},{6,4},{7,5},{8,10},{9,11},{10,... | collective-permute-start | bytes 208904 | tf_op jit(solution)/shard_map/ppermute | solution.py:23
  26.7 4.4 %collective-permute-start.5 = (f32[136,128]{1,0:T(8,128)S(1)}, f32[136,128]{1,0:T(8,128)S(1)}, u32[]{:S(2)}, u32[]{:S(2)}) collective-permute-start(f32[136,128]{1,0:T(8,128)S(1)} %add.20), channel_id=1, source_target_pairs={{0,4},{4,0},{8,12},{12,8},{16,20},{20,16},{24,28},{28,24},{1,5},{5... | collective-permute-start | bytes 208904 | tf_op jit(solution)/shard_map/ppermute | solution.py:23
  31.1 4.4 %collective-permute-start.6 = (f32[136,128]{1,0:T(8,128)S(1)}, f32[136,128]{1,0:T(8,128)S(1)}, u32[]{:S(2)}, u32[]{:S(2)}) collective-permute-start(f32[136,128]{1,0:T(8,128)S(1)} %add.21), channel_id=1, source_target_pairs={{0,8},{4,12},{8,0},{12,4},{16,24},{20,28},{24,16},{28,20},{1,9},{5... | collective-permute-start | bytes 208904 | tf_op jit(solution)/shard_map/ppermute | solution.py:23
  35.4 6.7 %collective-permute-start.7 = (f32[136,128]{1,0:T(8,128)S(1)}, f32[136,128]{1,0:T(8,128)S(1)}, u32[]{:S(2)}, u32[]{:S(2)}) collective-permute-start(f32[136,128]{1,0:T(8,128)S(1)} %add.22), channel_id=1, source_target_pairs={{0,16},{4,20},{8,24},{12,28},{16,0},{20,4},{24,8},{28,12},{1,17},{... | collective-permute-start | bytes 208904 | tf_op jit(solution)/shard_map/ppermute | solution.py:23
  42.2 1.3 %collective-permute-start.8 = (f32[136,128]{1,0:T(8,128)S(1)}, f32[136,128]{1,0:T(8,128)S(1)}, u32[]{:S(2)}, u32[]{:S(2)}) collective-permute-start(f32[136,128]{1,0:T(8,128)S(1)} %add.23.mine_ref), channel_id=1, source_target_pairs={{0,1},{1,0},{2,3},{3,2},{4,5},{5,4},{6,7},{7,6},{8,9},{9,8},{10,11... | collective-permute-start | bytes 208904 | tf_op jit(solution)/shard_map/ppermute | solution.py:23
  42.2 1.4 %collective-permute-start.9 = (f32[136,128]{1,0:T(8,128)S(1)}, f32[136,128]{1,0:T(8,128)S(1)}, u32[]{:S(2)}, u32[]{:S(2)}) collective-permute-start(f32[136,128]{1,0:T(8,128)S(1)} %shard_map.54.own_ref), channel_id=1, source_target_pairs={{0,1},{1,0},{2,3},{3,2},{4,5},{5,4},{6,7},{7,6},{8,9},{9,8},{10,11... | collective-permute-start | bytes 208904 | tf_op jit(solution)/shard_map/ppermute | solution.py:23

commit v4 on v3

--- a/solution.py
+++ b/solution.py
@@ -12,6 +12,7 @@
 VMEM = pl.BlockSpec(memory_space=pltpu.VMEM)
 SMEM = pl.BlockSpec(memory_space=pltpu.SMEM)
 BLOCK = 64
+CHUNKS = 2
 PANEL = 2
 
 
@@ -39,68 +40,57 @@
     return lax.dot_general(x, y, (dims, ((), ())), preferred_element_type=F32)
 
 
-def dot_parts(x, y, dims):
-    x1, x2, x3 = split(x)
-    y1, y2, y3 = split(y)
-    small = product(x1, y3, dims) + product(x2, y2, dims) + product(x3, y1, dims)
-    return product(x1, y1, dims) + (product(x1, y2, dims) + product(x2, y1, dims) + small)
-
-
-PIECES = 1
-
-
-def sketch_kernel(masks, keep, snapshots_ref, sketch_ref, *rest):
-    *outs, tall, wide, arrived, ready = rest
-    held = outs.pop() if keep else None
-    rows, step = tall.shape[0] // len(masks), tall.shape[0] // len(masks) // PIECES
+LEFT, RIGHT = (0, 0, 1, 0, 1, 2), (0, 1, 0, 2, 1, 0)
+
+
+def stacked(x, order, axis):
+    parts = split(x)
+    return jnp.concatenate([parts[i] for i in order], axis=axis)
+
+
+def dot_parts(x, y, over):
+    return product(stacked(x, LEFT, over[0]), stacked(y, RIGHT, over[1]), ((over[0],), (over[1],)))
+
+
+def sketch_kernel(masks, snapshots_ref, sketch_ref, *rest):
+    outs, (tall, wide, arrived, ready) = rest[: len(masks)], rest[len(masks) :]
+    rows = tall.shape[0] // len(masks)
     index = lax.axis_index("tm")
     fetch = pltpu.make_async_copy(sketch_ref, wide, ready)
     fetch.start()
     copies = []
     for i, mask in enumerate(masks):
-        start = pl.multiple_of((index ^ mask) * rows, rows)
-        for j in range(PIECES):
-            copies.append(
-                pltpu.make_async_copy(
-                    snapshots_ref.at[pl.ds(start + step * j, step)],
-                    tall.at[pl.ds(rows * i + step * j, step)],
-                    arrived.at[PIECES * i + j],
-                )
-            )
-            copies[-1].start()
+        block = pl.ds(pl.multiple_of((index ^ mask) * rows, rows), rows)
+        copies.append(pltpu.make_async_copy(snapshots_ref.at[block], tall.at[pl.ds(rows * i, rows)], arrived.at[i]))
+        copies[-1].start()
     fetch.wait()
-    if keep:
-        held[...] = wide[...]
     for i, out in enumerate(outs):
-        for j in range(PIECES):
-            copies[PIECES * i + j].wait()
-            block = tall[rows * i + step * j : rows * i + step * (j + 1), :]
-            out[step * j : step * (j + 1), :] = jnp.dot(block, wide[...], preferred_element_type=F32)
-
-
-def sketch_blocks(masks, snapshots, sketch, keep=False):
+        copies[i].wait()
+        out[...] = jnp.dot(tall[rows * i : rows * (i + 1), :], wide[...], preferred_element_type=F32)
+
+
+def sketch_blocks(masks, snapshots, sketch):
     rows = snapshots.shape[0] // lax.axis_size("tm")
     depth, columns = sketch.shape
     count = len(masks)
     return pl.pallas_call(
-        functools.partial(sketch_kernel, masks, keep),
-        out_shape=[jax.ShapeDtypeStruct((rows, columns), F32)] * count
-        + [jax.ShapeDtypeStruct((depth, columns), BF16)] * keep,
+        functools.partial(sketch_kernel, masks),
+        out_shape=[jax.ShapeDtypeStruct((rows, columns), F32)] * count,
         in_specs=[pl.BlockSpec(memory_space=pltpu.HBM)] * 2,
-        out_specs=[VMEM] * (count + keep),
+        out_specs=[VMEM] * count,
         scratch_shapes=[
             pltpu.VMEM((count * rows, depth), BF16),
             pltpu.VMEM((depth, columns), BF16),
-            pltpu.SemaphoreType.DMA((PIECES * count,)),
+            pltpu.SemaphoreType.DMA((count,)),
             pltpu.SemaphoreType.DMA,
         ],
-        compiler_params=params(53.5 if keep else 52),
+        compiler_params=params(),
         cost_estimate=pl.CostEstimate(
             flops=2 * count * rows * depth * columns,
             bytes_accessed=count * rows * (2 * depth + 4 * columns) + 2 * depth * columns,
             transcendentals=0,
         ),
-    )(snapshots, sketch)
+    )(pltpu.with_memory_space_constraint(snapshots, pltpu.HBM), pltpu.with_memory_space_constraint(sketch, pltpu.HBM))
 
 
 def gram_kernel(side_ref, kept_ref, near_ref, far_ref, sketched_ref, keep_ref, send_ref):
@@ -144,11 +134,6 @@
 
 def row(v, k):
     return jnp.broadcast_to(v[k : k + 1, :], (8, 128))
-
-
-def stacked(x, order):
-    parts = split(x)
-    return jnp.concatenate([parts[i] for i in order], axis=0)
 
 
 def factor(a, upper, inverse):
@@ -225,9 +210,10 @@
                 right[x].append(z)
         after = start + BLOCK
         if after < n:
-            y = stacked(jnp.concatenate([jnp.concatenate(v, axis=0) for v in right], axis=1), (0, 1, 0, 2, 1, 0))
+            y = jnp.concatenate([jnp.concatenate(v, axis=0) for v in right], axis=1)
+            y = stacked(y, RIGHT, 0)
             for x in range(after // 128, tiles):
-                update = product(stacked(jnp.concatenate(left[x], axis=0), (0, 0, 1, 0, 1, 2)), y, ((0,), (0,)))
+                update = product(stacked(jnp.concatenate(left[x], axis=0), LEFT, 0), y, ((0,), (0,)))
                 for top in range(max(after, 128 * x), 128 * x + 128, 8):
                     for k in range(tiles):
                         old = a[top : top + 8, 128 * k : 128 * k + 128]
@@ -250,22 +236,25 @@
     @pl.when(side_ref[0] == 1)
     def _():
         mixed = mine_ref[:h, :]
-        a[...] = jnp.where(lower | middle, mixed, mixed.T)
+        flipped = mixed.T
+        a[...] = jnp.where(lower | middle, mixed, flipped)
+        out_ref[:h, :] = jnp.where(lower, flipped, jnp.where(middle, mine_ref[h : h + 1, :], mixed))
         factor(a, upper, inverse)
-        out_ref[:h, :] = jnp.where(lower | middle, inverse[...], upper[...])
+        out_ref[h : 2 * h, :] = jnp.where(lower | middle, inverse[...], upper[...])
         diagonal = jnp.sum(jnp.where(middle, upper[...], 0.0), axis=0, keepdims=True)
-        out_ref[h:, :] = jnp.broadcast_to(diagonal, (8, h))
+        out_ref[2 * h :, :] = jnp.broadcast_to(diagonal, (8, h))
 
     @pl.when(side_ref[0] == 0)
     def _():
-        out_ref[...] = jnp.zeros_like(out_ref)
+        out_ref[:h, :] = mine_ref[:h, :]
+        out_ref[h:, :] = jnp.zeros((h + 8, h), F32)
 
 
 def first_factor(side, mine):
     h = mine.shape[1]
     return pl.pallas_call(
         first_kernel,
-        out_shape=jax.ShapeDtypeStruct(mine.shape, F32),
+        out_shape=jax.ShapeDtypeStruct((2 * h + 8, h), F32),
         in_specs=[SMEM, VMEM],
         out_specs=VMEM,
         scratch_shapes=[pltpu.VMEM((h, h), F32)] * 3,
@@ -275,47 +264,64 @@
 
 
 def basis_kernel(
-    scale, side_ref, mine_ref, other_ref, own_ref, sent_ref, rotation_ref, sketched_ref, basis_ref, triangle_ref, a, upper, inverse
+    scale, side_ref, own_ref, sent_ref, rotation_ref, sketched_ref, basis_ref, triangle_ref, a, upper, inverse, rest, basis, triangle, sent
 ):
     h = a.shape[0]
+    rows = basis.shape[0]
     lower, middle = triangles((h, h))
     first = side_ref[0] == 0
-    mine, other = mine_ref[...], other_ref[...]
-    below = jnp.where(first, mine[:h, :], other[:h, :])
-    mixed = jnp.where(first, other[:h, :], mine[:h, :])
-    factors = jnp.where(first, sent_ref[...], own_ref[...])
+    below = jnp.where(first, own_ref[:h, :], sent_ref[:h, :])
+    corner = jnp.where(first, sent_ref[:h, :], own_ref[:h, :])
+    factors = jnp.where(first, sent_ref[h:, :], own_ref[h:, :])
     inverse1 = jnp.where(lower | middle, factors[:h, :], 0.0)
     upper1 = jnp.where(lower, 0.0, jnp.where(middle, factors[h : h + 1, :], factors[:h, :]))
-    corner = jnp.where(lower, mixed.T, jnp.where(middle, mine[h : h + 1, :], mixed))
-    left = dot_parts(below, inverse1, ((1,), (1,)))
-    a[...] = corner - dot_parts(left, left, ((1,), (1,)))
-    ahead = dot_parts(left, inverse1, ((1,), (0,)))
+    left = dot_parts(below, inverse1, (1, 1))
+    a[...] = corner - dot_parts(left, left, (1, 1))
+    ahead = dot_parts(left, inverse1, (1, 0))
+    triangle[:h, :h] = upper1 * (1.0 / scale)
+    triangle[:h, h:] = left.T * (1.0 / scale)
+    triangle[h:, :h] = jnp.zeros((h, h), F32)
+    copies = [pltpu.make_async_copy(triangle.at[pl.ds(h * i, h)], triangle_ref.at[pl.ds(h * i, h)], sent.at[i]) for i in range(2)]
+    copies[0].start()
     x1, x2 = sketched_ref[:, :h], sketched_ref[:, h:]
-    mapping = dot_parts(inverse1, scale * rotation_ref[:h, :], ((0,), (0,)))
-    basis = dot_parts(x1, mapping, ((1,), (0,)))
-    rest = x2 - dot_parts(x1, ahead, ((1,), (1,)))
+    mapping = dot_parts(inverse1, scale * rotation_ref[:h, :], (0, 0))
+    basis[...] = dot_parts(x1, mapping, (1, 0))
+    rest[...] = stacked(x2 - dot_parts(x1, ahead, (1, 1)), LEFT, 1)
+    turned = stacked(scale * rotation_ref[h:, :], RIGHT, 0)
     factor(a, upper, inverse)
-    mapping = dot_parts(inverse[...], scale * rotation_ref[h:, :], ((0,), (0,)))
-    basis_ref[...] = basis + dot_parts(rest, mapping, ((1,), (0,)))
-    triangle_ref[:h, :h] = upper1 * (1.0 / scale)
-    triangle_ref[:h, h:] = left.T * (1.0 / scale)
-    triangle_ref[h:, :h] = jnp.zeros((h, h), F32)
-    triangle_ref[h:, h:] = upper[...] * (1.0 / scale)
-
-
-def basis_and_triangle(side, mine, other, own, sent, rotation, sketched, scale):
+    triangle[h:, h:] = upper[...] * (1.0 / scale)
+    copies[1].start()
+    mapping = stacked(product(stacked(inverse[...], LEFT, 0), turned, ((0,), (0,))), RIGHT, 0)
+    step = rows // CHUNKS
+    for i in range(CHUNKS):
+        part = pl.ds(step * i, step)
+        basis[part, :] += product(rest[part, :], mapping, ((1,), (0,)))
+        copies.append(pltpu.make_async_copy(basis.at[part], basis_ref.at[part], sent.at[2 + i]))
+        copies[-1].start()
+    for copy in copies:
+        copy.wait()
+
+
+def basis_and_triangle(side, own, sent, rotation, sketched, scale):
     rows, n = sketched.shape
+    h = n // 2
     return pl.pallas_call(
         functools.partial(basis_kernel, scale),
         out_shape=[jax.ShapeDtypeStruct((rows, n), F32), jax.ShapeDtypeStruct((n, n), F32)],
-        in_specs=[SMEM] + [VMEM] * 6,
-        out_specs=[VMEM] * 2,
-        scratch_shapes=[pltpu.VMEM((n // 2, n // 2), F32)] * 3,
+        in_specs=[SMEM] + [VMEM] * 4,
+        out_specs=[pl.BlockSpec(memory_space=pltpu.HBM)] * 2,
+        scratch_shapes=[pltpu.VMEM((h, h), F32)] * 3
+        + [
+            pltpu.VMEM((rows, len(LEFT) * h), BF16),
+            pltpu.VMEM((rows, n), F32),
+            pltpu.VMEM((n, n), F32),
+            pltpu.SemaphoreType.DMA((2 + CHUNKS,)),
+        ],
         compiler_params=params(),
         cost_estimate=pl.CostEstimate(
             flops=12 * rows * n * n + 40 * n * n * n, bytes_accessed=8 * rows * n + 12 * n * n, transcendentals=n
         ),
-    )(side, mine, other, own, sent, rotation, sketched)
+    )(side, own, sent, rotation, sketched)
 
 
 def shards(snapshots, sketch, rotation):
@@ -325,7 +331,7 @@
 
     kept, near = {}, {}
     for mask in range(lax.axis_size("tm") - 2, 0, -2):
-        leaving, sketch = sketch_blocks([mask | 1], snapshots, sketch, keep=True)
+        (leaving,) = sketch_blocks([mask | 1], snapshots, sketch)
         near[mask] = partner(leaving, "tm", 0)
         (kept[mask],) = sketch_blocks([mask], snapshots, sketch)
     for level in range(1, depth):
@@ -343,9 +349,8 @@
         mine = mine + partner(mine, "tm", level)
     for level in range(levels("space")):
         mine = mine + partner(mine, "space", level)
-    mine, own = lax.optimization_barrier((mine, first_factor(side, mine)))
-    other, sent = partner(mine, "tm", 0), partner(own, "tm", 0)
-    return tuple(basis_and_triangle(side, mine, other, own, sent, rotation, sketched, math.sqrt(cells)))
+    own = first_factor(side, mine)
+    return tuple(basis_and_triangle(side, own, partner(own, "tm", 0), rotation, sketched, math.sqrt(cells)))
 
 
 def solution(mesh):

time: 49.4 us -> 47.4 us (0.960)
  Pallas kernels: 11.7 us -> 10.1 us
  starting transfers between devices: 13.3 us -> 12.8 us
    pallas_call x1, Pallas kernels: 5.53 us -> 4.66 us  [basis_and_triangle(): pl.pallas_call(functools.partial(basis_kernel, scale), out_shape=[jax.Sha...]
    pallas_call x4, Pallas kernels: 5.56 us -> 4.9 us  [the longest x3 4.87 us: sketch_blocks(): pl.pallas_call(functools.partial(sketch_kernel, masks), out_shape=[jax.Sh...]
    ppermute x10 -> x9, starting transfers between devices: 13.3 us -> 12.8 us  [partner(): lax.ppermute(shard, axis, [(i, i ^ 1 << level) for i in range(lax.axis_si...]
    ppermute x10 -> x9, waiting for transfers between devices: 23.4 us -> 23.4 us  [partner(): lax.ppermute(shard, axis, [(i, i ^ 1 << level) for i in range(lax.axis_si...]
  transfers between devices with their start and end apart: 10 -> 9, of which waited for: 9 -> 8; matrix products, arithmetic and copies ran while one was open for 0% -> 0% of each run, Pallas kernels for 7% -> 7%
where the time goes in v4:
time: 47.4 us; the launch traced here: 47.2 us
  waiting for transfers between devices  23.4 us (49%)
  starting transfers between devices  12.8 us (27%)
  Pallas kernels  10.1 us (21%)
  between operations  0.73 us (2%)
    ppermute x9, waiting for transfers between devices, partner(): lax.ppermute(shard, axis, [(i, i ^ 1 << level) for i in range(lax.axis_si...  23.4 us
    ppermute x9, starting transfers between devices, partner(): lax.ppermute(shard, axis, [(i, i ^ 1 << level) for i in range(lax.axis_si...  12.8 us
    pallas_call x3, Pallas kernels, sketch_blocks(): pl.pallas_call(functools.partial(sketch_kernel, masks), out_shape=[jax.Sh...  4.87 us
    pallas_call x1, Pallas kernels, basis_and_triangle(): pl.pallas_call(functools.partial(basis_kernel, scale), out_shape=[jax.Sha...  4.66 us
  transfers between devices with their start and end apart: 9, of which 8 were waited for; matrix products, arithmetic and copies ran while one was open for 0% of the time, Pallas kernels for 7%

profile of v4, /device:TPU:0, one launch (start us, length us, event | category | flops | bytes accessed | tf_op | source)
XLA Modules:
  0.0 47.2 jit_solution(7358683815903470194)
XLA Ops:
  0.6 1.4 %shard_map.51 = f32[512,256]{1,0:T(8,128)S(1)} custom-call(bf16[2048,512]{1,0:T(8,128)(2,1)} %snapshots_ref.4, bf16[512,256]{1,0:T(8,128)(2,1)} %sketch_ref.5), custom_call_target="tpu_custom_call" | custom-call | flops 134217728 | bytes 1310720 | tf_op jit(solution)/shard_map/pallas_call | solution.py:76
  2.1 0.5 %collective-permute-start = (f32[512,256]{1,0:T(8,128)S(1)}, f32[512,256]{1,0:T(8,128)S(1)}, u32[]{:S(2)}, u32[]{:S(2)}) collective-permute-start(f32[512,256]{1,0:T(8,128)S(1)} %shard_map.51), channel_id=1, source_target_pairs={{0,1},{1,0},{2,3},{3,2},{4,5},{5,4},{6,7},{7,6},{8,9},{9,8},{10,11... | collective-permute-start | bytes 1572872 | tf_op jit(solution)/shard_map/ppermute | solution.py:24
  2.6 1.4 %shard_map.50 = f32[512,256]{1,0:T(8,128)S(1)} custom-call(bf16[2048,512]{1,0:T(8,128)(2,1)} %snapshots_ref.4, bf16[512,256]{1,0:T(8,128)(2,1)} %sketch_ref.5), custom_call_target="tpu_custom_call" | custom-call | flops 134217728 | bytes 1310720 | tf_op jit(solution)/shard_map/pallas_call | solution.py:76
  4.0 0.1 collective-permute-done
  4.1 0.1 add.18
  4.2 0.0 copy-start
  4.2 2.9 %collective-permute-start.2 = (f32[512,256]{1,0:T(8,128)S(1)}, f32[512,256]{1,0:T(8,128)S(1)}, u32[]{:S(2)}, u32[]{:S(2)}) collective-permute-start(f32[512,256]{1,0:T(8,128)S(1)} %add.18), channel_id=1, source_target_pairs={{0,2},{1,3},{2,0},{3,1},{4,6},{5,7},{6,4},{7,5},{8,10},{9,11},{10,... | collective-permute-start | bytes 1572872 | tf_op jit(solution)/shard_map/ppermute | solution.py:24
  7.1 2.0 %shard_map.52 = (f32[512,256]{1,0:T(8,128)S(1)}, f32[512,256]{1,0:T(8,128)S(1)}) custom-call(bf16[2048,512]{1,0:T(8,128)(2,1)} %snapshots_ref.4, bf16[512,256]{1,0:T(8,128)(2,1)} %sketch_ref.5), custom_call_target="tpu_custom_call" | custom-call | flops 268435456 | bytes 2359296 | tf_op jit(solution)/shard_map/pallas_call | solution.py:76
  9.1 0.1 collective-permute-start.1
  9.2 10.1 %collective-permute-done.2.far_ref = f32[512,256]{1,0:T(8,128)S(1)} collective-permute-done((f32[512,256]{1,0:T(8,128)S(1)}, f32[512,256]{1,0:T(8,128)S(1)}, u32[]{:S(2)}, u32[]{:S(2)}) %collective-permute-start.2) | collective-permute-done | bytes 524320 | tf_op jit(solution)/shard_map/ppermute | solution.py:24
  19.4 0.0 collective-permute-done.1.near_ref
  19.4 0.6 %shard_map.53 = (f32[512,256]{1,0:T(8,128)S(1)}, f32[136,128]{1,0:T(8,128)S(1)}, f32[136,128]{1,0:T(8,128)S(1)}) custom-call(s32[1]{0:T(128)} %bitcast.side_ref, f32[512,256]{1,0:T(8,128)S(1)} %get-tuple-element.9.kept_ref, f32[512,256]{1,0:T(8,128)S(1)} %collective-permute-done.1.near_ref, f32[512,256]{1,0:T(8,128)S(1)} %collective-permute-done.2.far_ref), custom_call_target="tpu_custom_call" | custom-call | flops 268435456 | bytes 2359296 | tf_op jit(solution)/shard_map/pallas_call | solution.py:119
  19.9 0.1 collective-permute-start.3
  20.0 1.2 %collective-permute-done.3 = f32[136,128]{1,0:T(8,128)S(1)} collective-permute-done((f32[136,128]{1,0:T(8,128)S(1)}, f32[136,128]{1,0:T(8,128)S(1)}, u32[]{:S(2)}, u32[]{:S(2)}) %collective-permute-start.3) | collective-permute-done | bytes 69664 | tf_op jit(solution)/shard_map/ppermute | solution.py:24
  21.3 1.8 %collective-permute-start.4 = (f32[136,128]{1,0:T(8,128)S(1)}, f32[136,128]{1,0:T(8,128)S(1)}, u32[]{:S(2)}, u32[]{:S(2)}) collective-permute-start(f32[136,128]{1,0:T(8,128)S(1)} %add.19), channel_id=1, source_target_pairs={{0,2},{1,3},{2,0},{3,1},{4,6},{5,7},{6,4},{7,5},{8,10},{9,11},{10,... | collective-permute-start | bytes 208904 | tf_op jit(solution)/shard_map/ppermute | solution.py:24
  23.1 2.6 %collective-permute-done.4 = f32[136,128]{1,0:T(8,128)S(1)} collective-permute-done((f32[136,128]{1,0:T(8,128)S(1)}, f32[136,128]{1,0:T(8,128)S(1)}, u32[]{:S(2)}, u32[]{:S(2)}) %collective-permute-start.4) | collective-permute-done | bytes 69664 | tf_op jit(solution)/shard_map/ppermute | solution.py:24
  25.7 1.8 %collective-permute-start.5 = (f32[136,128]{1,0:T(8,128)S(1)}, f32[136,128]{1,0:T(8,128)S(1)}, u32[]{:S(2)}, u32[]{:S(2)}) collective-permute-start(f32[136,128]{1,0:T(8,128)S(1)} %add.20), channel_id=1, source_target_pairs={{0,4},{4,0},{8,12},{12,8},{16,20},{20,16},{24,28},{28,24},{1,5},{5... | collective-permute-start | bytes 208904 | tf_op jit(solution)/shard_map/ppermute | solution.py:24
  27.5 2.5 %collective-permute-done.5 = f32[136,128]{1,0:T(8,128)S(1)} collective-permute-done((f32[136,128]{1,0:T(8,128)S(1)}, f32[136,128]{1,0:T(8,128)S(1)}, u32[]{:S(2)}, u32[]{:S(2)}) %collective-permute-start.5) | collective-permute-done | bytes 69664 | tf_op jit(solution)/shard_map/ppermute | solution.py:24
  30.0 1.9 %collective-permute-start.6 = (f32[136,128]{1,0:T(8,128)S(1)}, f32[136,128]{1,0:T(8,128)S(1)}, u32[]{:S(2)}, u32[]{:S(2)}) collective-permute-start(f32[136,128]{1,0:T(8,128)S(1)} %add.21), channel_id=1, source_target_pairs={{0,8},{4,12},{8,0},{12,4},{16,24},{20,28},{24,16},{28,20},{1,9},{5... | collective-permute-start | bytes 208904 | tf_op jit(solution)/shard_map/ppermute | solution.py:24
  31.9 2.5 %collective-permute-done.6 = f32[136,128]{1,0:T(8,128)S(1)} collective-permute-done((f32[136,128]{1,0:T(8,128)S(1)}, f32[136,128]{1,0:T(8,128)S(1)}, u32[]{:S(2)}, u32[]{:S(2)}) %collective-permute-start.6) | collective-permute-done | bytes 69664 | tf_op jit(solution)/shard_map/ppermute | solution.py:24
  34.4 3.6 %collective-permute-start.7 = (f32[136,128]{1,0:T(8,128)S(1)}, f32[136,128]{1,0:T(8,128)S(1)}, u32[]{:S(2)}, u32[]{:S(2)}) collective-permute-start(f32[136,128]{1,0:T(8,128)S(1)} %add.22), channel_id=1, source_target_pairs={{0,16},{4,20},{8,24},{12,28},{16,0},{20,4},{24,8},{28,12},{1,17},{... | collective-permute-start | bytes 208904 | tf_op jit(solution)/shard_map/ppermute | solution.py:24
  38.1 3.0 %collective-permute-done.7 = f32[136,128]{1,0:T(8,128)S(1)} collective-permute-done((f32[136,128]{1,0:T(8,128)S(1)}, f32[136,128]{1,0:T(8,128)S(1)}, u32[]{:S(2)}, u32[]{:S(2)}) %collective-permute-start.7) | collective-permute-done | bytes 69664 | tf_op jit(solution)/shard_map/ppermute | solution.py:24
  41.2 0.1 collective-permute-start.8
  41.2 1.3 %collective-permute-done.8.sent_ref = f32[264,128]{1,0:T(8,128)S(1)} collective-permute-done((f32[264,128]{1,0:T(8,128)S(1)}, f32[264,128]{1,0:T(8,128)S(1)}, u32[]{:S(2)}, u32[]{:S(2)}) %collective-permute-start.8) | collective-permute-done | bytes 135200 | tf_op jit(solution)/shard_map/ppermute | solution.py:24
  42.6 0.0 copy-done
  42.6 4.7 %shard_map.55 = (f32[512,256]{1,0:T(8,128)}, f32[256,256]{1,0:T(8,128)}) custom-call(s32[1]{0:T(128)} %bitcast.side_ref, f32[264,128]{1,0:T(8,128)S(1)} %shard_map.54.own_ref, f32[264,128]{1,0:T(8,128)S(1)} %collective-permute-done.8.sent_ref, f32[256,256]{1,0:T(8,128)S(1)} %copy-done, f32[512,256]{1,0:T(8,128)S(1)} %get-tuple-element.13.sketched_ref), custom_call_target="tpu_custom_call" | custom-call | flops 1073741824 | bytes 1835008 | tf_op jit(solution)/shard_map/pallas_call | solution.py:308
  (6 shorter events, 0.1 us)
Async XLA Ops:
  2.1 2.1 %collective-permute-start = (f32[512,256]{1,0:T(8,128)S(1)}, f32[512,256]{1,0:T(8,128)S(1)}, u32[]{:S(2)}, u32[]{:S(2)}) collective-permute-start(f32[512,256]{1,0:T(8,128)S(1)} %shard_map.51), channel_id=1, source_target_pairs={{0,1},{1,0},{2,3},{3,2},{4,5},{5,4},{6,7},{7,6},{8,9},{9,8},{10,11... | collective-permute-start | bytes 1572872 | tf_op jit(solution)/shard_map/ppermute | solution.py:24
  4.2 38.4 %copy-start = (f32[256,256]{1,0:T(8,128)S(1)}, f32[256,256]{1,0:T(8,128)}, u32[]{:S(2)}) copy-start(f32[256,256]{1,0:T(8,128)} %rotation_ref.1) | copy-start | bytes 786436
  4.2 15.2 %collective-permute-start.2 = (f32[512,256]{1,0:T(8,128)S(1)}, f32[512,256]{1,0:T(8,128)S(1)}, u32[]{:S(2)}, u32[]{:S(2)}) collective-permute-start(f32[512,256]{1,0:T(8,128)S(1)} %add.18), channel_id=1, source_target_pairs={{0,2},{1,3},{2,0},{3,1},{4,6},{5,7},{6,4},{7,5},{8,10},{9,11},{10,... | collective-permute-start | bytes 1572872 | tf_op jit(solution)/shard_map/ppermute | solution.py:24
  9.1 10.2 %collective-permute-start.1 = (f32[512,256]{1,0:T(8,128)S(1)}, f32[512,256]{1,0:T(8,128)S(1)}, u32[]{:S(2)}, u32[]{:S(2)}) collective-permute-start(f32[512,256]{1,0:T(8,128)S(1)} %get-tuple-element.10), channel_id=1, source_target_pairs={{0,1},{1,0},{2,3},{3,2},{4,5},{5,4},{6,7},{7,6},{8,9},{9,8},{10,11... | collective-permute-start | bytes 1572872 | tf_op jit(solution)/shard_map/ppermute | solution.py:24
  19.9 1.3 %collective-permute-start.3 = (f32[136,128]{1,0:T(8,128)S(1)}, f32[136,128]{1,0:T(8,128)S(1)}, u32[]{:S(2)}, u32[]{:S(2)}) collective-permute-start(f32[136,128]{1,0:T(8,128)S(1)} %get-tuple-element.12), channel_id=1, source_target_pairs={{0,1},{1,0},{2,3},{3,2},{4,5},{5,4},{6,7},{7,6},{8,9},{9,8},{10,11... | collective-permute-start | bytes 208904 | tf_op jit(solution)/shard_map/ppermute | solution.py:24
  21.3 4.4 %collective-permute-start.4 = (f32[136,128]{1,0:T(8,128)S(1)}, f32[136,128]{1,0:T(8,128)S(1)}, u32[]{:S(2)}, u32[]{:S(2)}) collective-permute-start(f32[136,128]{1,0:T(8,128)S(1)} %add.19), channel_id=1, source_target_pairs={{0,2},{1,3},{2,0},{3,1},{4,6},{5,7},{6,4},{7,5},{8,10},{9,11},{10,... | collective-permute-start | bytes 208904 | tf_op jit(solution)/shard_map/ppermute | solution.py:24
  25.7 4.4 %collective-permute-start.5 = (f32[136,128]{1,0:T(8,128)S(1)}, f32[136,128]{1,0:T(8,128)S(1)}, u32[]{:S(2)}, u32[]{:S(2)}) collective-permute-start(f32[136,128]{1,0:T(8,128)S(1)} %add.20), channel_id=1, source_target_pairs={{0,4},{4,0},{8,12},{12,8},{16,20},{20,16},{24,28},{28,24},{1,5},{5... | collective-permute-start | bytes 208904 | tf_op jit(solution)/shard_map/ppermute | solution.py:24
  30.0 4.4 %collective-permute-start.6 = (f32[136,128]{1,0:T(8,128)S(1)}, f32[136,128]{1,0:T(8,128)S(1)}, u32[]{:S(2)}, u32[]{:S(2)}) collective-permute-start(f32[136,128]{1,0:T(8,128)S(1)} %add.21), channel_id=1, source_target_pairs={{0,8},{4,12},{8,0},{12,4},{16,24},{20,28},{24,16},{28,20},{1,9},{5... | collective-permute-start | bytes 208904 | tf_op jit(solution)/shard_map/ppermute | solution.py:24
  34.4 6.7 %collective-permute-start.7 = (f32[136,128]{1,0:T(8,128)S(1)}, f32[136,128]{1,0:T(8,128)S(1)}, u32[]{:S(2)}, u32[]{:S(2)}) collective-permute-start(f32[136,128]{1,0:T(8,128)S(1)} %add.22), channel_id=1, source_target_pairs={{0,16},{4,20},{8,24},{12,28},{16,0},{20,4},{24,8},{28,12},{1,17},{... | collective-permute-start | bytes 208904 | tf_op jit(solution)/shard_map/ppermute | solution.py:24
  41.2 1.4 %collective-permute-start.8 = (f32[264,128]{1,0:T(8,128)S(1)}, f32[264,128]{1,0:T(8,128)S(1)}, u32[]{:S(2)}, u32[]{:S(2)}) collective-permute-start(f32[264,128]{1,0:T(8,128)S(1)} %shard_map.54.own_ref), channel_id=1, source_target_pairs={{0,1},{1,0},{2,3},{3,2},{4,5},{5,4},{6,7},{7,6},{8,9},{9,8},{10,11... | collective-permute-start | bytes 405512 | tf_op jit(solution)/shard_map/ppermute | solution.py:24

commit v5 on v4

--- a/solution.py
+++ b/solution.py
@@ -12,7 +12,7 @@
 VMEM = pl.BlockSpec(memory_space=pltpu.VMEM)
 SMEM = pl.BlockSpec(memory_space=pltpu.SMEM)
 BLOCK = 64
-CHUNKS = 2
+CHUNKS = 4
 PANEL = 2
 
 
@@ -20,8 +20,12 @@
     return pltpu.CompilerParams(vmem_limit_bytes=int(mib * 2**20))
 
 
-def partner(shard, axis, level):
-    return lax.ppermute(shard, axis, [(i, i ^ 1 << level) for i in range(lax.axis_size(axis))])
+AXES = ("space", "tm")
+
+
+def partner(shard, flip):
+    count = lax.axis_size("space") * lax.axis_size("tm")
+    return lax.ppermute(shard, AXES, [(i, i ^ flip) for i in range(count)])
 
 
 def levels(axis):
@@ -332,25 +336,27 @@
     kept, near = {}, {}
     for mask in range(lax.axis_size("tm") - 2, 0, -2):
         (leaving,) = sketch_blocks([mask | 1], snapshots, sketch)
-        near[mask] = partner(leaving, "tm", 0)
+        near[mask] = partner(leaving, 1)
         (kept[mask],) = sketch_blocks([mask], snapshots, sketch)
     for level in range(1, depth):
         for mask in [m for m in kept if m >> level & 1]:
             leaving = kept.pop(mask) + near.pop(mask)
-            arrived = partner(leaving, "tm", level)
+            arrived = partner(leaving, 1 << level)
             snapshots, leaving = lax.optimization_barrier((snapshots, leaving))
             if level < depth - 1:
                 near[mask ^ 1 << level] = near[mask ^ 1 << level] + arrived
     leaving, kept[0] = sketch_blocks([1, 0], snapshots, sketch)
-    near[0] = partner(leaving, "tm", 0)
+    near[0] = partner(leaving, 1)
     sketched, mine, send = gram_halves(side, kept[0], near[0], arrived)
-    mine = mine + partner(send, "tm", 0)
-    for level in range(1, depth):
-        mine = mine + partner(mine, "tm", level)
-    for level in range(levels("space")):
-        mine = mine + partner(mine, "space", level)
+    mine = mine + partner(send, 1)
+    flips = [1 << level for level in range(1, depth + levels("space"))]
+    if len(flips) > 1:
+        x, y, *flips = flips
+        mine = mine + ((partner(mine, x | y) + partner(mine, x)) + partner(mine, y))
+    for flip in flips:
+        mine = mine + partner(mine, flip)
     own = first_factor(side, mine)
-    return tuple(basis_and_triangle(side, own, partner(own, "tm", 0), rotation, sketched, math.sqrt(cells)))
+    return tuple(basis_and_triangle(side, own, partner(own, 1), rotation, sketched, math.sqrt(cells)))
 
 
 def solution(mesh):

time: 47.4 us -> 45.7 us (0.964)
  starting transfers between devices: 12.8 us -> 11.7 us
  waiting for transfers between devices: 23.4 us -> 22.9 us
    ppermute x9 -> x10, starting transfers between devices: 12.8 us -> 11.7 us  [partner(): return lax.ppermute(shard, AXES, [(i, i ^ flip) for i in range(count)])]
    ppermute x9 -> x10, waiting for transfers between devices: 23.4 us -> 22.9 us  [partner(): return lax.ppermute(shard, AXES, [(i, i ^ flip) for i in range(count)])]
  transfers between devices with their start and end apart: 9 -> 10, of which waited for: 8 -> 9; matrix products, arithmetic and copies ran while one was open for 0% -> 0% of each run, Pallas kernels for 7% -> 8%
where the time goes in v5:
time: 45.7 us; the launch traced here: 45.6 us
  waiting for transfers between devices  22.9 us (50%)
  starting transfers between devices  11.7 us (26%)
  Pallas kernels  10.1 us (22%)
  between operations  0.72 us (2%)
    ppermute x10, waiting for transfers between devices, partner(): return lax.ppermute(shard, AXES, [(i, i ^ flip) for i in range(count)])  22.9 us
    ppermute x10, starting transfers between devices, partner(): return lax.ppermute(shard, AXES, [(i, i ^ flip) for i in range(count)])  11.7 us
    pallas_call x3, Pallas kernels, sketch_blocks(): pl.pallas_call(functools.partial(sketch_kernel, masks), out_shape=[jax.Sh...  4.87 us
    pallas_call x1, Pallas kernels, basis_and_triangle(): pl.pallas_call(functools.partial(basis_kernel, scale), out_shape=[jax.Sha...  4.59 us
  transfers between devices with their start and end apart: 10, of which 9 were waited for; matrix products, arithmetic and copies ran while one was open for 0% of the time, Pallas kernels for 8%

profile of v5, /device:TPU:0, one launch (start us, length us, event | category | flops | bytes accessed | tf_op | source)
XLA Modules:
  0.0 45.6 jit_solution(12533065306689002478)
XLA Ops:
  0.6 1.4 %shard_map.51 = f32[512,256]{1,0:T(8,128)S(1)} custom-call(bf16[2048,512]{1,0:T(8,128)(2,1)} %snapshots_ref.4, bf16[512,256]{1,0:T(8,128)(2,1)} %sketch_ref.5), custom_call_target="tpu_custom_call" | custom-call | flops 134217728 | bytes 1310720 | tf_op jit(solution)/shard_map/pallas_call | solution.py:80
  2.1 0.5 %collective-permute-start = (f32[512,256]{1,0:T(8,128)S(1)}, f32[512,256]{1,0:T(8,128)S(1)}, u32[]{:S(2)}, u32[]{:S(2)}) collective-permute-start(f32[512,256]{1,0:T(8,128)S(1)} %shard_map.51), channel_id=1, source_target_pairs={{0,1},{1,0},{2,3},{3,2},{4,5},{5,4},{6,7},{7,6},{8,9},{9,8},{10,11... | collective-permute-start | bytes 1572872 | tf_op jit(solution)/shard_map/ppermute | solution.py:28
  2.6 1.4 %shard_map.50 = f32[512,256]{1,0:T(8,128)S(1)} custom-call(bf16[2048,512]{1,0:T(8,128)(2,1)} %snapshots_ref.4, bf16[512,256]{1,0:T(8,128)(2,1)} %sketch_ref.5), custom_call_target="tpu_custom_call" | custom-call | flops 134217728 | bytes 1310720 | tf_op jit(solution)/shard_map/pallas_call | solution.py:80
  4.0 0.1 collective-permute-done
  4.1 0.1 add.21
  4.2 0.0 copy-start
  4.2 2.9 %collective-permute-start.2 = (f32[512,256]{1,0:T(8,128)S(1)}, f32[512,256]{1,0:T(8,128)S(1)}, u32[]{:S(2)}, u32[]{:S(2)}) collective-permute-start(f32[512,256]{1,0:T(8,128)S(1)} %add.21), channel_id=1, source_target_pairs={{0,2},{1,3},{2,0},{3,1},{4,6},{5,7},{6,4},{7,5},{8,10},{9,11},{10,... | collective-permute-start | bytes 1572872 | tf_op jit(solution)/shard_map/ppermute | solution.py:28
  7.1 2.0 %shard_map.52 = (f32[512,256]{1,0:T(8,128)S(1)}, f32[512,256]{1,0:T(8,128)S(1)}) custom-call(bf16[2048,512]{1,0:T(8,128)(2,1)} %snapshots_ref.4, bf16[512,256]{1,0:T(8,128)(2,1)} %sketch_ref.5), custom_call_target="tpu_custom_call" | custom-call | flops 268435456 | bytes 2359296 | tf_op jit(solution)/shard_map/pallas_call | solution.py:80
  9.1 0.1 collective-permute-start.1
  9.2 10.1 %collective-permute-done.2.far_ref = f32[512,256]{1,0:T(8,128)S(1)} collective-permute-done((f32[512,256]{1,0:T(8,128)S(1)}, f32[512,256]{1,0:T(8,128)S(1)}, u32[]{:S(2)}, u32[]{:S(2)}) %collective-permute-start.2) | collective-permute-done | bytes 524320 | tf_op jit(solution)/shard_map/ppermute | solution.py:28
  19.4 0.0 collective-permute-done.1.near_ref
  19.4 0.6 %shard_map.53 = (f32[512,256]{1,0:T(8,128)S(1)}, f32[136,128]{1,0:T(8,128)S(1)}, f32[136,128]{1,0:T(8,128)S(1)}) custom-call(s32[1]{0:T(128)} %bitcast.side_ref, f32[512,256]{1,0:T(8,128)S(1)} %get-tuple-element.9.kept_ref, f32[512,256]{1,0:T(8,128)S(1)} %collective-permute-done.1.near_ref, f32[512,256]{1,0:T(8,128)S(1)} %collective-permute-done.2.far_ref), custom_call_target="tpu_custom_call" | custom-call | flops 268435456 | bytes 2359296 | tf_op jit(solution)/shard_map/pallas_call | solution.py:123
  19.9 0.1 collective-permute-start.3
  20.0 1.2 %collective-permute-done.3 = f32[136,128]{1,0:T(8,128)S(1)} collective-permute-done((f32[136,128]{1,0:T(8,128)S(1)}, f32[136,128]{1,0:T(8,128)S(1)}, u32[]{:S(2)}, u32[]{:S(2)}) %collective-permute-start.3) | collective-permute-done | bytes 69664 | tf_op jit(solution)/shard_map/ppermute | solution.py:28
  21.3 1.8 %collective-permute-start.6 = (f32[136,128]{1,0:T(8,128)S(1)}, f32[136,128]{1,0:T(8,128)S(1)}, u32[]{:S(2)}, u32[]{:S(2)}) collective-permute-start(f32[136,128]{1,0:T(8,128)S(1)} %add.22), channel_id=1, source_target_pairs={{0,4},{1,5},{2,6},{3,7},{4,0},{5,1},{6,2},{7,3},{8,12},{9,13},{10,... | collective-permute-start | bytes 208904 | tf_op jit(solution)/shard_map/ppermute | solution.py:28
  23.1 1.5 %collective-permute-start.5 = (f32[136,128]{1,0:T(8,128)S(1)}, f32[136,128]{1,0:T(8,128)S(1)}, u32[]{:S(2)}, u32[]{:S(2)}) collective-permute-start(f32[136,128]{1,0:T(8,128)S(1)} %add.22), channel_id=1, source_target_pairs={{0,2},{1,3},{2,0},{3,1},{4,6},{5,7},{6,4},{7,5},{8,10},{9,11},{10,... | collective-permute-start | bytes 208904 | tf_op jit(solution)/shard_map/ppermute | solution.py:28
  24.6 0.2 collective-permute-start.4
  24.8 0.8 %collective-permute-done.6 = f32[136,128]{1,0:T(8,128)S(1)} collective-permute-done((f32[136,128]{1,0:T(8,128)S(1)}, f32[136,128]{1,0:T(8,128)S(1)}, u32[]{:S(2)}, u32[]{:S(2)}) %collective-permute-start.6) | collective-permute-done | bytes 69664 | tf_op jit(solution)/shard_map/ppermute | solution.py:28
  25.6 2.5 %collective-permute-done.5 = f32[136,128]{1,0:T(8,128)S(1)} collective-permute-done((f32[136,128]{1,0:T(8,128)S(1)}, f32[136,128]{1,0:T(8,128)S(1)}, u32[]{:S(2)}, u32[]{:S(2)}) %collective-permute-start.5) | collective-permute-done | bytes 69664 | tf_op jit(solution)/shard_map/ppermute | solution.py:28
  28.1 1.7 %collective-permute-done.4 = f32[136,128]{1,0:T(8,128)S(1)} collective-permute-done((f32[136,128]{1,0:T(8,128)S(1)}, f32[136,128]{1,0:T(8,128)S(1)}, u32[]{:S(2)}, u32[]{:S(2)}) %collective-permute-start.4) | collective-permute-done | bytes 69664 | tf_op jit(solution)/shard_map/ppermute | solution.py:28
  29.8 1.6 %collective-permute-start.7 = (f32[136,128]{1,0:T(8,128)S(1)}, f32[136,128]{1,0:T(8,128)S(1)}, u32[]{:S(2)}, u32[]{:S(2)}) collective-permute-start(f32[136,128]{1,0:T(8,128)S(1)} %add_add_fusion), channel_id=1, source_target_pairs={{0,8},{1,9},{2,10},{3,11},{4,12},{5,13},{6,14},{7,15},{8,0},{9,1},... | collective-permute-start | bytes 208904 | tf_op jit(solution)/shard_map/ppermute | solution.py:28
  31.5 2.7 %collective-permute-done.7 = f32[136,128]{1,0:T(8,128)S(1)} collective-permute-done((f32[136,128]{1,0:T(8,128)S(1)}, f32[136,128]{1,0:T(8,128)S(1)}, u32[]{:S(2)}, u32[]{:S(2)}) %collective-permute-start.7) | collective-permute-done | bytes 69664 | tf_op jit(solution)/shard_map/ppermute | solution.py:28
  34.2 2.9 %collective-permute-start.8 = (f32[136,128]{1,0:T(8,128)S(1)}, f32[136,128]{1,0:T(8,128)S(1)}, u32[]{:S(2)}, u32[]{:S(2)}) collective-permute-start(f32[136,128]{1,0:T(8,128)S(1)} %add.26), channel_id=1, source_target_pairs={{0,16},{1,17},{2,18},{3,19},{4,20},{5,21},{6,22},{7,23},{8,24},{9,... | collective-permute-start | bytes 208904 | tf_op jit(solution)/shard_map/ppermute | solution.py:28
  37.1 2.4 %collective-permute-done.8 = f32[136,128]{1,0:T(8,128)S(1)} collective-permute-done((f32[136,128]{1,0:T(8,128)S(1)}, f32[136,128]{1,0:T(8,128)S(1)}, u32[]{:S(2)}, u32[]{:S(2)}) %collective-permute-start.8) | collective-permute-done | bytes 69664 | tf_op jit(solution)/shard_map/ppermute | solution.py:28
  39.5 0.1 collective-permute-start.9
  39.6 1.3 %collective-permute-done.9.sent_ref = f32[264,128]{1,0:T(8,128)S(1)} collective-permute-done((f32[264,128]{1,0:T(8,128)S(1)}, f32[264,128]{1,0:T(8,128)S(1)}, u32[]{:S(2)}, u32[]{:S(2)}) %collective-permute-start.9) | collective-permute-done | bytes 135200 | tf_op jit(solution)/shard_map/ppermute | solution.py:28
  41.0 0.0 copy-done
  41.0 4.6 %shard_map.55 = (f32[512,256]{1,0:T(8,128)}, f32[256,256]{1,0:T(8,128)}) custom-call(s32[1]{0:T(128)} %bitcast.side_ref, f32[264,128]{1,0:T(8,128)S(1)} %shard_map.54.own_ref, f32[264,128]{1,0:T(8,128)S(1)} %collective-permute-done.9.sent_ref, f32[256,256]{1,0:T(8,128)S(1)} %copy-done, f32[512,256]{1,0:T(8,128)S(1)} %get-tuple-element.13.sketched_ref), custom_call_target="tpu_custom_call" | custom-call | flops 1073741824 | bytes 1835008 | tf_op jit(solution)/shard_map/pallas_call | solution.py:312
  (5 shorter events, 0.1 us)
Async XLA Ops:
  2.1 2.1 %collective-permute-start = (f32[512,256]{1,0:T(8,128)S(1)}, f32[512,256]{1,0:T(8,128)S(1)}, u32[]{:S(2)}, u32[]{:S(2)}) collective-permute-start(f32[512,256]{1,0:T(8,128)S(1)} %shard_map.51), channel_id=1, source_target_pairs={{0,1},{1,0},{2,3},{3,2},{4,5},{5,4},{6,7},{7,6},{8,9},{9,8},{10,11... | collective-permute-start | bytes 1572872 | tf_op jit(solution)/shard_map/ppermute | solution.py:28
  4.2 36.8 %copy-start = (f32[256,256]{1,0:T(8,128)S(1)}, f32[256,256]{1,0:T(8,128)}, u32[]{:S(2)}) copy-start(f32[256,256]{1,0:T(8,128)} %rotation_ref.1) | copy-start | bytes 786436
  4.2 15.2 %collective-permute-start.2 = (f32[512,256]{1,0:T(8,128)S(1)}, f32[512,256]{1,0:T(8,128)S(1)}, u32[]{:S(2)}, u32[]{:S(2)}) collective-permute-start(f32[512,256]{1,0:T(8,128)S(1)} %add.21), channel_id=1, source_target_pairs={{0,2},{1,3},{2,0},{3,1},{4,6},{5,7},{6,4},{7,5},{8,10},{9,11},{10,... | collective-permute-start | bytes 1572872 | tf_op jit(solution)/shard_map/ppermute | solution.py:28
  9.1 10.2 %collective-permute-start.1 = (f32[512,256]{1,0:T(8,128)S(1)}, f32[512,256]{1,0:T(8,128)S(1)}, u32[]{:S(2)}, u32[]{:S(2)}) collective-permute-start(f32[512,256]{1,0:T(8,128)S(1)} %get-tuple-element.10), channel_id=1, source_target_pairs={{0,1},{1,0},{2,3},{3,2},{4,5},{5,4},{6,7},{7,6},{8,9},{9,8},{10,11... | collective-permute-start | bytes 1572872 | tf_op jit(solution)/shard_map/ppermute | solution.py:28
  19.9 1.3 %collective-permute-start.3 = (f32[136,128]{1,0:T(8,128)S(1)}, f32[136,128]{1,0:T(8,128)S(1)}, u32[]{:S(2)}, u32[]{:S(2)}) collective-permute-start(f32[136,128]{1,0:T(8,128)S(1)} %get-tuple-element.12), channel_id=1, source_target_pairs={{0,1},{1,0},{2,3},{3,2},{4,5},{5,4},{6,7},{7,6},{8,9},{9,8},{10,11... | collective-permute-start | bytes 208904 | tf_op jit(solution)/shard_map/ppermute | solution.py:28
  21.3 4.4 %collective-permute-start.6 = (f32[136,128]{1,0:T(8,128)S(1)}, f32[136,128]{1,0:T(8,128)S(1)}, u32[]{:S(2)}, u32[]{:S(2)}) collective-permute-start(f32[136,128]{1,0:T(8,128)S(1)} %add.22), channel_id=1, source_target_pairs={{0,4},{1,5},{2,6},{3,7},{4,0},{5,1},{6,2},{7,3},{8,12},{9,13},{10,... | collective-permute-start | bytes 208904 | tf_op jit(solution)/shard_map/ppermute | solution.py:28
  23.1 5.0 %collective-permute-start.5 = (f32[136,128]{1,0:T(8,128)S(1)}, f32[136,128]{1,0:T(8,128)S(1)}, u32[]{:S(2)}, u32[]{:S(2)}) collective-permute-start(f32[136,128]{1,0:T(8,128)S(1)} %add.22), channel_id=1, source_target_pairs={{0,2},{1,3},{2,0},{3,1},{4,6},{5,7},{6,4},{7,5},{8,10},{9,11},{10,... | collective-permute-start | bytes 208904 | tf_op jit(solution)/shard_map/ppermute | solution.py:28
  24.6 5.2 %collective-permute-start.4 = (f32[136,128]{1,0:T(8,128)S(1)}, f32[136,128]{1,0:T(8,128)S(1)}, u32[]{:S(2)}, u32[]{:S(2)}) collective-permute-start(f32[136,128]{1,0:T(8,128)S(1)} %add.22), channel_id=1, source_target_pairs={{0,6},{1,7},{2,4},{3,5},{4,2},{5,3},{6,0},{7,1},{8,14},{9,15},{10,... | collective-permute-start | bytes 208904 | tf_op jit(solution)/shard_map/ppermute | solution.py:28
  29.8 4.4 %collective-permute-start.7 = (f32[136,128]{1,0:T(8,128)S(1)}, f32[136,128]{1,0:T(8,128)S(1)}, u32[]{:S(2)}, u32[]{:S(2)}) collective-permute-start(f32[136,128]{1,0:T(8,128)S(1)} %add_add_fusion), channel_id=1, source_target_pairs={{0,8},{1,9},{2,10},{3,11},{4,12},{5,13},{6,14},{7,15},{8,0},{9,1},... | collective-permute-start | bytes 208904 | tf_op jit(solution)/shard_map/ppermute | solution.py:28
  34.2 5.3 %collective-permute-start.8 = (f32[136,128]{1,0:T(8,128)S(1)}, f32[136,128]{1,0:T(8,128)S(1)}, u32[]{:S(2)}, u32[]{:S(2)}) collective-permute-start(f32[136,128]{1,0:T(8,128)S(1)} %add.26), channel_id=1, source_target_pairs={{0,16},{1,17},{2,18},{3,19},{4,20},{5,21},{6,22},{7,23},{8,24},{9,... | collective-permute-start | bytes 208904 | tf_op jit(solution)/shard_map/ppermute | solution.py:28
  39.5 1.4 %collective-permute-start.9 = (f32[264,128]{1,0:T(8,128)S(1)}, f32[264,128]{1,0:T(8,128)S(1)}, u32[]{:S(2)}, u32[]{:S(2)}) collective-permute-start(f32[264,128]{1,0:T(8,128)S(1)} %shard_map.54.own_ref), channel_id=1, source_target_pairs={{0,1},{1,0},{2,3},{3,2},{4,5},{5,4},{6,7},{7,6},{8,9},{9,8},{10,11... | collective-permute-start | bytes 405512 | tf_op jit(solution)/shard_map/ppermute | solution.py:28

commit v6 on v5

--- a/solution.py
+++ b/solution.py
@@ -12,6 +12,8 @@
 VMEM = pl.BlockSpec(memory_space=pltpu.VMEM)
 SMEM = pl.BlockSpec(memory_space=pltpu.SMEM)
 BLOCK = 64
+SLICES = 4
+PARTS = 2
 CHUNKS = 4
 PANEL = 2
 
@@ -56,60 +58,129 @@
     return product(stacked(x, LEFT, over[0]), stacked(y, RIGHT, over[1]), ((over[0],), (over[1],)))
 
 
-def sketch_kernel(masks, snapshots_ref, sketch_ref, *rest):
-    outs, (tall, wide, arrived, ready) = rest[: len(masks)], rest[len(masks) :]
-    rows = tall.shape[0] // len(masks)
-    index = lax.axis_index("tm")
-    fetch = pltpu.make_async_copy(sketch_ref, wide, ready)
-    fetch.start()
-    copies = []
-    for i, mask in enumerate(masks):
-        block = pl.ds(pl.multiple_of((index ^ mask) * rows, rows), rows)
-        copies.append(pltpu.make_async_copy(snapshots_ref.at[block], tall.at[pl.ds(rows * i, rows)], arrived.at[i]))
-        copies[-1].start()
-    fetch.wait()
+def triangles(shape):
+    row = lax.broadcasted_iota(jnp.int32, shape, 0)
+    column = lax.broadcasted_iota(jnp.int32, shape, 1)
+    return row > column, row == column
+
+
+def rows_of(ref, mask, rows):
+    block = lax.axis_index("tm") ^ mask
+    return ref.at[pl.ds(pl.multiple_of(block * rows, rows), rows)]
+
+
+def in_hbm(x):
+    return pltpu.with_memory_space_constraint(x, pltpu.HBM)
+
+
+def leaving_kernel(leaves, stays, snapshots_ref, sketch_ref, *rest):
+    *outs, next_ref, wide, tall, arrived = rest
+    rows, step = tall.shape[0], outs[0].shape[0]
+    copies = [
+        pltpu.make_async_copy(sketch_ref, wide, arrived.at[0]),
+        pltpu.make_async_copy(rows_of(snapshots_ref, leaves, rows), tall, arrived.at[1]),
+        pltpu.make_async_copy(rows_of(snapshots_ref, stays, rows), next_ref, arrived.at[2]),
+    ]
+    for copy in copies:
+        copy.start()
+    copies[0].wait()
+    copies[1].wait()
     for i, out in enumerate(outs):
-        copies[i].wait()
-        out[...] = jnp.dot(tall[rows * i : rows * (i + 1), :], wide[...], preferred_element_type=F32)
-
-
-def sketch_blocks(masks, snapshots, sketch):
+        out[...] = jnp.dot(tall[step * i : step * (i + 1), :], wide[...], preferred_element_type=F32)
+    copies[2].wait()
+
+
+def sketch_leaving(leaves, stays, snapshots, sketch):
     rows = snapshots.shape[0] // lax.axis_size("tm")
     depth, columns = sketch.shape
-    count = len(masks)
-    return pl.pallas_call(
-        functools.partial(sketch_kernel, masks),
-        out_shape=[jax.ShapeDtypeStruct((rows, columns), F32)] * count,
+    return pl.pallas_call(
+        functools.partial(leaving_kernel, leaves, stays),
+        out_shape=[jax.ShapeDtypeStruct((rows // PARTS, columns), F32)] * PARTS
+        + [jax.ShapeDtypeStruct((rows, depth), BF16), jax.ShapeDtypeStruct((depth, columns), BF16)],
         in_specs=[pl.BlockSpec(memory_space=pltpu.HBM)] * 2,
-        out_specs=[VMEM] * count,
+        out_specs=[VMEM] * (PARTS + 2),
+        scratch_shapes=[pltpu.VMEM((rows, depth), BF16), pltpu.SemaphoreType.DMA((3,))],
+        compiler_params=params(),
+        cost_estimate=pl.CostEstimate(
+            flops=2 * rows * depth * columns, bytes_accessed=4 * rows * depth + 4 * depth * columns, transcendentals=0
+        ),
+    )(in_hbm(snapshots), in_hbm(sketch))
+
+
+def staying_kernel(rows_ref, sketch_ref, *outs):
+    step = outs[0].shape[0]
+    for i, out in enumerate(outs):
+        out[...] = jnp.dot(rows_ref[step * i : step * (i + 1), :], sketch_ref[...], preferred_element_type=F32)
+
+
+def sketch_staying(rows, sketch):
+    count, depth = rows.shape
+    columns = sketch.shape[1]
+    return pl.pallas_call(
+        staying_kernel,
+        out_shape=[jax.ShapeDtypeStruct((count // PARTS, columns), F32)] * PARTS,
+        in_specs=[VMEM] * 2,
+        out_specs=[VMEM] * PARTS,
+        compiler_params=params(),
+        cost_estimate=pl.CostEstimate(flops=2 * count * depth * columns, bytes_accessed=2 * count * depth, transcendentals=0),
+    )(rows, sketch)
+
+
+def last_kernel(snapshots_ref, sketch_ref, *refs):
+    *outs, tall, wide, arrived = refs
+    rows = tall.shape[0] // 2
+    copies = [pltpu.make_async_copy(sketch_ref, wide, arrived.at[0])]
+    for i in range(2):
+        copies.append(pltpu.make_async_copy(rows_of(snapshots_ref, 1 - i, rows), tall.at[pl.ds(rows * i, rows)], arrived.at[1 + i]))
+    for copy in copies:
+        copy.start()
+    copies[0].wait()
+    place = 0
+    for i, out in enumerate(outs):
+        if i in (0, SLICES):
+            copies[1 + i // SLICES].wait()
+        count = out.shape[0]
+        out[...] = jnp.dot(tall[place : place + count, :], wide[...], preferred_element_type=F32)
+        place += count
+
+
+def sketch_last(snapshots, sketch):
+    rows = snapshots.shape[0] // lax.axis_size("tm")
+    depth, columns = sketch.shape
+    return pl.pallas_call(
+        last_kernel,
+        out_shape=[jax.ShapeDtypeStruct((rows // SLICES, columns), F32)] * SLICES + [jax.ShapeDtypeStruct((rows, columns), F32)],
+        in_specs=[pl.BlockSpec(memory_space=pltpu.HBM)] * 2,
+        out_specs=[VMEM] * (SLICES + 1),
         scratch_shapes=[
-            pltpu.VMEM((count * rows, depth), BF16),
+            pltpu.VMEM((2 * rows, depth), BF16),
             pltpu.VMEM((depth, columns), BF16),
-            pltpu.SemaphoreType.DMA((count,)),
-            pltpu.SemaphoreType.DMA,
+            pltpu.SemaphoreType.DMA((3,)),
         ],
         compiler_params=params(),
-        cost_estimate=pl.CostEstimate(
-            flops=2 * count * rows * depth * columns,
-            bytes_accessed=count * rows * (2 * depth + 4 * columns) + 2 * depth * columns,
-            transcendentals=0,
-        ),
-    )(pltpu.with_memory_space_constraint(snapshots, pltpu.HBM), pltpu.with_memory_space_constraint(sketch, pltpu.HBM))
-
-
-def gram_kernel(side_ref, kept_ref, near_ref, far_ref, sketched_ref, keep_ref, send_ref):
-    sketched = (kept_ref[...] + near_ref[...]) + far_ref[...]
+        cost_estimate=pl.CostEstimate(flops=1, bytes_accessed=1, transcendentals=0),
+    )(in_hbm(snapshots), in_hbm(sketch))
+
+
+def gram_kernel(part, side_ref, kept_ref, far_ref, *rest):
+    near_refs, rest = rest[: SLICES // PARTS], rest[SLICES // PARTS :]
+    before, (sketched_ref, *outs) = rest[: min(part, 1)], rest[min(part, 1) :]
+    rows = far_ref.shape[0]
+    mine = slice(rows * part, rows * (part + 1))
+    sketched = (kept_ref[mine, :] + jnp.concatenate([ref[...] for ref in near_refs], axis=0)) + far_ref[...]
     sketched_ref[...] = sketched
-    high, middle, low = split(sketched)
-    rows = ((0,), (0,))
-    cross = product(high, middle, rows) + product(high, low, rows)
-    gram = product(high, high, rows) + (cross + cross.T + product(middle, middle, rows))
+    gram = dot_parts(sketched, sketched, (0, 0))
+    if before:
+        gram = gram + before[0][...]
+    if part < PARTS - 1:
+        outs[0][...] = gram
+        return
+    keep_ref, send_ref = outs
     h = gram.shape[0] // 2
-    row = lax.broadcasted_iota(jnp.int32, (h, h), 0)
-    column = lax.broadcasted_iota(jnp.int32, (h, h), 1)
+    lower, middle = triangles((h, h))
     corner = gram[h:, h:]
-    diagonal = jnp.sum(jnp.where(row == column, corner, 0.0), axis=0, keepdims=True)
-    mixed = jnp.where(row >= column, gram[:h, :h], corner)
+    diagonal = jnp.sum(jnp.where(middle, corner, 0.0), axis=0, keepdims=True)
+    mixed = jnp.where(lower | middle, gram[:h, :h], corner)
     first = side_ref[0] == 0
     keep_ref[:h, :] = jnp.where(first, gram[h:, :h], mixed)
     send_ref[:h, :] = jnp.where(first, mixed, gram[h:, :h])
@@ -117,19 +188,20 @@
     send_ref[h:, :] = jnp.broadcast_to(diagonal, (8, h))
 
 
-def gram_halves(side, kept, near, far):
-    rows, n = kept.shape
+def gram_part(part, side, kept, near, far, *before):
+    rows, n = far.shape
     half = jax.ShapeDtypeStruct((n // 2 + 8, n // 2), F32)
-    return pl.pallas_call(
-        gram_kernel,
-        out_shape=[jax.ShapeDtypeStruct((rows, n), F32), half, half],
-        in_specs=[SMEM, VMEM, VMEM, VMEM],
-        out_specs=[VMEM] * 3,
+    outs = [half, half] if part == PARTS - 1 else [jax.ShapeDtypeStruct((n, n), F32)]
+    return pl.pallas_call(
+        functools.partial(gram_kernel, part),
+        out_shape=[jax.ShapeDtypeStruct((rows, n), F32)] + outs,
+        in_specs=[SMEM] + [VMEM] * (2 + len(near) + len(before)),
+        out_specs=[VMEM] * (1 + len(outs)),
         compiler_params=params(),
         cost_estimate=pl.CostEstimate(
-            flops=8 * rows * n * n, bytes_accessed=16 * rows * n + 4 * n * n, transcendentals=0
+            flops=12 * rows * n * n, bytes_accessed=16 * rows * n + 4 * n * n, transcendentals=0
         ),
-    )(side, kept, near, far)
+    )(side, kept, far, *near, *before)
 
 
 def column(v, c):
@@ -227,12 +299,6 @@
                         a[top : top + 8, 128 * k : 128 * k + 128] = old - new
 
 
-def triangles(shape):
-    row = lax.broadcasted_iota(jnp.int32, shape, 0)
-    column = lax.broadcasted_iota(jnp.int32, shape, 1)
-    return row > column, row == column
-
-
 def first_kernel(side_ref, mine_ref, out_ref, a, upper, inverse):
     h = a.shape[0]
     lower, middle = triangles((h, h))
@@ -268,8 +334,10 @@
 
 
 def basis_kernel(
-    scale, side_ref, own_ref, sent_ref, rotation_ref, sketched_ref, basis_ref, triangle_ref, a, upper, inverse, rest, basis, triangle, sent
+    scale, side_ref, own_ref, sent_ref, rotation_ref, *refs
 ):
+    sketched_refs, refs = refs[:PARTS], refs[PARTS:]
+    basis_ref, triangle_ref, a, upper, inverse, rest, basis, triangle, sent = refs
     h = a.shape[0]
     rows = basis.shape[0]
     lower, middle = triangles((h, h))
@@ -287,10 +355,11 @@
     triangle[h:, :h] = jnp.zeros((h, h), F32)
     copies = [pltpu.make_async_copy(triangle.at[pl.ds(h * i, h)], triangle_ref.at[pl.ds(h * i, h)], sent.at[i]) for i in range(2)]
     copies[0].start()
-    x1, x2 = sketched_ref[:, :h], sketched_ref[:, h:]
     mapping = dot_parts(inverse1, scale * rotation_ref[:h, :], (0, 0))
-    basis[...] = dot_parts(x1, mapping, (1, 0))
-    rest[...] = stacked(x2 - dot_parts(x1, ahead, (1, 1)), LEFT, 1)
+    for i, ref in enumerate(sketched_refs):
+        x1, x2, part = ref[:, :h], ref[:, h:], pl.ds(rows // PARTS * i, rows // PARTS)
+        basis[part, :] = dot_parts(x1, mapping, (1, 0))
+        rest[part, :] = stacked(x2 - dot_parts(x1, ahead, (1, 1)), LEFT, 1)
     turned = stacked(scale * rotation_ref[h:, :], RIGHT, 0)
     factor(a, upper, inverse)
     triangle[h:, h:] = upper[...] * (1.0 / scale)
@@ -307,12 +376,12 @@
 
 
 def basis_and_triangle(side, own, sent, rotation, sketched, scale):
-    rows, n = sketched.shape
+    rows, n = sketched[0].shape[0] * PARTS, sketched[0].shape[1]
     h = n // 2
     return pl.pallas_call(
         functools.partial(basis_kernel, scale),
         out_shape=[jax.ShapeDtypeStruct((rows, n), F32), jax.ShapeDtypeStruct((n, n), F32)],
-        in_specs=[SMEM] + [VMEM] * 4,
+        in_specs=[SMEM] + [VMEM] * (3 + PARTS),
         out_specs=[pl.BlockSpec(memory_space=pltpu.HBM)] * 2,
         scratch_shapes=[pltpu.VMEM((h, h), F32)] * 3
         + [
@@ -325,7 +394,7 @@
         cost_estimate=pl.CostEstimate(
             flops=12 * rows * n * n + 40 * n * n * n, bytes_accessed=8 * rows * n + 12 * n * n, transcendentals=n
         ),
-    )(side, own, sent, rotation, sketched)
+    )(side, own, sent, rotation, *sketched)
 
 
 def shards(snapshots, sketch, rotation):
@@ -335,19 +404,25 @@
 
     kept, near = {}, {}
     for mask in range(lax.axis_size("tm") - 2, 0, -2):
-        (leaving,) = sketch_blocks([mask | 1], snapshots, sketch)
-        near[mask] = partner(leaving, 1)
-        (kept[mask],) = sketch_blocks([mask], snapshots, sketch)
+        *leaving, rows, held = sketch_leaving(mask | 1, mask, snapshots, sketch)
+        near[mask] = [partner(part, 1) for part in leaving]
+        kept[mask] = sketch_staying(rows, held)
     for level in range(1, depth):
         for mask in [m for m in kept if m >> level & 1]:
-            leaving = kept.pop(mask) + near.pop(mask)
-            arrived = partner(leaving, 1 << level)
-            snapshots, leaving = lax.optimization_barrier((snapshots, leaving))
+            leaving = [x + y for x, y in zip(kept.pop(mask), near.pop(mask))]
+            arrived = [partner(part, 1 << level) for part in leaving]
+            snapshots, *leaving = lax.optimization_barrier((snapshots, *leaving))
             if level < depth - 1:
-                near[mask ^ 1 << level] = near[mask ^ 1 << level] + arrived
-    leaving, kept[0] = sketch_blocks([1, 0], snapshots, sketch)
-    near[0] = partner(leaving, 1)
-    sketched, mine, send = gram_halves(side, kept[0], near[0], arrived)
+                stays = mask ^ 1 << level
+                near[stays] = [x + y for x, y in zip(near[stays], arrived)]
+    *leaving, kept = sketch_last(snapshots, sketch)
+    near = [partner(part, 1) for part in leaving]
+    sketched, before = [], []
+    for part in range(PARTS):
+        count = SLICES // PARTS
+        rows, *before = gram_part(part, side, kept, near[count * part : count * (part + 1)], arrived[part], *before)
+        sketched.append(rows)
+    mine, send = before
     mine = mine + partner(send, 1)
     flips = [1 << level for level in range(1, depth + levels("space"))]
     if len(flips) > 1:

time: 45.7 us -> 45.2 us (0.989)
  Pallas kernels: 10.1 us -> 8.96 us
  starting transfers between devices: 11.7 us -> 12.8 us
  waiting for transfers between devices: 22.9 us -> 22.3 us
    ppermute x10 -> x15, starting transfers between devices: 11.7 us -> 12.8 us  [partner(): return lax.ppermute(shard, AXES, [(i, i ^ flip) for i in range(count)])]
    pallas_call x4 -> x5, Pallas kernels: 5.43 us -> 4.34 us  [the longest x1 1.77 us: sketch_last(): pl.pallas_call(last_kernel, out_shape=[jax.ShapeDtypeStruct((rows // SLIC...]
    ppermute x10 -> x15, waiting for transfers between devices: 22.9 us -> 22.3 us  [partner(): return lax.ppermute(shard, AXES, [(i, i ^ flip) for i in range(count)])]
  transfers between devices with their start and end apart: 10 -> 15, of which waited for: 9 -> 12; matrix products, arithmetic and copies ran while one was open for 0% -> 0% of each run, Pallas kernels for 8% -> 5%
where the time goes in v6:
time: 45.2 us; the launch traced here: 45 us
  waiting for transfers between devices  22.3 us (49%)
  starting transfers between devices  12.8 us (28%)
  Pallas kernels  8.96 us (20%)
  between operations  0.75 us (2%)
    ppermute x15, waiting for transfers between devices, partner(): return lax.ppermute(shard, AXES, [(i, i ^ flip) for i in range(count)])  22.3 us
    ppermute x15, starting transfers between devices, partner(): return lax.ppermute(shard, AXES, [(i, i ^ flip) for i in range(count)])  12.8 us
    pallas_call x1, Pallas kernels, basis_and_triangle(): pl.pallas_call(functools.partial(basis_kernel, scale), out_shape=[jax.Sha...  4.59 us
    pallas_call x1, Pallas kernels, sketch_last(): pl.pallas_call(last_kernel, out_shape=[jax.ShapeDtypeStruct((rows // SLIC...  1.77 us
    pallas_call x1, Pallas kernels, sketch_leaving(): pl.pallas_call(functools.partial(leaving_kernel, leaves, stays), out_shap...  1.46 us
  transfers between devices with their start and end apart: 15, of which 12 were waited for; matrix products, arithmetic and copies ran while one was open for 0% of the time, Pallas kernels for 5%

profile of v6, /device:TPU:0, one launch (start us, length us, event | category | flops | bytes accessed | tf_op | source)
XLA Modules:
  0.0 45.0 jit_solution(5477120223599321523)
XLA Ops:
  0.6 1.5 %shard_map.50 = (f32[256,256]{1,0:T(8,128)S(1)}, f32[256,256]{1,0:T(8,128)S(1)}, bf16[512,512]{1,0:T(8,128)(2,1)S(1)}, bf16[512,256]{1,0:T(8,128)(2,1)S(1)}) custom-call(bf16[2048,512]{1,0:T(8,128)(2,1)} %snapshots_ref.2, bf16[512,256]{1,0:T(8,128)(2,1)} %sketch_ref.3), custom_call_target="tpu_custom_call" | custom-call | flops 134217728 | bytes 1572864 | tf_op jit(solution)/shard_map/pallas_call | solution.py:96
  2.1 0.5 %collective-permute-start = (f32[256,256]{1,0:T(8,128)S(1)}, f32[256,256]{1,0:T(8,128)S(1)}, u32[]{:S(2)}, u32[]{:S(2)}) collective-permute-start(f32[256,256]{1,0:T(8,128)S(1)} %get-tuple-element.22), channel_id=1, source_target_pairs={{0,1},{1,0},{2,3},{3,2},{4,5},{5,4},{6,7},{7,6},{8,9},{9,8},{10,11... | collective-permute-start | bytes 786440 | tf_op jit(solution)/shard_map/ppermute | solution.py:30
  2.6 0.1 collective-permute-start.1
  2.7 0.3 shard_map.51
  3.0 0.8 %collective-permute-done = f32[256,256]{1,0:T(8,128)S(1)} collective-permute-done((f32[256,256]{1,0:T(8,128)S(1)}, f32[256,256]{1,0:T(8,128)S(1)}, u32[]{:S(2)}, u32[]{:S(2)}) %collective-permute-start) | collective-permute-done | bytes 262176 | tf_op jit(solution)/shard_map/ppermute | solution.py:30
  3.8 2.9 %collective-permute-start.5 = (f32[256,256]{1,0:T(8,128)S(1)}, f32[256,256]{1,0:T(8,128)S(1)}, u32[]{:S(2)}, u32[]{:S(2)}) collective-permute-start(f32[256,256]{1,0:T(8,128)S(1)} %add.24), channel_id=1, source_target_pairs={{0,2},{1,3},{2,0},{3,1},{4,6},{5,7},{6,4},{7,5},{8,10},{9,11},{10,... | collective-permute-start | bytes 786440 | tf_op jit(solution)/shard_map/ppermute | solution.py:30
  6.8 1.8 %shard_map.52 = (f32[128,256]{1,0:T(8,128)S(1)}, f32[128,256]{1,0:T(8,128)S(1)}, f32[128,256]{1,0:T(8,128)S(1)}, f32[128,256]{1,0:T(8,128)S(1)}, f32[512,256]{1,0:T(8,128)S(1)}) custom-call(bf16[2048,512]{1,0:T(8,128)(2,1)} %snapshots_ref.2, bf16[512,256]{1,0:T(8,128)(2,1)} %sketch_ref.3), custom_call_target="tpu_custom_call" | custom-call | flops 1 | bytes 1 | tf_op jit(solution)/shard_map/pallas_call | solution.py:150
  8.6 0.4 collective-permute-start.2
  9.0 0.1 collective-permute-start.7
  9.1 0.4 collective-permute-start.3
  9.6 0.4 collective-permute-done.6.rest_0_
  10.0 0.1 collective-permute-start.4
  10.1 0.3 collective-permute-done.7.rest_1_
  10.4 3.4 %collective-permute-done.5.far_ref = f32[256,256]{1,0:T(8,128)S(1)} collective-permute-done((f32[256,256]{1,0:T(8,128)S(1)}, f32[256,256]{1,0:T(8,128)S(1)}, u32[]{:S(2)}, u32[]{:S(2)}) %collective-permute-start.5) | collective-permute-done | bytes 262176 | tf_op jit(solution)/shard_map/ppermute | solution.py:30
  13.8 0.4 shard_map.53
  14.3 4.7 %collective-permute-done.2.far_ref = f32[256,256]{1,0:T(8,128)S(1)} collective-permute-done((f32[256,256]{1,0:T(8,128)S(1)}, f32[256,256]{1,0:T(8,128)S(1)}, u32[]{:S(2)}, u32[]{:S(2)}) %collective-permute-start.2) | collective-permute-done | bytes 262176 | tf_op jit(solution)/shard_map/ppermute | solution.py:30
  19.0 0.4 shard_map.54
  19.4 0.1 collective-permute-start.8
  19.5 1.2 %collective-permute-done.8 = f32[136,128]{1,0:T(8,128)S(1)} collective-permute-done((f32[136,128]{1,0:T(8,128)S(1)}, f32[136,128]{1,0:T(8,128)S(1)}, u32[]{:S(2)}, u32[]{:S(2)}) %collective-permute-start.8) | collective-permute-done | bytes 69664 | tf_op jit(solution)/shard_map/ppermute | solution.py:30
  20.7 1.8 %collective-permute-start.11 = (f32[136,128]{1,0:T(8,128)S(1)}, f32[136,128]{1,0:T(8,128)S(1)}, u32[]{:S(2)}, u32[]{:S(2)}) collective-permute-start(f32[136,128]{1,0:T(8,128)S(1)} %add.26), channel_id=1, source_target_pairs={{0,4},{1,5},{2,6},{3,7},{4,0},{5,1},{6,2},{7,3},{8,12},{9,13},{10,... | collective-permute-start | bytes 208904 | tf_op jit(solution)/shard_map/ppermute | solution.py:30
  22.6 1.5 %collective-permute-start.10 = (f32[136,128]{1,0:T(8,128)S(1)}, f32[136,128]{1,0:T(8,128)S(1)}, u32[]{:S(2)}, u32[]{:S(2)}) collective-permute-start(f32[136,128]{1,0:T(8,128)S(1)} %add.26), channel_id=1, source_target_pairs={{0,2},{1,3},{2,0},{3,1},{4,6},{5,7},{6,4},{7,5},{8,10},{9,11},{10,... | collective-permute-start | bytes 208904 | tf_op jit(solution)/shard_map/ppermute | solution.py:30
  24.0 0.2 collective-permute-start.9
  24.3 0.8 %collective-permute-done.11 = f32[136,128]{1,0:T(8,128)S(1)} collective-permute-done((f32[136,128]{1,0:T(8,128)S(1)}, f32[136,128]{1,0:T(8,128)S(1)}, u32[]{:S(2)}, u32[]{:S(2)}) %collective-permute-start.11) | collective-permute-done | bytes 69664 | tf_op jit(solution)/shard_map/ppermute | solution.py:30
  25.1 2.5 %collective-permute-done.10 = f32[136,128]{1,0:T(8,128)S(1)} collective-permute-done((f32[136,128]{1,0:T(8,128)S(1)}, f32[136,128]{1,0:T(8,128)S(1)}, u32[]{:S(2)}, u32[]{:S(2)}) %collective-permute-start.10) | collective-permute-done | bytes 69664 | tf_op jit(solution)/shard_map/ppermute | solution.py:30
  27.5 1.7 %collective-permute-done.9 = f32[136,128]{1,0:T(8,128)S(1)} collective-permute-done((f32[136,128]{1,0:T(8,128)S(1)}, f32[136,128]{1,0:T(8,128)S(1)}, u32[]{:S(2)}, u32[]{:S(2)}) %collective-permute-start.9) | collective-permute-done | bytes 69664 | tf_op jit(solution)/shard_map/ppermute | solution.py:30
  29.3 1.6 %collective-permute-start.12 = (f32[136,128]{1,0:T(8,128)S(1)}, f32[136,128]{1,0:T(8,128)S(1)}, u32[]{:S(2)}, u32[]{:S(2)}) collective-permute-start(f32[136,128]{1,0:T(8,128)S(1)} %add_add_fusion), channel_id=1, source_target_pairs={{0,8},{1,9},{2,10},{3,11},{4,12},{5,13},{6,14},{7,15},{8,0},{9,1},... | collective-permute-start | bytes 208904 | tf_op jit(solution)/shard_map/ppermute | solution.py:30
  30.9 2.7 %collective-permute-done.12 = f32[136,128]{1,0:T(8,128)S(1)} collective-permute-done((f32[136,128]{1,0:T(8,128)S(1)}, f32[136,128]{1,0:T(8,128)S(1)}, u32[]{:S(2)}, u32[]{:S(2)}) %collective-permute-start.12) | collective-permute-done | bytes 69664 | tf_op jit(solution)/shard_map/ppermute | solution.py:30
  33.7 2.9 %collective-permute-start.13 = (f32[136,128]{1,0:T(8,128)S(1)}, f32[136,128]{1,0:T(8,128)S(1)}, u32[]{:S(2)}, u32[]{:S(2)}) collective-permute-start(f32[136,128]{1,0:T(8,128)S(1)} %add.30), channel_id=1, source_target_pairs={{0,16},{1,17},{2,18},{3,19},{4,20},{5,21},{6,22},{7,23},{8,24},{9,... | collective-permute-start | bytes 208904 | tf_op jit(solution)/shard_map/ppermute | solution.py:30
  36.5 2.4 %collective-permute-done.13 = f32[136,128]{1,0:T(8,128)S(1)} collective-permute-done((f32[136,128]{1,0:T(8,128)S(1)}, f32[136,128]{1,0:T(8,128)S(1)}, u32[]{:S(2)}, u32[]{:S(2)}) %collective-permute-start.13) | collective-permute-done | bytes 69664 | tf_op jit(solution)/shard_map/ppermute | solution.py:30
  39.0 0.1 collective-permute-start.14
  39.1 1.3 %collective-permute-done.14.sent_ref = f32[264,128]{1,0:T(8,128)S(1)} collective-permute-done((f32[264,128]{1,0:T(8,128)S(1)}, f32[264,128]{1,0:T(8,128)S(1)}, u32[]{:S(2)}, u32[]{:S(2)}) %collective-permute-start.14) | collective-permute-done | bytes 135200 | tf_op jit(solution)/shard_map/ppermute | solution.py:30
  40.4 4.6 %shard_map.56 = (f32[512,256]{1,0:T(8,128)}, f32[256,256]{1,0:T(8,128)}) custom-call(s32[1]{0:T(128)} %bitcast.side_ref, f32[264,128]{1,0:T(8,128)S(1)} %shard_map.55.own_ref, f32[264,128]{1,0:T(8,128)S(1)} %collective-permute-done.14.sent_ref, f32[256,256]{1,0:T(8,128)S(1)} %copy-done, f32[256,256]{1,0:T(8,128)S(1)} %get-tuple-element.34.refs_0_, ...), custom_call_target="tpu_custom_call" | custom-call | flops 1073741824 | bytes 1835008 | tf_op jit(solution)/shard_map/pallas_call | solution.py:381
  (13 shorter events, 0.2 us)
Async XLA Ops:
  2.1 1.7 %collective-permute-start = (f32[256,256]{1,0:T(8,128)S(1)}, f32[256,256]{1,0:T(8,128)S(1)}, u32[]{:S(2)}, u32[]{:S(2)}) collective-permute-start(f32[256,256]{1,0:T(8,128)S(1)} %get-tuple-element.22), channel_id=1, source_target_pairs={{0,1},{1,0},{2,3},{3,2},{4,5},{5,4},{6,7},{7,6},{8,9},{9,8},{10,11... | collective-permute-start | bytes 786440 | tf_op jit(solution)/shard_map/ppermute | solution.py:30
  2.6 4.1 %collective-permute-start.1 = (f32[256,256]{1,0:T(8,128)S(1)}, f32[256,256]{1,0:T(8,128)S(1)}, u32[]{:S(2)}, u32[]{:S(2)}) collective-permute-start(f32[256,256]{1,0:T(8,128)S(1)} %get-tuple-element.24), channel_id=1, source_target_pairs={{0,1},{1,0},{2,3},{3,2},{4,5},{5,4},{6,7},{7,6},{8,9},{9,8},{10,11... | collective-permute-start | bytes 786440 | tf_op jit(solution)/shard_map/ppermute | solution.py:30
  3.8 10.0 %collective-permute-start.5 = (f32[256,256]{1,0:T(8,128)S(1)}, f32[256,256]{1,0:T(8,128)S(1)}, u32[]{:S(2)}, u32[]{:S(2)}) collective-permute-start(f32[256,256]{1,0:T(8,128)S(1)} %add.24), channel_id=1, source_target_pairs={{0,2},{1,3},{2,0},{3,1},{4,6},{5,7},{6,4},{7,5},{8,10},{9,11},{10,... | collective-permute-start | bytes 786440 | tf_op jit(solution)/shard_map/ppermute | solution.py:30
  8.6 31.9 %copy-start = (f32[256,256]{1,0:T(8,128)S(1)}, f32[256,256]{1,0:T(8,128)}, u32[]{:S(2)}) copy-start(f32[256,256]{1,0:T(8,128)} %rotation_ref.1) | copy-start | bytes 786436
  8.6 1.4 %collective-permute-start.6 = (f32[128,256]{1,0:T(8,128)S(1)}, f32[128,256]{1,0:T(8,128)S(1)}, u32[]{:S(2)}, u32[]{:S(2)}) collective-permute-start(f32[128,256]{1,0:T(8,128)S(1)} %get-tuple-element.29), channel_id=1, source_target_pairs={{0,1},{1,0},{2,3},{3,2},{4,5},{5,4},{6,7},{7,6},{8,9},{9,8},{10,11... | collective-permute-start | bytes 393224 | tf_op jit(solution)/shard_map/ppermute | solution.py:30
  8.6 10.3 %collective-permute-start.2 = (f32[256,256]{1,0:T(8,128)S(1)}, f32[256,256]{1,0:T(8,128)S(1)}, u32[]{:S(2)}, u32[]{:S(2)}) collective-permute-start(f32[256,256]{1,0:T(8,128)S(1)} %add.25), channel_id=1, source_target_pairs={{0,2},{1,3},{2,0},{3,1},{4,6},{5,7},{6,4},{7,5},{8,10},{9,11},{10,... | collective-permute-start | bytes 786440 | tf_op jit(solution)/shard_map/ppermute | solution.py:30
  9.0 1.3 %collective-permute-start.7 = (f32[128,256]{1,0:T(8,128)S(1)}, f32[128,256]{1,0:T(8,128)S(1)}, u32[]{:S(2)}, u32[]{:S(2)}) collective-permute-start(f32[128,256]{1,0:T(8,128)S(1)} %get-tuple-element.30), channel_id=1, source_target_pairs={{0,1},{1,0},{2,3},{3,2},{4,5},{5,4},{6,7},{7,6},{8,9},{9,8},{10,11... | collective-permute-start | bytes 393224 | tf_op jit(solution)/shard_map/ppermute | solution.py:30
  9.1 5.1 %collective-permute-start.3 = (f32[128,256]{1,0:T(8,128)S(1)}, f32[128,256]{1,0:T(8,128)S(1)}, u32[]{:S(2)}, u32[]{:S(2)}) collective-permute-start(f32[128,256]{1,0:T(8,128)S(1)} %get-tuple-element.27), channel_id=1, source_target_pairs={{0,1},{1,0},{2,3},{3,2},{4,5},{5,4},{6,7},{7,6},{8,9},{9,8},{10,11... | collective-permute-start | bytes 393224 | tf_op jit(solution)/shard_map/ppermute | solution.py:30
  10.0 4.3 %collective-permute-start.4 = (f32[128,256]{1,0:T(8,128)S(1)}, f32[128,256]{1,0:T(8,128)S(1)}, u32[]{:S(2)}, u32[]{:S(2)}) collective-permute-start(f32[128,256]{1,0:T(8,128)S(1)} %get-tuple-element.28), channel_id=1, source_target_pairs={{0,1},{1,0},{2,3},{3,2},{4,5},{5,4},{6,7},{7,6},{8,9},{9,8},{10,11... | collective-permute-start | bytes 393224 | tf_op jit(solution)/shard_map/ppermute | solution.py:30
  19.4 1.3 %collective-permute-start.8 = (f32[136,128]{1,0:T(8,128)S(1)}, f32[136,128]{1,0:T(8,128)S(1)}, u32[]{:S(2)}, u32[]{:S(2)}) collective-permute-start(f32[136,128]{1,0:T(8,128)S(1)} %get-tuple-element.33), channel_id=1, source_target_pairs={{0,1},{1,0},{2,3},{3,2},{4,5},{5,4},{6,7},{7,6},{8,9},{9,8},{10,11... | collective-permute-start | bytes 208904 | tf_op jit(solution)/shard_map/ppermute | solution.py:30
  20.7 4.4 %collective-permute-start.11 = (f32[136,128]{1,0:T(8,128)S(1)}, f32[136,128]{1,0:T(8,128)S(1)}, u32[]{:S(2)}, u32[]{:S(2)}) collective-permute-start(f32[136,128]{1,0:T(8,128)S(1)} %add.26), channel_id=1, source_target_pairs={{0,4},{1,5},{2,6},{3,7},{4,0},{5,1},{6,2},{7,3},{8,12},{9,13},{10,... | collective-permute-start | bytes 208904 | tf_op jit(solution)/shard_map/ppermute | solution.py:30
  22.6 5.0 %collective-permute-start.10 = (f32[136,128]{1,0:T(8,128)S(1)}, f32[136,128]{1,0:T(8,128)S(1)}, u32[]{:S(2)}, u32[]{:S(2)}) collective-permute-start(f32[136,128]{1,0:T(8,128)S(1)} %add.26), channel_id=1, source_target_pairs={{0,2},{1,3},{2,0},{3,1},{4,6},{5,7},{6,4},{7,5},{8,10},{9,11},{10,... | collective-permute-start | bytes 208904 | tf_op jit(solution)/shard_map/ppermute | solution.py:30
  24.0 5.2 %collective-permute-start.9 = (f32[136,128]{1,0:T(8,128)S(1)}, f32[136,128]{1,0:T(8,128)S(1)}, u32[]{:S(2)}, u32[]{:S(2)}) collective-permute-start(f32[136,128]{1,0:T(8,128)S(1)} %add.26), channel_id=1, source_target_pairs={{0,6},{1,7},{2,4},{3,5},{4,2},{5,3},{6,0},{7,1},{8,14},{9,15},{10,... | collective-permute-start | bytes 208904 | tf_op jit(solution)/shard_map/ppermute | solution.py:30
  29.3 4.4 %collective-permute-start.12 = (f32[136,128]{1,0:T(8,128)S(1)}, f32[136,128]{1,0:T(8,128)S(1)}, u32[]{:S(2)}, u32[]{:S(2)}) collective-permute-start(f32[136,128]{1,0:T(8,128)S(1)} %add_add_fusion), channel_id=1, source_target_pairs={{0,8},{1,9},{2,10},{3,11},{4,12},{5,13},{6,14},{7,15},{8,0},{9,1},... | collective-permute-start | bytes 208904 | tf_op jit(solution)/shard_map/ppermute | solution.py:30
  33.7 5.3 %collective-permute-start.13 = (f32[136,128]{1,0:T(8,128)S(1)}, f32[136,128]{1,0:T(8,128)S(1)}, u32[]{:S(2)}, u32[]{:S(2)}) collective-permute-start(f32[136,128]{1,0:T(8,128)S(1)} %add.30), channel_id=1, source_target_pairs={{0,16},{1,17},{2,18},{3,19},{4,20},{5,21},{6,22},{7,23},{8,24},{9,... | collective-permute-start | bytes 208904 | tf_op jit(solution)/shard_map/ppermute | solution.py:30
  39.0 1.4 %collective-permute-start.14 = (f32[264,128]{1,0:T(8,128)S(1)}, f32[264,128]{1,0:T(8,128)S(1)}, u32[]{:S(2)}, u32[]{:S(2)}) collective-permute-start(f32[264,128]{1,0:T(8,128)S(1)} %shard_map.55.own_ref), channel_id=1, source_target_pairs={{0,1},{1,0},{2,3},{3,2},{4,5},{5,4},{6,7},{7,6},{8,9},{9,8},{10,11... | collective-permute-start | bytes 405512 | tf_op jit(solution)/shard_map/ppermute | solution.py:30

commit v7 on v6

--- a/solution.py
+++ b/solution.py
@@ -13,7 +13,7 @@
 SMEM = pl.BlockSpec(memory_space=pltpu.SMEM)
 BLOCK = 64
 SLICES = 4
-PARTS = 2
+PARTS = 4
 CHUNKS = 4
 PANEL = 2
 
@@ -165,25 +165,29 @@
 def gram_kernel(part, side_ref, kept_ref, far_ref, *rest):
     near_refs, rest = rest[: SLICES // PARTS], rest[SLICES // PARTS :]
     before, (sketched_ref, *outs) = rest[: min(part, 1)], rest[min(part, 1) :]
-    rows = far_ref.shape[0]
-    mine = slice(rows * part, rows * (part + 1))
+    count = far_ref.shape[0]
+    mine = slice(count * part, count * (part + 1))
     sketched = (kept_ref[mine, :] + jnp.concatenate([ref[...] for ref in near_refs], axis=0)) + far_ref[...]
     sketched_ref[...] = sketched
-    gram = dot_parts(sketched, sketched, (0, 0))
+    left, right = stacked(sketched, LEFT, 0), stacked(sketched, RIGHT, 0)
+    h = sketched.shape[1] // 2
+    rows = ((0,), (0,))
+    top, bottom = product(left[:, :h], right[:, :h], rows), product(left[:, h:], right, rows)
     if before:
-        gram = gram + before[0][...]
+        top, bottom = top + before[0][:h, :h], bottom + before[0][h:, :]
     if part < PARTS - 1:
-        outs[0][...] = gram
+        (gram_ref,) = outs
+        gram_ref[:h, :h] = top
+        gram_ref[h:, :] = bottom
         return
     keep_ref, send_ref = outs
-    h = gram.shape[0] // 2
     lower, middle = triangles((h, h))
-    corner = gram[h:, h:]
+    corner = bottom[:, h:]
     diagonal = jnp.sum(jnp.where(middle, corner, 0.0), axis=0, keepdims=True)
-    mixed = jnp.where(lower | middle, gram[:h, :h], corner)
+    mixed = jnp.where(lower | middle, top, corner)
     first = side_ref[0] == 0
-    keep_ref[:h, :] = jnp.where(first, gram[h:, :h], mixed)
-    send_ref[:h, :] = jnp.where(first, mixed, gram[h:, :h])
+    keep_ref[:h, :] = jnp.where(first, bottom[:, :h], mixed)
+    send_ref[:h, :] = jnp.where(first, mixed, bottom[:, :h])
     keep_ref[h:, :] = jnp.broadcast_to(diagonal, (8, h))
     send_ref[h:, :] = jnp.broadcast_to(diagonal, (8, h))
 
@@ -427,7 +431,7 @@
     flips = [1 << level for level in range(1, depth + levels("space"))]
     if len(flips) > 1:
         x, y, *flips = flips
-        mine = mine + ((partner(mine, x | y) + partner(mine, x)) + partner(mine, y))
+        mine = mine + ((partner(mine, x | y) + partner(mine, y)) + partner(mine, x))
     for flip in flips:
         mine = mine + partner(mine, flip)
     own = first_factor(side, mine)

time: 45.2 us -> 45 us (level)
  waiting for transfers between devices: 22.3 us -> 17.7 us
  starting transfers between devices: 12.8 us -> 17 us
    ppermute x15 -> x19, waiting for transfers between devices: 22.3 us -> 17.7 us  [partner(): return lax.ppermute(shard, AXES, [(i, i ^ flip) for i in range(count)])]
    ppermute x15 -> x19, starting transfers between devices: 12.8 us -> 17 us  [partner(): return lax.ppermute(shard, AXES, [(i, i ^ flip) for i in range(count)])]
    pallas_call x2 -> x4, Pallas kernels: 0.83 us -> 1.19 us  [gram_part(): pl.pallas_call(functools.partial(gram_kernel, part), out_shape=[jax.Shape...]
  transfers between devices with their start and end apart: 15 -> 19, of which waited for: 12 -> 11; matrix products, arithmetic and copies ran while one was open for 0% -> 0% of each run, Pallas kernels for 5% -> 7%
where the time goes in v7:
time: 45 us; the launch traced here: 44.9 us
  waiting for transfers between devices  17.7 us (39%)
  starting transfers between devices  17 us (38%)
  Pallas kernels  9.36 us (21%)
  between operations  0.77 us (2%)
    ppermute x19, waiting for transfers between devices, partner(): return lax.ppermute(shard, AXES, [(i, i ^ flip) for i in range(count)])  17.7 us
    ppermute x19, starting transfers between devices, partner(): return lax.ppermute(shard, AXES, [(i, i ^ flip) for i in range(count)])  17 us
    pallas_call x1, Pallas kernels, basis_and_triangle(): pl.pallas_call(functools.partial(basis_kernel, scale), out_shape=[jax.Sha...  4.62 us
    pallas_call x1, Pallas kernels, sketch_last(): pl.pallas_call(last_kernel, out_shape=[jax.ShapeDtypeStruct((rows // SLIC...  1.75 us
    pallas_call x1, Pallas kernels, sketch_leaving(): pl.pallas_call(functools.partial(leaving_kernel, leaves, stays), out_shap...  1.47 us
    pallas_call x4, Pallas kernels, gram_part(): pl.pallas_call(functools.partial(gram_kernel, part), out_shape=[jax.Shape...  1.19 us
  transfers between devices with their start and end apart: 19, of which 11 were waited for; matrix products, arithmetic and copies ran while one was open for 0% of the time, Pallas kernels for 7%

profile of v7, /device:TPU:0, one launch (start us, length us, event | category | flops | bytes accessed | tf_op | source)
XLA Modules:
  0.0 44.9 jit_solution(5397389137056471766)
XLA Ops:
  0.6 1.5 %shard_map.50 = (f32[128,256]{1,0:T(8,128)S(1)}, f32[128,256]{1,0:T(8,128)S(1)}, f32[128,256]{1,0:T(8,128)S(1)}, f32[128,256]{1,0:T(8,128)S(1)}, bf16[512,512]{1...) custom-call(bf16[2048,512]{1,0:T(8,128)(2,1)} %snapshots_ref.2, bf16[512,256]{1,0:T(8,128)(2,1)} %sketch_ref.3), custom_call_target="tpu_custom_call" | custom-call | flops 134217728 | bytes 1572864 | tf_op jit(solution)/shard_map/pallas_call | solution.py:96
  2.1 0.5 %collective-permute-start = (f32[128,256]{1,0:T(8,128)S(1)}, f32[128,256]{1,0:T(8,128)S(1)}, u32[]{:S(2)}, u32[]{:S(2)}) collective-permute-start(f32[128,256]{1,0:T(8,128)S(1)} %get-tuple-element.30), channel_id=1, source_target_pairs={{0,1},{1,0},{2,3},{3,2},{4,5},{5,4},{6,7},{7,6},{8,9},{9,8},{10,11... | collective-permute-start | bytes 393224 | tf_op jit(solution)/shard_map/ppermute | solution.py:30
  2.7 0.4 collective-permute-start.2
  3.2 0.3 shard_map.51
  3.5 0.1 collective-permute-done
  3.6 2.9 %collective-permute-start.10 = (f32[128,256]{1,0:T(8,128)S(1)}, f32[128,256]{1,0:T(8,128)S(1)}, u32[]{:S(2)}, u32[]{:S(2)}) collective-permute-start(f32[128,256]{1,0:T(8,128)S(1)} %add.30), channel_id=1, source_target_pairs={{0,2},{1,3},{2,0},{3,1},{4,6},{5,7},{6,4},{7,5},{8,10},{9,11},{10,... | collective-permute-start | bytes 393224 | tf_op jit(solution)/shard_map/ppermute | solution.py:30
  6.6 0.2 collective-permute-start.8
  6.8 1.8 %shard_map.52 = (f32[128,256]{1,0:T(8,128)S(1)}, f32[128,256]{1,0:T(8,128)S(1)}, f32[128,256]{1,0:T(8,128)S(1)}, f32[128,256]{1,0:T(8,128)S(1)}, f32[512,256]{1,0:T(8,128)S(1)}) custom-call(bf16[2048,512]{1,0:T(8,128)(2,1)} %snapshots_ref.2, bf16[512,256]{1,0:T(8,128)(2,1)} %sketch_ref.3), custom_call_target="tpu_custom_call" | custom-call | flops 1 | bytes 1 | tf_op jit(solution)/shard_map/pallas_call | solution.py:150
  8.6 0.1 collective-permute-start.11
  8.7 0.5 %collective-permute-start.9 = (f32[128,256]{1,0:T(8,128)S(1)}, f32[128,256]{1,0:T(8,128)S(1)}, u32[]{:S(2)}, u32[]{:S(2)}) collective-permute-start(f32[128,256]{1,0:T(8,128)S(1)} %get-tuple-element.41), channel_id=1, source_target_pairs={{0,1},{1,0},{2,3},{3,2},{4,5},{5,4},{6,7},{7,6},{8,9},{9,8},{10,11... | collective-permute-start | bytes 393224 | tf_op jit(solution)/shard_map/ppermute | solution.py:30
  9.1 1.9 %collective-permute-start.6 = (f32[128,256]{1,0:T(8,128)S(1)}, f32[128,256]{1,0:T(8,128)S(1)}, u32[]{:S(2)}, u32[]{:S(2)}) collective-permute-start(f32[128,256]{1,0:T(8,128)S(1)} %add.32), channel_id=1, source_target_pairs={{0,2},{1,3},{2,0},{3,1},{4,6},{5,7},{6,4},{7,5},{8,10},{9,11},{10,... | collective-permute-start | bytes 393224 | tf_op jit(solution)/shard_map/ppermute | solution.py:30
  11.1 2.6 %collective-permute-done.8.far_ref = f32[128,256]{1,0:T(8,128)S(1)} collective-permute-done((f32[128,256]{1,0:T(8,128)S(1)}, f32[128,256]{1,0:T(8,128)S(1)}, u32[]{:S(2)}, u32[]{:S(2)}) %collective-permute-start.8) | collective-permute-done | bytes 131104 | tf_op jit(solution)/shard_map/ppermute | solution.py:30
  13.6 2.1 %collective-permute-start.4 = (f32[128,256]{1,0:T(8,128)S(1)}, f32[128,256]{1,0:T(8,128)S(1)}, u32[]{:S(2)}, u32[]{:S(2)}) collective-permute-start(f32[128,256]{1,0:T(8,128)S(1)} %add.33), channel_id=1, source_target_pairs={{0,2},{1,3},{2,0},{3,1},{4,6},{5,7},{6,4},{7,5},{8,10},{9,11},{10,... | collective-permute-start | bytes 393224 | tf_op jit(solution)/shard_map/ppermute | solution.py:30
  15.7 0.3 shard_map.53
  16.0 0.3 shard_map.54
  16.3 0.1 collective-permute-done.6.far_ref
  16.4 0.3 shard_map.55
  16.7 2.0 %collective-permute-done.4.far_ref = f32[128,256]{1,0:T(8,128)S(1)} collective-permute-done((f32[128,256]{1,0:T(8,128)S(1)}, f32[128,256]{1,0:T(8,128)S(1)}, u32[]{:S(2)}, u32[]{:S(2)}) %collective-permute-start.4) | collective-permute-done | bytes 131104 | tf_op jit(solution)/shard_map/ppermute | solution.py:30
  18.8 0.3 shard_map.56
  19.2 1.2 %collective-permute-done.12 = f32[136,128]{1,0:T(8,128)S(1)} collective-permute-done((f32[136,128]{1,0:T(8,128)S(1)}, f32[136,128]{1,0:T(8,128)S(1)}, u32[]{:S(2)}, u32[]{:S(2)}) %collective-permute-start.12) | collective-permute-done | bytes 69664 | tf_op jit(solution)/shard_map/ppermute | solution.py:30
  20.4 1.9 %collective-permute-start.15 = (f32[136,128]{1,0:T(8,128)S(1)}, f32[136,128]{1,0:T(8,128)S(1)}, u32[]{:S(2)}, u32[]{:S(2)}) collective-permute-start(f32[136,128]{1,0:T(8,128)S(1)} %add.34), channel_id=1, source_target_pairs={{0,2},{1,3},{2,0},{3,1},{4,6},{5,7},{6,4},{7,5},{8,10},{9,11},{10,... | collective-permute-start | bytes 208904 | tf_op jit(solution)/shard_map/ppermute | solution.py:30
  22.4 1.5 %collective-permute-start.14 = (f32[136,128]{1,0:T(8,128)S(1)}, f32[136,128]{1,0:T(8,128)S(1)}, u32[]{:S(2)}, u32[]{:S(2)}) collective-permute-start(f32[136,128]{1,0:T(8,128)S(1)} %add.34), channel_id=1, source_target_pairs={{0,4},{1,5},{2,6},{3,7},{4,0},{5,1},{6,2},{7,3},{8,12},{9,13},{10,... | collective-permute-start | bytes 208904 | tf_op jit(solution)/shard_map/ppermute | solution.py:30
  23.9 0.1 collective-permute-start.13
  24.0 0.9 %collective-permute-done.15 = f32[136,128]{1,0:T(8,128)S(1)} collective-permute-done((f32[136,128]{1,0:T(8,128)S(1)}, f32[136,128]{1,0:T(8,128)S(1)}, u32[]{:S(2)}, u32[]{:S(2)}) %collective-permute-start.15) | collective-permute-done | bytes 69664 | tf_op jit(solution)/shard_map/ppermute | solution.py:30
  24.9 1.8 %collective-permute-done.14 = f32[136,128]{1,0:T(8,128)S(1)} collective-permute-done((f32[136,128]{1,0:T(8,128)S(1)}, f32[136,128]{1,0:T(8,128)S(1)}, u32[]{:S(2)}, u32[]{:S(2)}) %collective-permute-start.14) | collective-permute-done | bytes 69664 | tf_op jit(solution)/shard_map/ppermute | solution.py:30
  26.7 2.4 %collective-permute-done.13 = f32[136,128]{1,0:T(8,128)S(1)} collective-permute-done((f32[136,128]{1,0:T(8,128)S(1)}, f32[136,128]{1,0:T(8,128)S(1)}, u32[]{:S(2)}, u32[]{:S(2)}) %collective-permute-start.13) | collective-permute-done | bytes 69664 | tf_op jit(solution)/shard_map/ppermute | solution.py:30
  29.1 1.6 %collective-permute-start.16 = (f32[136,128]{1,0:T(8,128)S(1)}, f32[136,128]{1,0:T(8,128)S(1)}, u32[]{:S(2)}, u32[]{:S(2)}) collective-permute-start(f32[136,128]{1,0:T(8,128)S(1)} %add_add_fusion), channel_id=1, source_target_pairs={{0,8},{1,9},{2,10},{3,11},{4,12},{5,13},{6,14},{7,15},{8,0},{9,1},... | collective-permute-start | bytes 208904 | tf_op jit(solution)/shard_map/ppermute | solution.py:30
  30.8 2.7 %collective-permute-done.16 = f32[136,128]{1,0:T(8,128)S(1)} collective-permute-done((f32[136,128]{1,0:T(8,128)S(1)}, f32[136,128]{1,0:T(8,128)S(1)}, u32[]{:S(2)}, u32[]{:S(2)}) %collective-permute-start.16) | collective-permute-done | bytes 69664 | tf_op jit(solution)/shard_map/ppermute | solution.py:30
  33.5 2.9 %collective-permute-start.17 = (f32[136,128]{1,0:T(8,128)S(1)}, f32[136,128]{1,0:T(8,128)S(1)}, u32[]{:S(2)}, u32[]{:S(2)}) collective-permute-start(f32[136,128]{1,0:T(8,128)S(1)} %add.38), channel_id=1, source_target_pairs={{0,16},{1,17},{2,18},{3,19},{4,20},{5,21},{6,22},{7,23},{8,24},{9,... | collective-permute-start | bytes 208904 | tf_op jit(solution)/shard_map/ppermute | solution.py:30
  36.4 2.4 %collective-permute-done.17 = f32[136,128]{1,0:T(8,128)S(1)} collective-permute-done((f32[136,128]{1,0:T(8,128)S(1)}, f32[136,128]{1,0:T(8,128)S(1)}, u32[]{:S(2)}, u32[]{:S(2)}) %collective-permute-start.17) | collective-permute-done | bytes 69664 | tf_op jit(solution)/shard_map/ppermute | solution.py:30
  38.9 1.3 %collective-permute-done.18.sent_ref = f32[264,128]{1,0:T(8,128)S(1)} collective-permute-done((f32[264,128]{1,0:T(8,128)S(1)}, f32[264,128]{1,0:T(8,128)S(1)}, u32[]{:S(2)}, u32[]{:S(2)}) %collective-permute-start.18) | collective-permute-done | bytes 135200 | tf_op jit(solution)/shard_map/ppermute | solution.py:30
  40.3 4.6 %shard_map.58 = (f32[512,256]{1,0:T(8,128)}, f32[256,256]{1,0:T(8,128)}) custom-call(s32[1]{0:T(128)} %bitcast.side_ref, f32[264,128]{1,0:T(8,128)S(1)} %shard_map.57.own_ref, f32[264,128]{1,0:T(8,128)S(1)} %collective-permute-done.18.sent_ref, f32[256,256]{1,0:T(8,128)S(1)} %copy-done, f32[128,256]{1,0:T(8,128)S(1)} %get-tuple-element.48.refs_0_, ...), custom_call_target="tpu_custom_call" | custom-call | flops 1073741824 | bytes 1835008 | tf_op jit(solution)/shard_map/pallas_call | solution.py:385
  (25 shorter events, 0.5 us)
Async XLA Ops:
  2.1 1.5 %collective-permute-start = (f32[128,256]{1,0:T(8,128)S(1)}, f32[128,256]{1,0:T(8,128)S(1)}, u32[]{:S(2)}, u32[]{:S(2)}) collective-permute-start(f32[128,256]{1,0:T(8,128)S(1)} %get-tuple-element.30), channel_id=1, source_target_pairs={{0,1},{1,0},{2,3},{3,2},{4,5},{5,4},{6,7},{7,6},{8,9},{9,8},{10,11... | collective-permute-start | bytes 393224 | tf_op jit(solution)/shard_map/ppermute | solution.py:30
  2.6 3.9 %collective-permute-start.1 = (f32[128,256]{1,0:T(8,128)S(1)}, f32[128,256]{1,0:T(8,128)S(1)}, u32[]{:S(2)}, u32[]{:S(2)}) collective-permute-start(f32[128,256]{1,0:T(8,128)S(1)} %get-tuple-element.32), channel_id=1, source_target_pairs={{0,1},{1,0},{2,3},{3,2},{4,5},{5,4},{6,7},{7,6},{8,9},{9,8},{10,11... | collective-permute-start | bytes 393224 | tf_op jit(solution)/shard_map/ppermute | solution.py:30
  2.7 4.0 %collective-permute-start.2 = (f32[128,256]{1,0:T(8,128)S(1)}, f32[128,256]{1,0:T(8,128)S(1)}, u32[]{:S(2)}, u32[]{:S(2)}) collective-permute-start(f32[128,256]{1,0:T(8,128)S(1)} %get-tuple-element.34), channel_id=1, source_target_pairs={{0,1},{1,0},{2,3},{3,2},{4,5},{5,4},{6,7},{7,6},{8,9},{9,8},{10,11... | collective-permute-start | bytes 393224 | tf_op jit(solution)/shard_map/ppermute | solution.py:30
  3.1 3.6 %collective-permute-start.3 = (f32[128,256]{1,0:T(8,128)S(1)}, f32[128,256]{1,0:T(8,128)S(1)}, u32[]{:S(2)}, u32[]{:S(2)}) collective-permute-start(f32[128,256]{1,0:T(8,128)S(1)} %get-tuple-element.36), channel_id=1, source_target_pairs={{0,1},{1,0},{2,3},{3,2},{4,5},{5,4},{6,7},{7,6},{8,9},{9,8},{10,11... | collective-permute-start | bytes 393224 | tf_op jit(solution)/shard_map/ppermute | solution.py:30
  3.6 7.4 %collective-permute-start.10 = (f32[128,256]{1,0:T(8,128)S(1)}, f32[128,256]{1,0:T(8,128)S(1)}, u32[]{:S(2)}, u32[]{:S(2)}) collective-permute-start(f32[128,256]{1,0:T(8,128)S(1)} %add.30), channel_id=1, source_target_pairs={{0,2},{1,3},{2,0},{3,1},{4,6},{5,7},{6,4},{7,5},{8,10},{9,11},{10,... | collective-permute-start | bytes 393224 | tf_op jit(solution)/shard_map/ppermute | solution.py:30
  6.6 7.1 %collective-permute-start.8 = (f32[128,256]{1,0:T(8,128)S(1)}, f32[128,256]{1,0:T(8,128)S(1)}, u32[]{:S(2)}, u32[]{:S(2)}) collective-permute-start(f32[128,256]{1,0:T(8,128)S(1)} %add.31), channel_id=1, source_target_pairs={{0,2},{1,3},{2,0},{3,1},{4,6},{5,7},{6,4},{7,5},{8,10},{9,11},{10,... | collective-permute-start | bytes 393224 | tf_op jit(solution)/shard_map/ppermute | solution.py:30
  8.6 7.1 %collective-permute-start.11 = (f32[128,256]{1,0:T(8,128)S(1)}, f32[128,256]{1,0:T(8,128)S(1)}, u32[]{:S(2)}, u32[]{:S(2)}) collective-permute-start(f32[128,256]{1,0:T(8,128)S(1)} %get-tuple-element.42), channel_id=1, source_target_pairs={{0,1},{1,0},{2,3},{3,2},{4,5},{5,4},{6,7},{7,6},{8,9},{9,8},{10,11... | collective-permute-start | bytes 393224 | tf_op jit(solution)/shard_map/ppermute | solution.py:30
  8.7 7.3 %collective-permute-start.9 = (f32[128,256]{1,0:T(8,128)S(1)}, f32[128,256]{1,0:T(8,128)S(1)}, u32[]{:S(2)}, u32[]{:S(2)}) collective-permute-start(f32[128,256]{1,0:T(8,128)S(1)} %get-tuple-element.41), channel_id=1, source_target_pairs={{0,1},{1,0},{2,3},{3,2},{4,5},{5,4},{6,7},{7,6},{8,9},{9,8},{10,11... | collective-permute-start | bytes 393224 | tf_op jit(solution)/shard_map/ppermute | solution.py:30
  9.1 7.3 %collective-permute-start.6 = (f32[128,256]{1,0:T(8,128)S(1)}, f32[128,256]{1,0:T(8,128)S(1)}, u32[]{:S(2)}, u32[]{:S(2)}) collective-permute-start(f32[128,256]{1,0:T(8,128)S(1)} %add.32), channel_id=1, source_target_pairs={{0,2},{1,3},{2,0},{3,1},{4,6},{5,7},{6,4},{7,5},{8,10},{9,11},{10,... | collective-permute-start | bytes 393224 | tf_op jit(solution)/shard_map/ppermute | solution.py:30
  11.1 5.4 %collective-permute-start.7 = (f32[128,256]{1,0:T(8,128)S(1)}, f32[128,256]{1,0:T(8,128)S(1)}, u32[]{:S(2)}, u32[]{:S(2)}) collective-permute-start(f32[128,256]{1,0:T(8,128)S(1)} %get-tuple-element.40), channel_id=1, source_target_pairs={{0,1},{1,0},{2,3},{3,2},{4,5},{5,4},{6,7},{7,6},{8,9},{9,8},{10,11... | collective-permute-start | bytes 393224 | tf_op jit(solution)/shard_map/ppermute | solution.py:30
  13.6 5.1 %collective-permute-start.4 = (f32[128,256]{1,0:T(8,128)S(1)}, f32[128,256]{1,0:T(8,128)S(1)}, u32[]{:S(2)}, u32[]{:S(2)}) collective-permute-start(f32[128,256]{1,0:T(8,128)S(1)} %add.33), channel_id=1, source_target_pairs={{0,2},{1,3},{2,0},{3,1},{4,6},{5,7},{6,4},{7,5},{8,10},{9,11},{10,... | collective-permute-start | bytes 393224 | tf_op jit(solution)/shard_map/ppermute | solution.py:30
  15.7 3.1 %collective-permute-start.5 = (f32[128,256]{1,0:T(8,128)S(1)}, f32[128,256]{1,0:T(8,128)S(1)}, u32[]{:S(2)}, u32[]{:S(2)}) collective-permute-start(f32[128,256]{1,0:T(8,128)S(1)} %get-tuple-element.39), channel_id=1, source_target_pairs={{0,1},{1,0},{2,3},{3,2},{4,5},{5,4},{6,7},{7,6},{8,9},{9,8},{10,11... | collective-permute-start | bytes 393224 | tf_op jit(solution)/shard_map/ppermute | solution.py:30
  16.0 24.2 %copy-start = (f32[256,256]{1,0:T(8,128)S(1)}, f32[256,256]{1,0:T(8,128)}, u32[]{:S(2)}) copy-start(f32[256,256]{1,0:T(8,128)} %rotation_ref.1) | copy-start | bytes 786436
  19.1 1.3 %collective-permute-start.12 = (f32[136,128]{1,0:T(8,128)S(1)}, f32[136,128]{1,0:T(8,128)S(1)}, u32[]{:S(2)}, u32[]{:S(2)}) collective-permute-start(f32[136,128]{1,0:T(8,128)S(1)} %get-tuple-element.47), channel_id=1, source_target_pairs={{0,1},{1,0},{2,3},{3,2},{4,5},{5,4},{6,7},{7,6},{8,9},{9,8},{10,11... | collective-permute-start | bytes 208904 | tf_op jit(solution)/shard_map/ppermute | solution.py:30
  20.4 4.5 %collective-permute-start.15 = (f32[136,128]{1,0:T(8,128)S(1)}, f32[136,128]{1,0:T(8,128)S(1)}, u32[]{:S(2)}, u32[]{:S(2)}) collective-permute-start(f32[136,128]{1,0:T(8,128)S(1)} %add.34), channel_id=1, source_target_pairs={{0,2},{1,3},{2,0},{3,1},{4,6},{5,7},{6,4},{7,5},{8,10},{9,11},{10,... | collective-permute-start | bytes 208904 | tf_op jit(solution)/shard_map/ppermute | solution.py:30
  22.4 4.3 %collective-permute-start.14 = (f32[136,128]{1,0:T(8,128)S(1)}, f32[136,128]{1,0:T(8,128)S(1)}, u32[]{:S(2)}, u32[]{:S(2)}) collective-permute-start(f32[136,128]{1,0:T(8,128)S(1)} %add.34), channel_id=1, source_target_pairs={{0,4},{1,5},{2,6},{3,7},{4,0},{5,1},{6,2},{7,3},{8,12},{9,13},{10,... | collective-permute-start | bytes 208904 | tf_op jit(solution)/shard_map/ppermute | solution.py:30
  23.9 5.2 %collective-permute-start.13 = (f32[136,128]{1,0:T(8,128)S(1)}, f32[136,128]{1,0:T(8,128)S(1)}, u32[]{:S(2)}, u32[]{:S(2)}) collective-permute-start(f32[136,128]{1,0:T(8,128)S(1)} %add.34), channel_id=1, source_target_pairs={{0,6},{1,7},{2,4},{3,5},{4,2},{5,3},{6,0},{7,1},{8,14},{9,15},{10,... | collective-permute-start | bytes 208904 | tf_op jit(solution)/shard_map/ppermute | solution.py:30
  29.1 4.4 %collective-permute-start.16 = (f32[136,128]{1,0:T(8,128)S(1)}, f32[136,128]{1,0:T(8,128)S(1)}, u32[]{:S(2)}, u32[]{:S(2)}) collective-permute-start(f32[136,128]{1,0:T(8,128)S(1)} %add_add_fusion), channel_id=1, source_target_pairs={{0,8},{1,9},{2,10},{3,11},{4,12},{5,13},{6,14},{7,15},{8,0},{9,1},... | collective-permute-start | bytes 208904 | tf_op jit(solution)/shard_map/ppermute | solution.py:30
  33.5 5.3 %collective-permute-start.17 = (f32[136,128]{1,0:T(8,128)S(1)}, f32[136,128]{1,0:T(8,128)S(1)}, u32[]{:S(2)}, u32[]{:S(2)}) collective-permute-start(f32[136,128]{1,0:T(8,128)S(1)} %add.38), channel_id=1, source_target_pairs={{0,16},{1,17},{2,18},{3,19},{4,20},{5,21},{6,22},{7,23},{8,24},{9,... | collective-permute-start | bytes 208904 | tf_op jit(solution)/shard_map/ppermute | solution.py:30
  38.8 1.4 %collective-permute-start.18 = (f32[264,128]{1,0:T(8,128)S(1)}, f32[264,128]{1,0:T(8,128)S(1)}, u32[]{:S(2)}, u32[]{:S(2)}) collective-permute-start(f32[264,128]{1,0:T(8,128)S(1)} %shard_map.57.own_ref), channel_id=1, source_target_pairs={{0,1},{1,0},{2,3},{3,2},{4,5},{5,4},{6,7},{7,6},{8,9},{9,8},{10,11... | collective-permute-start | bytes 405512 | tf_op jit(solution)/shard_map/ppermute | solution.py:30
